TPU v7x, 32 devices: a whole 2x2x4 slice. The times are simulated.
32 devices in a mesh: comp: 4 (over z), sub: 8 (over y, x, core).
Axes of the slice: x: 2, y: 2, z: 4, core: 2. Of those that a mesh axis runs over, the one named last changes fastest.
Arguments:
- atmos_profiles: bfloat16 [4, 72, 262144], P(None, None, ('comp', 'sub')), may hold values from -6 to 6
- atmos_mixing: bfloat16 [72, 72], replicated
- drag_factor: float32 [262144], P(('comp', 'sub')), may hold values from 0.5 to 1.5
- surface_before: float32 [4, 262144], P(None, ('comp', 'sub')), may hold values from -6 to 6
- downward_fluxes: float32 [4, 262144], P(None, ('comp', 'sub')), may hold values from -6 to 6
- land_weight: float32 [262144], P(('comp', 'sub')), may hold values from 0.05 to 1
- land_surface: float32 [4, 262144], P(None, ('comp', 'sub')), may hold values from -6 to 6
- ocean_state: float32 [4, 60, 262144], P(None, None, ('comp', 'sub')), may hold values from -6 to 6
- ocean_mixing: float32 [60, 60], replicated
- sea_mask: int32 [262144], P(('comp', 'sub')), may hold values 0 or 1
- exchange_slot: int32 [4, 262144], P(None, ('comp', 'sub')), may hold values from 0 to 65535, as said below
- parent_column: int32 [4, 262144], P(None, ('comp', 'sub')), may hold values from 0 to 8191, as said below
- ocean_weight: float32 [4, 262144], P(None, ('comp', 'sub')), may hold values from 0.1 to 1
- atmos_weight: float32 [4, 262144], P(None, ('comp', 'sub')), may hold values from 0.05 to 0.5
Outputs:
- atmos_updated: bfloat16 [4, 72, 262144], P(None, None, ('comp', 'sub'))
- ocean_updated: float32 [4, 60, 262144], P(None, None, ('comp', 'sub'))
- surface_state: float32 [4, 262144], P(None, ('comp', 'sub'))
Inputs may be any that keep to these rules, and one draw needn't show every extreme that they name: Within the 8192 cells of one device block along the second dimension, all 32768 values are distinct, at most 2048 of them share one value of exchange_slot // 2048, and in every block some value of exchange_slot // 2048 is shared by exactly 2048 of them. In every aligned group of 128 cells along the second dimension (one k), the values are t * 128 + 0, 1, ..., 127 in order, for one t. In every aligned group of 128 cells along the second dimension (one k), all values share one value of parent_column // 128.
All inputs are finite; a program needn't handle non-finite values. No bound on the sum of `sea_mask` on one device may be relied on, other than what follows from the above.
Results may differ from a plain program's by a relative error of at most 0.001.
Values sent between devices are 32-bit elements; how exact they have to be, the bound alone decides.
No kernel may reach another device: no remote copies, remote signals or barrier semaphores. Data moves between devices by JAX's collectives and lax.ppermute only.
A program may use at most 128 MiB of HBM per device.

v0:
```python
import functools

import jax
import jax.numpy as jnp
from jax import lax
from jax.experimental import pallas as pl
from jax.experimental.pallas import tpu as pltpu
from jax.sharding import PartitionSpec as P

couple_rate = 0.5
LANES = 128
params = pltpu.CompilerParams(vmem_limit_bytes=24 * 1024 * 1024)
stream_params = pltpu.CompilerParams(vmem_limit_bytes=56 * 1024 * 1024)
vmem = pl.BlockSpec(memory_space=pltpu.VMEM)
smem = pl.BlockSpec(memory_space=pltpu.SMEM)
AXES = ("far", "near", "sub")


def window(index):
    return pl.ds(pl.multiple_of(index * LANES, LANES), LANES)


def request_kernel(per_owner, slot_ref, column_ref, place_ref, wanted_ref):
    intersections, cells = slot_ref.shape
    near, spots = wanted_ref.shape
    windows = cells // LANES
    lane = lax.broadcasted_iota(jnp.int32, (intersections, windows), 1)

    def heads(ref):
        found = jnp.zeros((intersections, windows), jnp.int32)
        for step in range(windows):
            head = ref[:, step * LANES : step * LANES + 1]
            found = jnp.where(lane == step, head, found)
        return found // LANES

    place = heads(slot_ref)
    column_window = heads(column_ref)
    owner = place // per_owner
    peer = owner % near
    spot = owner // near * per_owner + place % per_owner
    place_ref[...] = peer * spots + spot
    peer_ids = lax.broadcasted_iota(jnp.int32, (near, windows), 0)
    spot_ids = lax.broadcasted_iota(jnp.int32, (spots, windows), 0)
    wanted = jnp.zeros((near, spots), jnp.float32)
    for k in range(intersections):
        row = slice(k, k + 1)
        peer_hot = jnp.where(peer_ids == peer[row], 1.0, 0.0)
        spot_hot = jnp.where(
            spot_ids == spot[row], column_window[row].astype(jnp.float32), 0.0
        )
        wanted = wanted + lax.dot_general(
            peer_hot.astype(jnp.bfloat16),
            spot_hot.astype(jnp.bfloat16),
            (((1,), (1,)), ((), ())),
            preferred_element_type=jnp.float32,
        )
    wanted_ref[...] = wanted.astype(jnp.int32)


def flux_kernel(last, x_ref, drag_ref, before_ref, down_ref, forcing_ref, tend_ref):
    def row(ref, index):
        return ref[index : index + 1, :]

    bottom = [x_ref[member].astype(jnp.float32)[last : last + 1, :] for member in range(4)]
    east = bottom[2] - row(before_ref, 2)
    north = bottom[3] - row(before_ref, 3)
    transfer = drag_ref[...] * jnp.sqrt(1.0 + east * east + north * north)
    sensible = transfer * (row(before_ref, 0) - bottom[0])
    latent = transfer * (row(before_ref, 1) - bottom[1])
    east_stress = couple_rate * (transfer * east)
    north_stress = couple_rate * (transfer * north)
    forcing_ref[0:1, :] = couple_rate * (
        row(down_ref, 0) + row(down_ref, 1) - sensible - latent
    )
    forcing_ref[1:2, :] = couple_rate * (latent - row(down_ref, 2) - row(down_ref, 3))
    forcing_ref[2:3, :] = east_stress
    forcing_ref[3:4, :] = north_stress
    tend_ref[0:1, :] = couple_rate * sensible
    tend_ref[1:2, :] = couple_rate * latent
    tend_ref[2:3, :] = -east_stress
    tend_ref[3:4, :] = -north_stress


def surface_rates(profiles, drag_factor, surface_before, downward):
    fields, levels, columns = profiles.shape
    block = min(4096, columns)
    tall = 16
    at = (levels - 1) // tall
    rows = pl.BlockSpec((fields, block), lambda i: (0, i))
    return pl.pallas_call(
        functools.partial(flux_kernel, levels - 1 - at * tall),
        grid=(columns // block,),
        in_specs=[
            pl.BlockSpec((fields, tall, block), lambda i: (0, at, i)),
            pl.BlockSpec((1, block), lambda i: (0, i)),
            rows,
            rows,
        ],
        out_specs=[rows, rows],
        out_shape=[jax.ShapeDtypeStruct((fields, columns), jnp.float32)] * 2,
        compiler_params=stream_params,
        name="surface_rates",
    )(profiles, drag_factor.reshape(1, columns), surface_before, downward)


def atmos_kernel(mix_ref, tend_ref, x_ref, out_ref):
    mix = mix_ref[...]
    lowest = mix[:, mix.shape[1] - 1 :].astype(jnp.float32)
    for member in range(x_ref.shape[0]):
        mixed = jnp.dot(mix, x_ref[member], preferred_element_type=jnp.float32)
        out_ref[member] = (mixed + lowest * tend_ref[member : member + 1, :]).astype(jnp.bfloat16)


def diffuse_atmos(profiles, mixing, tendency):
    fields, levels, columns = profiles.shape
    block = min(1024, columns)
    return pl.pallas_call(
        atmos_kernel,
        grid=(columns // block,),
        in_specs=[
            pl.BlockSpec((levels, levels), lambda i: (0, 0)),
            pl.BlockSpec((fields, block), lambda i: (0, i)),
            pl.BlockSpec((fields, levels, block), lambda i: (0, 0, i)),
        ],
        out_specs=pl.BlockSpec((fields, levels, block), lambda i: (0, 0, i)),
        out_shape=jax.ShapeDtypeStruct(profiles.shape, jnp.bfloat16),
        compiler_params=stream_params,
        cost_estimate=pl.CostEstimate(
            flops=2 * fields * levels * levels * columns,
            bytes_accessed=4 * fields * levels * columns,
            transcendentals=0,
        ),
        name="diffuse_atmos",
    )(mixing, tendency, profiles)


def top_kernel(mix_ref, x_ref, out_ref):
    levels = x_ref.shape[0]
    total = mix_ref[0, 0] * x_ref[0]
    for level in range(1, levels):
        total = total + mix_ref[0, level] * x_ref[level]
    out_ref[...] = total


def top_level(state, mixing):
    levels, fields, cells = state.shape
    block = min(1024, cells)
    return pl.pallas_call(
        top_kernel,
        grid=(cells // block,),
        in_specs=[smem, pl.BlockSpec((levels, fields, block), lambda i: (0, 0, i))],
        out_specs=pl.BlockSpec((fields, block), lambda i: (0, i)),
        out_shape=jax.ShapeDtypeStruct((fields, cells), jnp.float32),
        compiler_params=stream_params,
        cost_estimate=pl.CostEstimate(
            flops=2 * fields * levels * cells,
            bytes_accessed=4 * fields * levels * cells,
            transcendentals=0,
        ),
        name="top_level",
    )(mixing[0:1], state)


def serve_kernel(per_owner, far_ref, asked_ref, own_ref, other_ref, out_ref, blocks_ref):
    far = far_ref[0]
    blocks_ref[far] = own_ref[...]
    blocks_ref[1 - far] = other_ref[...]

    def body(peer, carry):
        for shard in range(2):
            for slot in range(per_owner):
                spot = shard * per_owner + slot
                out_ref[peer, :, spot * LANES : (spot + 1) * LANES] = blocks_ref[
                    shard, :, window(asked_ref[peer, spot])
                ]
        return carry

    lax.fori_loop(0, out_ref.shape[0], body, 0)


def split_high(values):
    high = values.astype(jnp.bfloat16).astype(jnp.float32)
    return jnp.concatenate([high, values - high], axis=0)


GROUP = 8


def middle_kernel(
    place_ref,
    corner_ref,
    arrived_ref,
    column_ref,
    ocean_weight_ref,
    atmos_weight_ref,
    mask_ref,
    base_ref,
    state_ref,
    forcing_ref,
    send_ref,
    lanes_ref,
    *share_refs,
):
    intersections, cells = column_ref.shape
    windows = cells // LANES
    fields = base_ref.shape[0]
    spots = arrived_ref.shape[2] // LANES
    send_ref[...] = jnp.zeros(send_ref.shape, jnp.float32)
    for ref in share_refs:
        ref[...] = jnp.zeros(ref.shape, jnp.float32)
    corner = corner_ref[0, 0]
    group_tiles = GROUP * intersections
    steps = LANES // intersections
    for first in range(0, windows, steps):
        tall = jnp.concatenate(
            [
                column_ref[:, (first + step) * LANES : (first + step + 1) * LANES] & (LANES - 1)
                for step in range(steps)
            ],
            axis=0,
        )
        turned = tall.astype(jnp.float32).T.astype(jnp.bfloat16)
        for part in range(steps // GROUP):
            lanes_ref[first // GROUP + part, :, :group_tiles] = turned[
                :, part * group_tiles : (part + 1) * group_tiles
            ]
    column_ids = lax.broadcasted_iota(jnp.int32, (LANES, LANES), 1)
    column_ids = column_ids.astype(jnp.float32).astype(jnp.bfloat16)
    one, zero = jnp.bfloat16(1.0), jnp.bfloat16(0.0)
    field_ids = lax.broadcasted_iota(jnp.int32, (fields, LANES), 0)
    share_rows = lax.broadcasted_iota(jnp.int32, (2 * intersections, LANES), 0)
    first_half = share_rows % intersections < 2
    blank = jnp.zeros((2 * fields, LANES), jnp.float32)
    top = 2 * fields * intersections

    def body(group, carry):
        turned = lanes_ref[group]
        for inner in range(GROUP):
            step = group * GROUP + inner
            here = window(step)
            lanes = column_ref[:, here] & (LANES - 1)
            ocean_weight = ocean_weight_ref[:, here]
            total = jnp.zeros((fields, LANES), jnp.float32)
            weight = jnp.zeros((1, LANES), jnp.float32)
            where = []
            for k in range(intersections):
                place = place_ref[k, step]
                peer, spot = place // spots, place % spots
                where.append((peer, spot))
                picked = jnp.take_along_axis(
                    arrived_ref[peer, :, window(spot)],
                    jnp.broadcast_to(lanes[k : k + 1], (fields, LANES)),
                    axis=1,
                    mode="promise_in_bounds",
                )
                total = total + ocean_weight[k : k + 1] * picked
                weight = weight + ocean_weight[k : k + 1]
            forcing = total / weight
            forcing_ref[:, here] = forcing
            mask = mask_ref[:, here]
            surface = jnp.where(
                mask == 1, base_ref[:, here] + corner * forcing, state_ref[0, :, here]
            )
            share = atmos_weight_ref[:, here] * mask.astype(jnp.float32)
            hot = []
            for k in range(intersections):
                tile = inner * intersections + k
                lane_of = jnp.broadcast_to(turned[:, tile : tile + 1], (LANES, LANES))
                hot.append(jnp.where(lane_of == column_ids, one, zero))
            hot = jnp.concatenate(
                [
                    jnp.concatenate([hot[0], hot[1]], axis=1),
                    jnp.concatenate([hot[2], hot[3]], axis=1),
                ],
                axis=0,
            )
            parts = [split_high(share[k : k + 1] * surface) for k in range(intersections)]
            share_parts = split_high(share)
            left = [parts[0], parts[1], blank, blank, jnp.where(first_half, share_parts, 0.0)]
            right = [blank, blank, parts[2], parts[3], jnp.where(first_half, 0.0, share_parts)]
            rows = jnp.concatenate(
                [jnp.concatenate(left, axis=0), jnp.concatenate(right, axis=0)], axis=1
            ).astype(jnp.bfloat16)
            spread = jnp.dot(rows, hot, preferred_element_type=jnp.float32)
            for k in range(intersections):
                peer, spot = where[k]
                side = slice((k % 2) * LANES, (k % 2 + 1) * LANES)
                at = 2 * fields * k
                send_ref[peer, :, window(spot)] = (
                    spread[at : at + fields, side] + spread[at + fields : at + 2 * fields, side]
                )
                shared = (
                    spread[top + k : top + k + 1, side]
                    + spread[top + intersections + k : top + intersections + k + 1, side]
                )
                share_refs[k][peer, :, window(spot // fields)] += jnp.where(
                    field_ids == spot % fields, shared, 0.0
                )
        return carry

    lax.fori_loop(0, windows // GROUP, body, 0)
    shares = share_refs[0][...]
    for ref in share_refs[1:]:
        shares = shares + ref[...]
    send_ref[:, :, spots * LANES :] = shares


def ocean_kernel(mix_ref, forcing_ref, mask_ref, x_ref, out_ref, high_ref, low_ref):
    levels, fields, block = x_ref.shape
    rows = levels * fields

    @pl.when(pl.program_id(0) == 0)
    def _():
        level = lax.broadcasted_iota(jnp.int32, (rows, levels), 0) // fields
        pick = (level == lax.broadcasted_iota(jnp.int32, (rows, levels), 1)).astype(jnp.float32)
        tall = jnp.dot(pick, mix_ref[...], precision=lax.Precision.HIGHEST)
        wide = lax.dot_general(
            tall, pick, (((1,), (1,)), ((), ())), precision=lax.Precision.HIGHEST
        )
        down = lax.broadcasted_iota(jnp.int32, (rows, rows), 0) % fields
        across = lax.broadcasted_iota(jnp.int32, (rows, rows), 1) % fields
        wide = jnp.where(down == across, wide, 0.0)
        high = wide.astype(jnp.bfloat16)
        high_ref[...] = high
        low_ref[...] = (wide - high.astype(jnp.float32)).astype(jnp.bfloat16)

    flat = x_ref[...].reshape(rows, block)
    push = jnp.concatenate(
        [forcing_ref[...], jnp.zeros((rows - fields, block), jnp.float32)], axis=0
    )
    loaded = flat + push
    high = loaded.astype(jnp.bfloat16)
    low = (loaded - high.astype(jnp.float32)).astype(jnp.bfloat16)
    mixed = (
        jnp.dot(high_ref[...], high, preferred_element_type=jnp.float32)
        + jnp.dot(high_ref[...], low, preferred_element_type=jnp.float32)
        + jnp.dot(low_ref[...], high, preferred_element_type=jnp.float32)
    )
    out_ref[...] = jnp.where(mask_ref[...] == 1, mixed, flat).reshape(levels, fields, block)


def diffuse_ocean(state, mixing, forcing, mask):
    levels, fields, cells = state.shape
    block = min(1024, cells)
    rows = levels * fields
    return pl.pallas_call(
        ocean_kernel,
        grid=(cells // block,),
        in_specs=[
            pl.BlockSpec(mixing.shape, lambda i: (0, 0)),
            pl.BlockSpec((fields, block), lambda i: (0, i)),
            pl.BlockSpec((1, block), lambda i: (0, i)),
            pl.BlockSpec((levels, fields, block), lambda i: (0, 0, i)),
        ],
        out_specs=pl.BlockSpec((levels, fields, block), lambda i: (0, 0, i)),
        out_shape=jax.ShapeDtypeStruct(state.shape, jnp.float32),
        scratch_shapes=[pltpu.VMEM((rows, rows), jnp.bfloat16)] * 2,
        compiler_params=stream_params,
        cost_estimate=pl.CostEstimate(
            flops=6 * rows * rows * cells,
            bytes_accessed=8 * rows * cells,
            transcendentals=0,
        ),
        name="diffuse_ocean",
    )(mixing, forcing, mask, state)


def collect_kernel(per_owner, far_ref, asked_ref, back_ref, keep_ref, send_ref, *sums):
    near, fields, _ = back_ref.shape
    columns = sums[0].shape[1]
    quarter = columns // fields
    chains = len(sums) // 4
    spots = 2 * per_owner
    for ref in sums:
        ref[...] = jnp.zeros(ref.shape, jnp.float32)

    def body(step, carry):
        for spot in range(spots):
            shard = spot // per_owner
            for chain in range(chains):
                peer = step * chains + chain
                at = window(asked_ref[peer, spot])
                tile = spots + spot // fields
                row = spot % fields
                values, shares = sums[4 * chain + shard], sums[4 * chain + 2 + shard]
                values[:, at] += back_ref[peer, :, spot * LANES : (spot + 1) * LANES]
                shares[:, at] += back_ref[
                    peer, row : row + 1, tile * LANES : (tile + 1) * LANES
                ]
        return carry

    lax.fori_loop(0, near // chains, body, 0)
    far = far_ref[0]
    total = []
    for kind in range(4):
        value = sums[kind][...]
        for chain in range(1, chains):
            value = value + sums[4 * chain + kind][...]
        total.append(value)
    for ref, first in ((keep_ref, 0), (send_ref, 1)):
        ref[:, :columns] = jnp.where(far == first, total[0], total[1])
        shares = jnp.where(far == first, total[2], total[3])
        for row in range(fields):
            ref[row : row + 1, columns : columns + quarter] = shares[
                :, row * quarter : (row + 1) * quarter
            ]


def final_kernel(keep_ref, other_ref, land_weight_ref, land_ref, out_ref):
    fields, columns = out_ref.shape
    quarter = columns // fields
    both = keep_ref[:, :columns] + other_ref[:, :columns]
    shares = keep_ref[:, columns:] + other_ref[:, columns:]
    land_weight = land_weight_ref[...]
    total = both + land_weight * land_ref[...]
    for row in range(fields):
        part = slice(row * quarter, (row + 1) * quarter)
        out_ref[:, part] = total[:, part] / (shares[row : row + 1] + land_weight[:, part])


def per_device(
    atmos_profiles,
    atmos_mixing,
    drag_factor,
    surface_before,
    downward_fluxes,
    land_weight,
    land_surface,
    ocean_state,
    ocean_mixing,
    sea_mask,
    exchange_slot,
    parent_column,
    ocean_weight,
    atmos_weight,
):
    near = lax.axis_size("near") * lax.axis_size("sub")
    devices = 2 * near
    fields, _, columns = atmos_profiles.shape
    intersections, cells = exchange_slot.shape
    capacity = 2 * intersections * cells // devices
    per_owner = capacity // LANES
    spots = 2 * per_owner
    mask = sea_mask.reshape(1, cells)
    state = ocean_state.transpose(1, 0, 2)
    far = lax.axis_index("far").astype(jnp.int32).reshape(1)

    def to_near(values):
        return lax.all_to_all(values, ("near", "sub"), split_axis=0, concat_axis=0, tiled=True)

    def to_far(values):
        return lax.ppermute(values, "far", ((0, 1), (1, 0)))

    place, wanted = pl.pallas_call(
        functools.partial(request_kernel, per_owner),
        in_specs=[vmem] * 2,
        out_specs=[vmem] * 2,
        out_shape=[
            jax.ShapeDtypeStruct((intersections, cells // LANES), jnp.int32),
            jax.ShapeDtypeStruct((near, spots), jnp.int32),
        ],
        compiler_params=params,
        name="requests",
    )(exchange_slot, parent_column)
    asked = to_near(wanted)
    forcing_rows, tendency = surface_rates(
        atmos_profiles, drag_factor, surface_before, downward_fluxes
    )
    other_rows = to_far(forcing_rows)
    served = pl.pallas_call(
        functools.partial(serve_kernel, per_owner),
        in_specs=[smem, smem, vmem, vmem],
        out_specs=vmem,
        out_shape=jax.ShapeDtypeStruct((near, fields, spots * LANES), jnp.float32),
        scratch_shapes=[pltpu.VMEM((2, fields, columns), jnp.float32)],
        compiler_params=params,
        name="serve_windows",
    )(far, asked, forcing_rows, other_rows)
    arrived = to_near(served)
    base = top_level(state, ocean_mixing)
    atmos_updated = diffuse_atmos(atmos_profiles, atmos_mixing, tendency)
    arrived, atmos_updated, base = lax.optimization_barrier((arrived, atmos_updated, base))

    def whole(*shape):
        return pl.BlockSpec(shape, lambda i: (0,) * len(shape))

    lanes_out = (spots + spots // fields) * LANES
    forcing, send = pl.pallas_call(
        middle_kernel,
        grid=(1,),
        in_specs=[
            smem,
            smem,
            whole(near, fields, spots * LANES),
            whole(intersections, cells),
            whole(intersections, cells),
            whole(intersections, cells),
            whole(1, cells),
            whole(fields, cells),
            whole(1, fields, cells),
        ],
        out_specs=[whole(fields, cells), whole(near, fields, lanes_out)],
        out_shape=[
            jax.ShapeDtypeStruct((fields, cells), jnp.float32),
            jax.ShapeDtypeStruct((near, fields, lanes_out), jnp.float32),
        ],
        scratch_shapes=[pltpu.VMEM((cells // LANES // GROUP, LANES, LANES), jnp.bfloat16)]
        + [pltpu.VMEM((near, fields, spots // fields * LANES), jnp.float32)] * intersections,
        compiler_params=params,
        name="forcing_and_windows",
    )(
        place,
        ocean_mixing[0:1, 0:1],
        arrived,
        parent_column,
        ocean_weight,
        atmos_weight,
        mask,
        base,
        state,
    )
    back = to_near(send)
    ocean_updated = diffuse_ocean(state, ocean_mixing, forcing, mask).transpose(1, 0, 2)
    back, ocean_updated = lax.optimization_barrier((back, ocean_updated))

    chains = 2
    packed = (fields, columns + columns // fields)
    keep, away = pl.pallas_call(
        functools.partial(collect_kernel, per_owner),
        in_specs=[smem, smem, vmem],
        out_specs=[vmem] * 2,
        out_shape=[jax.ShapeDtypeStruct(packed, jnp.float32)] * 2,
        scratch_shapes=(
            [pltpu.VMEM((fields, columns), jnp.float32)] * 2
            + [pltpu.VMEM((1, columns), jnp.float32)] * 2
        )
        * chains,
        compiler_params=params,
        name="collect_windows",
    )(far, asked, back)
    surface_state = pl.pallas_call(
        final_kernel,
        in_specs=[vmem] * 4,
        out_specs=vmem,
        out_shape=jax.ShapeDtypeStruct((fields, columns), jnp.float32),
        compiler_params=params,
        name="surface_state",
    )(keep, to_far(away), land_weight.reshape(1, columns), land_surface)
    return (atmos_updated, ocean_updated, surface_state)


def solution(mesh):
    comp, sub = mesh.devices.shape
    halves = jax.sharding.Mesh(mesh.devices.reshape(2, comp // 2, sub), AXES)
    split = P(None, AXES)
    return jax.shard_map(
        per_device,
        mesh=halves,
        in_specs=(
            P(None, None, AXES),
            P(),
            P(AXES),
            split,
            split,
            P(AXES),
            split,
            P(None, None, AXES),
            P(),
            P(AXES),
            split,
            split,
            split,
            split,
        ),
        out_specs=(P(None, None, AXES), P(None, None, AXES), split),
        check_vma=False,
    )
```

profile of v0, /device:TPU:0, one launch (start us, length us, event | category | flops | bytes accessed | tf_op | source)
XLA Modules:
  0.0 93.9 jit_solution(16508237341491230027)
XLA Ops:
  0.6 0.0 copy-start.2
  0.6 0.0 copy-start.9
  0.7 2.0 %surface_rates.1 = (f32[4,8192]{1,0:T(4,128)}, f32[4,8192]{1,0:T(4,128)}) custom-call(bf16[4,72,8192]{2,1,0:T(8,128)(2,1)} %x_ref.3, f32[1,8192]{1,0:T(1,128)} %bitcast.19, f32[4,8192]{1,0:T(4,128)} %before_ref.1, f32[4,8192]{1,0:T(4,128)} %down_ref.1), custom_call_target="tpu_custom_call" | custom-call | tf_op jit(solution)/shard_map/surface_rates/pallas_call | solution.py:90
  2.6 4.0 %collective-permute-start = (f32[4,8192]{1,0:T(4,128)}, f32[4,8192]{1,0:T(4,128)S(1)}, u32[]{:S(2)}, u32[]{:S(2)}) collective-permute-start(f32[4,8192]{1,0:T(4,128)} %get-tuple-element.17.own_ref), channel_id=1, source_target_pairs={{0,16},{16,0},{1,17},{17,1},{2,18},{18,2},{3,19},{19,3},{4,20},{20... | collective-permute-start | bytes 393224 | tf_op jit(solution)/shard_map/ppermute | solution.py:452
  6.7 0.0 copy-done.2
  6.7 0.0 copy-done.9
  6.7 0.9 %requests.1 = (s32[4,64]{1,0:T(4,128)S(1)}, s32[16,32]{1,0:T(8,128)}) custom-call(s32[4,8192]{1,0:T(4,128)S(1)} %copy-done.9, s32[4,8192]{1,0:T(4,128)S(1)} %copy-done.2), custom_call_target="tpu_custom_call" | custom-call | tf_op jit(solution)/shard_map/requests/pallas_call | solution.py:454
  7.6 4.8 %all-to-all-start = ((s32[16,1,32]{2,1,0:T(1,128)}), s32[16,1,32]{2,1,0:T(1,128)S(1)}, u32[]{:S(2)}, u32[]{:S(2)}) async-start(s32[16,1,32]{2,1,0:T(1,128)} %bitcast.2), calls=%async_computation | async-start | bytes 16384 | tf_op jit(solution)/shard_map/all_to_all | solution.py:449
  12.5 5.4 %all-to-all-done = s32[16,1,32]{2,1,0:T(1,128)S(1)} async-done(((s32[16,1,32]{2,1,0:T(1,128)}), s32[16,1,32]{2,1,0:T(1,128)S(1)}, u32[]{:S(2)}, u32[]{:S(2)}) %all-to-all-start) | async-done | bytes 2080 | tf_op jit(solution)/shard_map/all_to_all | solution.py:449
  17.9 0.0 collective-permute-done.other_ref
  17.9 0.9 copy-done.8
  18.8 2.6 %serve_windows.1 = f32[16,4,4096]{2,1,0:T(4,128)} custom-call(s32[1]{0:T(128)} %bitcast.far_ref, s32[16,32]{1,0:T(8,128)S(1)} %bitcast.15, f32[4,8192]{1,0:T(4,128)S(1)} %copy-done.8, f32[4,8192]{1,0:T(4,128)S(1)} %collective-permute-done.other_ref), custom_call_target="tpu_custom_call" | custom-call | tf_op jit(solution)/shard_map/serve_windows/pallas_call | solution.py:470
  21.4 3.7 %all-to-all-start.1 = ((f32[16,4,4096]{2,1,0:T(4,128)}), f32[16,4,4096]{2,1,0:T(4,128)S(1)}, u32[]{:S(2)}, u32[]{:S(2)}) async-start(f32[16,4,4096]{2,1,0:T(4,128)} %serve_windows.1), calls=%async_computation.1 | async-start | bytes 2097152 | tf_op jit(solution)/shard_map/all_to_all | solution.py:449
  25.0 1.2 %slice.7.corner_ref = f32[1,1]{1,0:T(1,128)} slice(f32[60,60]{1,0:T(8,128)} %mix_ref.3), slice={[0:1], [0:1]} | slice | bytes 8 | tf_op jit(solution)/shard_map/slice | solution.py:513
  26.2 1.2 %slice.6.mix_ref = f32[1,60]{1,0:T(1,128)} slice(f32[60,60]{1,0:T(8,128)} %mix_ref.3), slice={[0:1], [0:60]} | slice | bytes 480 | tf_op jit(solution)/shard_map/slice | solution.py:161
  27.4 6.7 %top_level.1.base_ref = f32[4,8192]{1,0:T(4,128)} custom-call(f32[1,60]{1,0:T(1,128)} %slice.6.mix_ref, f32[60,4,8192]{2,1,0:T(4,128)} %bitcast.10), custom_call_target="tpu_custom_call" | custom-call | flops 3932160 | bytes 7864320 | tf_op jit(solution)/shard_map/top_level/pallas_call | solution.py:148
  34.2 0.0 copy-start.6
  34.2 8.0 %diffuse_atmos.1 = bf16[4,72,8192]{2,1,0:T(8,128)(2,1)} custom-call(bf16[72,72]{1,0:T(8,128)(2,1)} %mix_ref.2, f32[4,8192]{1,0:T(4,128)} %get-tuple-element.18.tend_ref, bf16[4,72,8192]{2,1,0:T(8,128)(2,1)} %x_ref.3), custom_call_target="tpu_custom_call" | custom-call | flops 339738624 | bytes 9437184 | tf_op jit(solution)/shard_map/diffuse_atmos/pallas_call | solution.py:117
  42.1 0.0 all-to-all-done.1.arrived_ref
  42.2 0.0 copy-start
  42.2 3.2 %copy-done = f32[4,60,8192]{2,0,1:T(4,128)S(1)} copy-done((f32[4,60,8192]{2,0,1:T(4,128)S(1)}, f32[4,60,8192]{2,0,1:T(4,128)}, u32[]{:S(2)}) %copy-start) | copy-done | bytes 7864344
  45.4 10.3 %forcing_and_windows.1 = (f32[4,8192]{1,0:T(4,128)S(1)}, f32[16,4,5120]{2,1,0:T(4,128)}) custom-call(s32[4,64]{1,0:T(4,128)S(1)} %get-tuple-element.20.place_ref, f32[1,1]{1,0:T(1,128)} %slice.7.corner_ref, f32[16,4,4096]{2,1,0:T(4,128)S(1)} %all-to-all-done.1.arrived_ref, s32[4,8192]{1,0:T(4,128)S(1)} %copy-done.2, f32[4,8192]{1,0:T(4,128)S(1)} %copy-done.3, ...), custom_call_target="tpu_custom_call" | custom-call | tf_op jit(solution)/shard_map/forcing_and_windows/pallas_call | solution.py:488
  55.7 0.7 copy-done.5
  56.4 5.1 %all-to-all-start.2 = ((f32[16,4,5120]{2,1,0:T(4,128)}), f32[16,4,5120]{2,1,0:T(4,128)S(1)}, u32[]{:S(2)}, u32[]{:S(2)}) async-start(f32[16,4,5120]{2,1,0:T(4,128)} %get-tuple-element.23), calls=%async_computation.2 | async-start | bytes 2621440 | tf_op jit(solution)/shard_map/all_to_all | solution.py:449
  61.5 0.0 copy-start.7
  61.5 0.0 copy-start.10
  61.5 11.5 %diffuse_ocean.1 = f32[60,4,8192]{2,1,0:T(4,128)} custom-call(f32[60,60]{1,0:T(8,128)} %mix_ref.3, f32[4,8192]{1,0:T(4,128)} %copy-done.5, s32[1,8192]{1,0:T(1,128)} %bitcast.13, f32[60,4,8192]{2,1,0:T(4,128)} %bitcast.11), custom_call_target="tpu_custom_call" | custom-call | flops 2831155200 | bytes 15728640 | tf_op jit(solution)/shard_map/diffuse_ocean/pallas_call | solution.py:346
  73.0 7.8 %all-to-all-done.2.back_ref = f32[16,4,5120]{2,1,0:T(4,128)S(1)} async-done(((f32[16,4,5120]{2,1,0:T(4,128)}), f32[16,4,5120]{2,1,0:T(4,128)S(1)}, u32[]{:S(2)}, u32[]{:S(2)}) %all-to-all-start.2) | async-done | bytes 1310752 | tf_op jit(solution)/shard_map/all_to_all | solution.py:449
  80.8 2.3 %collect_windows.1 = (f32[4,10240]{1,0:T(4,128)S(1)}, f32[4,10240]{1,0:T(4,128)S(1)}) custom-call(s32[1]{0:T(128)} %bitcast.far_ref, s32[16,32]{1,0:T(8,128)S(1)} %bitcast.16, f32[16,4,5120]{2,1,0:T(4,128)S(1)} %all-to-all-done.2.back_ref), custom_call_target="tpu_custom_call" | custom-call | tf_op jit(solution)/shard_map/collect_windows/pallas_call | solution.py:528
  83.1 0.4 collective-permute-start.1
  83.5 9.8 %collective-permute-done.1.other_ref = f32[4,10240]{1,0:T(4,128)S(1)} collective-permute-done((f32[4,10240]{1,0:T(4,128)S(1)}, f32[4,10240]{1,0:T(4,128)S(1)}, u32[]{:S(2)}, u32[]{:S(2)}) %collective-permute-start.1) | collective-permute-done | bytes 163872 | tf_op jit(solution)/shard_map/ppermute | solution.py:452
  93.2 0.7 surface_state.1
  (11 shorter events, 0.0 us)
Async XLA Ops:
  0.6 6.1 %copy-start.2 = (s32[4,8192]{1,0:T(4,128)S(1)}, s32[4,8192]{1,0:T(4,128)}, u32[]{:S(2)}) copy-start(s32[4,8192]{1,0:T(4,128)} %column_ref.3) | copy-start | bytes 393220
  0.6 6.0 %copy-start.9 = (s32[4,8192]{1,0:T(4,128)S(1)}, s32[4,8192]{1,0:T(4,128)}, u32[]{:S(2)}) copy-start(s32[4,8192]{1,0:T(4,128)} %slot_ref.1) | copy-start | bytes 393220
  2.6 15.3 %collective-permute-start = (f32[4,8192]{1,0:T(4,128)}, f32[4,8192]{1,0:T(4,128)S(1)}, u32[]{:S(2)}, u32[]{:S(2)}) collective-permute-start(f32[4,8192]{1,0:T(4,128)} %get-tuple-element.17.own_ref), channel_id=1, source_target_pairs={{0,16},{16,0},{1,17},{17,1},{2,18},{18,2},{3,19},{19,3},{4,20},{20... | collective-permute-start | bytes 393224 | tf_op jit(solution)/shard_map/ppermute | solution.py:452
  7.6 10.3 %all-to-all-start = ((s32[16,1,32]{2,1,0:T(1,128)}), s32[16,1,32]{2,1,0:T(1,128)S(1)}, u32[]{:S(2)}, u32[]{:S(2)}) async-start(s32[16,1,32]{2,1,0:T(1,128)} %bitcast.2), calls=%async_computation | async-start | bytes 16384 | tf_op jit(solution)/shard_map/all_to_all | solution.py:449
  17.9 0.9 copy-start.8
  21.4 20.8 %all-to-all-start.1 = ((f32[16,4,4096]{2,1,0:T(4,128)}), f32[16,4,4096]{2,1,0:T(4,128)S(1)}, u32[]{:S(2)}, u32[]{:S(2)}) async-start(f32[16,4,4096]{2,1,0:T(4,128)} %serve_windows.1), calls=%async_computation.1 | async-start | bytes 2097152 | tf_op jit(solution)/shard_map/all_to_all | solution.py:449
  34.2 8.0 %copy-start.1 = (f32[4,8192]{1,0:T(4,128)S(1)}, f32[4,8192]{1,0:T(4,128)}, u32[]{:S(2)}) copy-start(f32[4,8192]{1,0:T(4,128)} %top_level.1.base_ref) | copy-start | bytes 393220
  34.2 8.0 %copy-start.3 = (f32[4,8192]{1,0:T(4,128)S(1)}, f32[4,8192]{1,0:T(4,128)}, u32[]{:S(2)}) copy-start(f32[4,8192]{1,0:T(4,128)} %ocean_weight_ref.1) | copy-start | bytes 393220
  34.2 8.0 %copy-start.4 = (f32[4,8192]{1,0:T(4,128)S(1)}, f32[4,8192]{1,0:T(4,128)}, u32[]{:S(2)}) copy-start(f32[4,8192]{1,0:T(4,128)} %atmos_weight_ref.1) | copy-start | bytes 393220
  34.2 8.0 %copy-start.6 = (s32[8192]{0:T(1024)S(1)}, s32[8192]{0:T(1024)}, u32[]{:S(2)}) copy-start(s32[8192]{0:T(1024)} %param.23) | copy-start | bytes 98308
  42.2 3.2 %copy-start = (f32[4,60,8192]{2,0,1:T(4,128)S(1)}, f32[4,60,8192]{2,0,1:T(4,128)}, u32[]{:S(2)}) copy-start(f32[4,60,8192]{2,0,1:T(4,128)} %param.21) | copy-start | bytes 23592964
  55.7 0.7 copy-start.5
  56.4 24.4 %all-to-all-start.2 = ((f32[16,4,5120]{2,1,0:T(4,128)}), f32[16,4,5120]{2,1,0:T(4,128)S(1)}, u32[]{:S(2)}, u32[]{:S(2)}) async-start(f32[16,4,5120]{2,1,0:T(4,128)} %get-tuple-element.23), calls=%async_computation.2 | async-start | bytes 2621440 | tf_op jit(solution)/shard_map/all_to_all | solution.py:449
  61.5 31.7 %copy-start.7 = (f32[4,8192]{1,0:T(4,128)S(1)}, f32[4,8192]{1,0:T(4,128)}, u32[]{:S(2)}) copy-start(f32[4,8192]{1,0:T(4,128)} %land_ref.1) | copy-start | bytes 393220
  61.5 31.7 %copy-start.10 = (f32[8192]{0:T(1024)S(1)}, f32[8192]{0:T(1024)}, u32[]{:S(2)}) copy-start(f32[8192]{0:T(1024)} %param.19) | copy-start | bytes 98308
  83.1 10.1 %collective-permute-start.1 = (f32[4,10240]{1,0:T(4,128)S(1)}, f32[4,10240]{1,0:T(4,128)S(1)}, u32[]{:S(2)}, u32[]{:S(2)}) collective-permute-start(f32[4,10240]{1,0:T(4,128)S(1)} %get-tuple-element.28), channel_id=1, source_target_pairs={{0,16},{16,0},{1,17},{17,1},{2,18},{18,2},{3,19},{19,3},{4,20},{20... | collective-permute-start | bytes 491528 | tf_op jit(solution)/shard_map/ppermute | solution.py:452
where the time goes:
time: 95 us; the launch traced here: 93.9 us
  Pallas kernels  45 us (47%)
  waiting for transfers between devices  23 us (24%)
  starting transfers between devices  18 us (19%)
  local copies, waits for them, and re-layouts  7.25 us (8%)
    all_to_all x3, starting transfers between devices, to_near(): lax.all_to_all(values, ('near', 'sub'), split_axis=0, concat_axis=0, tile...  13.6 us
    all_to_all x3, waiting for transfers between devices, to_near(): lax.all_to_all(values, ('near', 'sub'), split_axis=0, concat_axis=0, tile...  13.2 us
    pallas_call x1, Pallas kernels, diffuse_ocean(): pl.pallas_call(ocean_kernel, grid=(cells // block,), in_specs=[pl.BlockSp...  11.5 us
    pallas_call x1, Pallas kernels, per_device(): pl.pallas_call(middle_kernel, grid=(1,), in_specs=[smem, smem, whole(near...  10.3 us
    ppermute x2, waiting for transfers between devices, to_far(): return lax.ppermute(values, 'far', ((0, 1), (1, 0)))  9.76 us
    pallas_call x1, Pallas kernels, diffuse_atmos(): pl.pallas_call(atmos_kernel, grid=(columns // block,), in_specs=[pl.Block...  7.97 us
    pallas_call x1, Pallas kernels, top_level(): pl.pallas_call(top_kernel, grid=(cells // block,), in_specs=[smem, pl.Blo...  6.71 us
    unnamed x22, local copies, waits for them, and re-layouts  4.83 us
  transfers between devices with their start and end apart: 5, of which 3 were waited for; matrix products, arithmetic and copies ran while one was open for 3% of the time, Pallas kernels for 29%

commit v1 on v0

--- a/solution.py
+++ b/solution.py
@@ -20,7 +20,7 @@
     return pl.ds(pl.multiple_of(index * LANES, LANES), LANES)
 
 
-def request_kernel(per_owner, slot_ref, column_ref, place_ref, wanted_ref):
+def request_kernel(per_owner, slot_ref, column_ref, place_ref, spot_ref, wanted_ref):
     intersections, cells = slot_ref.shape
     near, spots = wanted_ref.shape
     windows = cells // LANES
@@ -38,7 +38,8 @@
     owner = place // per_owner
     peer = owner % near
     spot = owner // near * per_owner + place % per_owner
-    place_ref[...] = peer * spots + spot
+    place_ref[...] = place
+    spot_ref[...] = peer * spots + spot
     peer_ids = lax.broadcasted_iota(jnp.int32, (near, windows), 0)
     spot_ids = lax.broadcasted_iota(jnp.int32, (spots, windows), 0)
     wanted = jnp.zeros((near, spots), jnp.float32)
@@ -103,25 +104,30 @@
     )(profiles, drag_factor.reshape(1, columns), surface_before, downward)
 
 
-def atmos_kernel(mix_ref, tend_ref, x_ref, out_ref):
+def atmos_kernel(mix_ref, tend_ref, *refs):
     mix = mix_ref[...]
     lowest = mix[:, mix.shape[1] - 1 :].astype(jnp.float32)
-    for member in range(x_ref.shape[0]):
-        mixed = jnp.dot(mix, x_ref[member], preferred_element_type=jnp.float32)
+    out_ref = refs[-1]
+    for member, x_ref in enumerate(refs[:-1]):
+        mixed = jnp.dot(mix, x_ref[0], preferred_element_type=jnp.float32)
         out_ref[member] = (mixed + lowest * tend_ref[member : member + 1, :]).astype(jnp.bfloat16)
 
 
 def diffuse_atmos(profiles, mixing, tendency):
     fields, levels, columns = profiles.shape
-    block = min(1024, columns)
+    block = min(2048, columns)
+
+    def field(member):
+        return pl.BlockSpec((1, levels, block), lambda i: (member, 0, i))
+
     return pl.pallas_call(
         atmos_kernel,
         grid=(columns // block,),
         in_specs=[
             pl.BlockSpec((levels, levels), lambda i: (0, 0)),
             pl.BlockSpec((fields, block), lambda i: (0, i)),
-            pl.BlockSpec((fields, levels, block), lambda i: (0, 0, i)),
-        ],
+        ]
+        + [field(member) for member in range(fields)],
         out_specs=pl.BlockSpec((fields, levels, block), lambda i: (0, 0, i)),
         out_shape=jax.ShapeDtypeStruct(profiles.shape, jnp.bfloat16),
         compiler_params=stream_params,
@@ -131,26 +137,41 @@
             transcendentals=0,
         ),
         name="diffuse_atmos",
-    )(mixing, tendency, profiles)
-
-
-def top_kernel(mix_ref, x_ref, out_ref):
-    levels = x_ref.shape[0]
-    total = mix_ref[0, 0] * x_ref[0]
-    for level in range(1, levels):
-        total = total + mix_ref[0, level] * x_ref[level]
-    out_ref[...] = total
+    )(mixing, tendency, *[profiles] * fields)
+
+
+def level_specs(levels, fields, block):
+    count = 4 if levels % 4 == 0 else 1
+
+    def part(number):
+        return pl.BlockSpec((levels // count, fields, block), lambda i: (number, 0, i))
+
+    return [part(number) for number in range(count)]
+
+
+def top_kernel(mix_ref, *refs):
+    state_refs, base_ref, first_ref = refs[:-2], refs[-2], refs[-1]
+    total = None
+    level = 0
+    for ref in state_refs:
+        for inner in range(ref.shape[0]):
+            term = mix_ref[0, level] * ref[inner]
+            total = term if total is None else total + term
+            level += 1
+    base_ref[...] = total
+    first_ref[...] = state_refs[0][0]
 
 
 def top_level(state, mixing):
     levels, fields, cells = state.shape
-    block = min(1024, cells)
+    block = min(2048, cells)
+    specs = level_specs(levels, fields, block)
     return pl.pallas_call(
         top_kernel,
         grid=(cells // block,),
-        in_specs=[smem, pl.BlockSpec((levels, fields, block), lambda i: (0, 0, i))],
-        out_specs=pl.BlockSpec((fields, block), lambda i: (0, i)),
-        out_shape=jax.ShapeDtypeStruct((fields, cells), jnp.float32),
+        in_specs=[smem] + specs,
+        out_specs=[pl.BlockSpec((fields, block), lambda i: (0, i))] * 2,
+        out_shape=[jax.ShapeDtypeStruct((fields, cells), jnp.float32)] * 2,
         compiler_params=stream_params,
         cost_estimate=pl.CostEstimate(
             flops=2 * fields * levels * cells,
@@ -158,7 +179,7 @@
             transcendentals=0,
         ),
         name="top_level",
-    )(mixing[0:1], state)
+    )(mixing, *[state] * len(specs))
 
 
 def serve_kernel(per_owner, far_ref, asked_ref, own_ref, other_ref, out_ref, blocks_ref):
@@ -170,9 +191,7 @@
         for shard in range(2):
             for slot in range(per_owner):
                 spot = shard * per_owner + slot
-                out_ref[peer, :, spot * LANES : (spot + 1) * LANES] = blocks_ref[
-                    shard, :, window(asked_ref[peer, spot])
-                ]
+                out_ref[peer, spot] = blocks_ref[shard, :, window(asked_ref[peer, spot])]
         return carry
 
     lax.fori_loop(0, out_ref.shape[0], body, 0)
@@ -187,8 +206,10 @@
 
 
 def middle_kernel(
+    far_ref,
     place_ref,
-    corner_ref,
+    spot_ref,
+    mix_ref,
     arrived_ref,
     column_ref,
     ocean_weight_ref,
@@ -197,18 +218,20 @@
     base_ref,
     state_ref,
     forcing_ref,
-    send_ref,
+    away_ref,
+    home_ref,
     lanes_ref,
+    value_ref,
     *share_refs,
 ):
     intersections, cells = column_ref.shape
     windows = cells // LANES
     fields = base_ref.shape[0]
-    spots = arrived_ref.shape[2] // LANES
-    send_ref[...] = jnp.zeros(send_ref.shape, jnp.float32)
-    for ref in share_refs:
+    near, packed = away_ref.shape[:2]
+    per_owner = packed * fields // (fields + 1)
+    for ref in (value_ref, *share_refs):
         ref[...] = jnp.zeros(ref.shape, jnp.float32)
-    corner = corner_ref[0, 0]
+    corner = mix_ref[0, 0]
     group_tiles = GROUP * intersections
     steps = LANES // intersections
     for first in range(0, windows, steps):
@@ -244,11 +267,9 @@
             weight = jnp.zeros((1, LANES), jnp.float32)
             where = []
             for k in range(intersections):
-                place = place_ref[k, step]
-                peer, spot = place // spots, place % spots
-                where.append((peer, spot))
+                where.append(place_ref[k, step])
                 picked = jnp.take_along_axis(
-                    arrived_ref[peer, :, window(spot)],
+                    arrived_ref[spot_ref[k, step]],
                     jnp.broadcast_to(lanes[k : k + 1], (fields, LANES)),
                     axis=1,
                     mode="promise_in_bounds",
@@ -259,7 +280,7 @@
             forcing_ref[:, here] = forcing
             mask = mask_ref[:, here]
             surface = jnp.where(
-                mask == 1, base_ref[:, here] + corner * forcing, state_ref[0, :, here]
+                mask == 1, base_ref[:, here] + corner * forcing, state_ref[:, here]
             )
             share = atmos_weight_ref[:, here] * mask.astype(jnp.float32)
             hot = []
@@ -283,30 +304,37 @@
             ).astype(jnp.bfloat16)
             spread = jnp.dot(rows, hot, preferred_element_type=jnp.float32)
             for k in range(intersections):
-                peer, spot = where[k]
+                place = where[k]
                 side = slice((k % 2) * LANES, (k % 2 + 1) * LANES)
                 at = 2 * fields * k
-                send_ref[peer, :, window(spot)] = (
+                value_ref[place] = (
                     spread[at : at + fields, side] + spread[at + fields : at + 2 * fields, side]
                 )
                 shared = (
                     spread[top + k : top + k + 1, side]
                     + spread[top + intersections + k : top + intersections + k + 1, side]
                 )
-                share_refs[k][peer, :, window(spot // fields)] += jnp.where(
-                    field_ids == spot % fields, shared, 0.0
+                share_refs[k][lax.div(place, fields)] += jnp.where(
+                    field_ids == lax.rem(place, fields), shared, 0.0
                 )
         return carry
 
     lax.fori_loop(0, windows // GROUP, body, 0)
-    shares = share_refs[0][...]
-    for ref in share_refs[1:]:
-        shares = shares + ref[...]
-    send_ref[:, :, spots * LANES :] = shares
-
-
-def ocean_kernel(mix_ref, forcing_ref, mask_ref, x_ref, out_ref, high_ref, low_ref):
-    levels, fields, block = x_ref.shape
+    far = far_ref[0]
+    rows = per_owner // fields
+    for ref, shard in ((away_ref, 1 - far), (home_ref, far)):
+        values = value_ref[pl.ds(shard * near * per_owner, near * per_owner)]
+        ref[:, :per_owner] = values.reshape(near, per_owner, fields, LANES)
+        at = pl.ds(shard * near * rows, near * rows)
+        shares = share_refs[0][at]
+        for share_ref in share_refs[1:]:
+            shares = shares + share_ref[at]
+        ref[:, per_owner:] = shares.reshape(near, rows, fields, LANES)
+
+
+def ocean_kernel(mix_ref, forcing_ref, mask_ref, *refs):
+    x_refs, (out_ref, high_ref, low_ref) = refs[:-3], refs[-3:]
+    levels, fields, block = out_ref.shape
     rows = levels * fields
 
     @pl.when(pl.program_id(0) == 0)
@@ -324,7 +352,9 @@
         high_ref[...] = high
         low_ref[...] = (wide - high.astype(jnp.float32)).astype(jnp.bfloat16)
 
-    flat = x_ref[...].reshape(rows, block)
+    flat = jnp.concatenate(
+        [ref[...].reshape(rows // len(x_refs), block) for ref in x_refs], axis=0
+    )
     push = jnp.concatenate(
         [forcing_ref[...], jnp.zeros((rows - fields, block), jnp.float32)], axis=0
     )
@@ -343,6 +373,7 @@
     levels, fields, cells = state.shape
     block = min(1024, cells)
     rows = levels * fields
+    specs = level_specs(levels, fields, block)
     return pl.pallas_call(
         ocean_kernel,
         grid=(cells // block,),
@@ -350,8 +381,8 @@
             pl.BlockSpec(mixing.shape, lambda i: (0, 0)),
             pl.BlockSpec((fields, block), lambda i: (0, i)),
             pl.BlockSpec((1, block), lambda i: (0, i)),
-            pl.BlockSpec((levels, fields, block), lambda i: (0, 0, i)),
-        ],
+        ]
+        + specs,
         out_specs=pl.BlockSpec((levels, fields, block), lambda i: (0, 0, i)),
         out_shape=jax.ShapeDtypeStruct(state.shape, jnp.float32),
         scratch_shapes=[pltpu.VMEM((rows, rows), jnp.bfloat16)] * 2,
@@ -362,48 +393,52 @@
             transcendentals=0,
         ),
         name="diffuse_ocean",
-    )(mixing, forcing, mask, state)
-
-
-def collect_kernel(per_owner, far_ref, asked_ref, back_ref, keep_ref, send_ref, *sums):
-    near, fields, _ = back_ref.shape
+    )(mixing, forcing, mask, *[state] * len(specs))
+
+
+def collect_kernel(per_owner, home, far_ref, asked_ref, back_ref, out_ref, *sums):
+    near, packed, fields, _ = back_ref.shape
     columns = sums[0].shape[1]
     quarter = columns // fields
-    chains = len(sums) // 4
-    spots = 2 * per_owner
+    chains = len(sums) // 2
+    far = far_ref[0]
+    first = (far if home else 1 - far) * per_owner
     for ref in sums:
         ref[...] = jnp.zeros(ref.shape, jnp.float32)
 
     def body(step, carry):
-        for spot in range(spots):
-            shard = spot // per_owner
+        for slot in range(per_owner):
             for chain in range(chains):
                 peer = step * chains + chain
-                at = window(asked_ref[peer, spot])
-                tile = spots + spot // fields
-                row = spot % fields
-                values, shares = sums[4 * chain + shard], sums[4 * chain + 2 + shard]
-                values[:, at] += back_ref[peer, :, spot * LANES : (spot + 1) * LANES]
-                shares[:, at] += back_ref[
-                    peer, row : row + 1, tile * LANES : (tile + 1) * LANES
-                ]
+                at = window(asked_ref[peer, first + slot])
+                tile, row = per_owner + slot // fields, slot % fields
+                sums[chain][:, at] += back_ref[peer, slot]
+                sums[chains + chain][:, at] += back_ref[peer, tile, row : row + 1]
         return carry
 
     lax.fori_loop(0, near // chains, body, 0)
-    far = far_ref[0]
-    total = []
-    for kind in range(4):
-        value = sums[kind][...]
-        for chain in range(1, chains):
-            value = value + sums[4 * chain + kind][...]
-        total.append(value)
-    for ref, first in ((keep_ref, 0), (send_ref, 1)):
-        ref[:, :columns] = jnp.where(far == first, total[0], total[1])
-        shares = jnp.where(far == first, total[2], total[3])
-        for row in range(fields):
-            ref[row : row + 1, columns : columns + quarter] = shares[
-                :, row * quarter : (row + 1) * quarter
-            ]
+    values, shares = sums[0][...], sums[chains][...]
+    for chain in range(1, chains):
+        values = values + sums[chain][...]
+        shares = shares + sums[chains + chain][...]
+    out_ref[:, :columns] = values
+    for row in range(fields):
+        out_ref[row : row + 1, columns:] = shares[:, row * quarter : (row + 1) * quarter]
+
+
+def collect(asked, far, back, per_owner, columns, home):
+    fields = back.shape[2]
+    chains = 4
+    return pl.pallas_call(
+        functools.partial(collect_kernel, per_owner, home),
+        in_specs=[smem, smem, vmem],
+        out_specs=vmem,
+        out_shape=jax.ShapeDtypeStruct((fields, columns + columns // fields), jnp.float32),
+        scratch_shapes=[pltpu.VMEM((fields, columns), jnp.float32)] * chains
+        + [pltpu.VMEM((1, columns), jnp.float32)] * chains,
+        compiler_params=params,
+        name="collect_home" if home else "collect_away",
+    )(far, asked, back)
 
 
 def final_kernel(keep_ref, other_ref, land_weight_ref, land_ref, out_ref):
@@ -451,93 +486,93 @@
     def to_far(values):
         return lax.ppermute(values, "far", ((0, 1), (1, 0)))
 
-    place, wanted = pl.pallas_call(
+    forcing_rows, tendency = surface_rates(
+        atmos_profiles, drag_factor, surface_before, downward_fluxes
+    )
+    exchange_slot, forcing_rows = lax.optimization_barrier((exchange_slot, forcing_rows))
+    place, spot, wanted = pl.pallas_call(
         functools.partial(request_kernel, per_owner),
         in_specs=[vmem] * 2,
-        out_specs=[vmem] * 2,
+        out_specs=[vmem] * 3,
         out_shape=[
+            jax.ShapeDtypeStruct((intersections, cells // LANES), jnp.int32),
             jax.ShapeDtypeStruct((intersections, cells // LANES), jnp.int32),
             jax.ShapeDtypeStruct((near, spots), jnp.int32),
         ],
-        compiler_params=params,
+        compiler_params=stream_params,
         name="requests",
     )(exchange_slot, parent_column)
+    forcing_rows, wanted = lax.optimization_barrier((forcing_rows, wanted))
     asked = to_near(wanted)
-    forcing_rows, tendency = surface_rates(
-        atmos_profiles, drag_factor, surface_before, downward_fluxes
-    )
     other_rows = to_far(forcing_rows)
     served = pl.pallas_call(
         functools.partial(serve_kernel, per_owner),
         in_specs=[smem, smem, vmem, vmem],
         out_specs=vmem,
-        out_shape=jax.ShapeDtypeStruct((near, fields, spots * LANES), jnp.float32),
+        out_shape=jax.ShapeDtypeStruct((near, spots, fields, LANES), jnp.float32),
         scratch_shapes=[pltpu.VMEM((2, fields, columns), jnp.float32)],
         compiler_params=params,
         name="serve_windows",
     )(far, asked, forcing_rows, other_rows)
     arrived = to_near(served)
-    base = top_level(state, ocean_mixing)
+    base, first_level = top_level(state, ocean_mixing)
     atmos_updated = diffuse_atmos(atmos_profiles, atmos_mixing, tendency)
     arrived, atmos_updated, base = lax.optimization_barrier((arrived, atmos_updated, base))
 
     def whole(*shape):
         return pl.BlockSpec(shape, lambda i: (0,) * len(shape))
 
-    lanes_out = (spots + spots // fields) * LANES
-    forcing, send = pl.pallas_call(
+    rows = per_owner // fields
+    sent = (near, per_owner + rows, fields, LANES)
+    forcing, away, home = pl.pallas_call(
         middle_kernel,
         grid=(1,),
         in_specs=[
             smem,
             smem,
-            whole(near, fields, spots * LANES),
+            smem,
+            smem,
+            whole(near * spots, fields, LANES),
             whole(intersections, cells),
             whole(intersections, cells),
             whole(intersections, cells),
             whole(1, cells),
             whole(fields, cells),
-            whole(1, fields, cells),
+            whole(fields, cells),
         ],
-        out_specs=[whole(fields, cells), whole(near, fields, lanes_out)],
+        out_specs=[whole(fields, cells), whole(*sent), whole(*sent)],
         out_shape=[
             jax.ShapeDtypeStruct((fields, cells), jnp.float32),
-            jax.ShapeDtypeStruct((near, fields, lanes_out), jnp.float32),
+            jax.ShapeDtypeStruct(sent, jnp.float32),
+            jax.ShapeDtypeStruct(sent, jnp.float32),
         ],
-        scratch_shapes=[pltpu.VMEM((cells // LANES // GROUP, LANES, LANES), jnp.bfloat16)]
-        + [pltpu.VMEM((near, fields, spots // fields * LANES), jnp.float32)] * intersections,
+        scratch_shapes=[
+            pltpu.VMEM((cells // LANES // GROUP, LANES, LANES), jnp.bfloat16),
+            pltpu.VMEM((near * spots, fields, LANES), jnp.float32),
+        ]
+        + [pltpu.VMEM((2 * near * rows, fields, LANES), jnp.float32)] * intersections,
         compiler_params=params,
         name="forcing_and_windows",
     )(
+        far,
         place,
-        ocean_mixing[0:1, 0:1],
-        arrived,
+        spot,
+        ocean_mixing,
+        arrived.reshape(near * spots, fields, LANES),
         parent_column,
         ocean_weight,
         atmos_weight,
         mask,
         base,
-        state,
+        first_level,
     )
-    back = to_near(send)
+    back_away = to_near(away)
+    back_home = to_near(home)
+    sums_away = collect(asked, far, back_away, per_owner, columns, False)
+    other_sums = to_far(sums_away)
     ocean_updated = diffuse_ocean(state, ocean_mixing, forcing, mask).transpose(1, 0, 2)
-    back, ocean_updated = lax.optimization_barrier((back, ocean_updated))
-
-    chains = 2
-    packed = (fields, columns + columns // fields)
-    keep, away = pl.pallas_call(
-        functools.partial(collect_kernel, per_owner),
-        in_specs=[smem, smem, vmem],
-        out_specs=[vmem] * 2,
-        out_shape=[jax.ShapeDtypeStruct(packed, jnp.float32)] * 2,
-        scratch_shapes=(
-            [pltpu.VMEM((fields, columns), jnp.float32)] * 2
-            + [pltpu.VMEM((1, columns), jnp.float32)] * 2
-        )
-        * chains,
-        compiler_params=params,
-        name="collect_windows",
-    )(far, asked, back)
+    back_home, ocean_updated = lax.optimization_barrier((back_home, ocean_updated))
+    sums_home = collect(asked, far, back_home, per_owner, columns, True)
     surface_state = pl.pallas_call(
         final_kernel,
         in_specs=[vmem] * 4,
@@ -545,7 +580,7 @@
         out_shape=jax.ShapeDtypeStruct((fields, columns), jnp.float32),
         compiler_params=params,
         name="surface_state",
-    )(keep, to_far(away), land_weight.reshape(1, columns), land_surface)
+    )(sums_home, other_sums, land_weight.reshape(1, columns), land_surface)
     return (atmos_updated, ocean_updated, surface_state)
 
 

time: 95 us -> 89.2 us (0.939)
  blocking collectives: 0 us -> 15.1 us
  waiting for transfers between devices: 23 us -> 12 us
  local copies, waits for them, and re-layouts: 7.25 us -> 0.96 us
  Pallas kernels: 45 us -> 43 us
  starting transfers between devices: 18 us -> 16.5 us
    all_to_all x0 -> x1, blocking collectives: none -> 15.1 us  [to_near(): lax.all_to_all(values, ('near', 'sub'), split_axis=0, concat_axis=0, tile...]
    ppermute x2, waiting for transfers between devices: 9.76 us -> 0.01 us  [to_far(): return lax.ppermute(values, 'far', ((0, 1), (1, 0)))]
    unnamed x22 -> x26, local copies, waits for them, and re-layouts: 4.83 us -> 0.96 us
    slice x2 -> x0, local copies, waits for them, and re-layouts: 2.42 us -> none  [the longest x1 1.23 us: per_device(): ocean_mixing[0:1, 0:1]]
    pallas_call x1, Pallas kernels: 7.97 us -> 6.05 us  [diffuse_atmos(): pl.pallas_call(atmos_kernel, grid=(columns // block,), in_specs=[pl.Block...]
    pallas_call x3 -> x4, Pallas kernels: 19.3 us -> 17.6 us  [the longest x1 10 us: per_device(): pl.pallas_call(middle_kernel, grid=(1,), in_specs=[smem, smem, smem, smem...]
    all_to_all x3, starting transfers between devices: 13.6 us -> 12.1 us  [to_near(): lax.all_to_all(values, ('near', 'sub'), split_axis=0, concat_axis=0, tile...]
    all_to_all x3, waiting for transfers between devices: 13.2 us -> 12 us  [to_near(): lax.all_to_all(values, ('near', 'sub'), split_axis=0, concat_axis=0, tile...]
  transfers between devices with their start and end apart: 5 -> 5, of which waited for: 3 -> 3; matrix products, arithmetic and copies ran while one was open for 3% -> 0% of each run, Pallas kernels for 29% -> 29%
where the time goes in v1:
time: 89.2 us; the launch traced here: 88.5 us
  Pallas kernels  43 us (48%)
  starting transfers between devices  16.5 us (18%)
  blocking collectives  15.1 us (17%)
  waiting for transfers between devices  12 us (13%)
  local copies, waits for them, and re-layouts  0.96 us (1%)
    all_to_all x1, blocking collectives, to_near(): lax.all_to_all(values, ('near', 'sub'), split_axis=0, concat_axis=0, tile...  15.1 us
    pallas_call x1, Pallas kernels, diffuse_ocean(): pl.pallas_call(ocean_kernel, grid=(cells // block,), in_specs=[pl.BlockSp...  12.3 us
    all_to_all x3, starting transfers between devices, to_near(): lax.all_to_all(values, ('near', 'sub'), split_axis=0, concat_axis=0, tile...  12.1 us
    all_to_all x3, waiting for transfers between devices, to_near(): lax.all_to_all(values, ('near', 'sub'), split_axis=0, concat_axis=0, tile...  12 us
    pallas_call x1, Pallas kernels, per_device(): pl.pallas_call(middle_kernel, grid=(1,), in_specs=[smem, smem, smem, smem...  10 us
    pallas_call x1, Pallas kernels, diffuse_atmos(): pl.pallas_call(atmos_kernel, grid=(columns // block,), in_specs=[pl.Block...  6.05 us
    pallas_call x1, Pallas kernels, top_level(): pl.pallas_call(top_kernel, grid=(cells // block,), in_specs=[smem] + spec...  4.73 us
    ppermute x2, starting transfers between devices, to_far(): return lax.ppermute(values, 'far', ((0, 1), (1, 0)))  4.44 us
  transfers between devices with their start and end apart: 5, of which 3 were waited for; matrix products, arithmetic and copies ran while one was open for 0% of the time, Pallas kernels for 29%

profile of v1, /device:TPU:0, one launch (start us, length us, event | category | flops | bytes accessed | tf_op | source)
XLA Modules:
  0.0 88.5 jit_solution(7020264439218027543)
XLA Ops:
  0.6 1.9 %surface_rates.1 = (f32[4,8192]{1,0:T(4,128)}, f32[4,8192]{1,0:T(4,128)}) custom-call(bf16[4,72,8192]{2,1,0:T(8,128)(2,1)} %refs_3_.1, f32[1,8192]{1,0:T(1,128)} %bitcast.27, f32[4,8192]{1,0:T(4,128)} %before_ref.1, f32[4,8192]{1,0:T(4,128)} %down_ref.1), custom_call_target="tpu_custom_call" | custom-call | tf_op jit(solution)/shard_map/surface_rates/pallas_call | solution.py:91
  2.5 1.9 %requests.1 = (s32[4,64]{1,0:T(4,128)}, s32[4,64]{1,0:T(4,128)}, s32[16,32]{1,0:T(8,128)}) custom-call(s32[4,8192]{1,0:T(4,128)} %slot_ref, s32[4,8192]{1,0:T(4,128)} %column_ref.3), custom_call_target="tpu_custom_call" | custom-call | tf_op jit(solution)/shard_map/requests/pallas_call | solution.py:493
  4.5 4.0 %collective-permute-start = (f32[4,8192]{1,0:T(4,128)}, f32[4,8192]{1,0:T(4,128)S(1)}, u32[]{:S(2)}, u32[]{:S(2)}) collective-permute-start(f32[4,8192]{1,0:T(4,128)} %get-tuple-element.27.own_ref), channel_id=1, source_target_pairs={{0,16},{16,0},{1,17},{17,1},{2,18},{18,2},{3,19},{19,3},{4,20},{20... | collective-permute-start | bytes 393224 | tf_op jit(solution)/shard_map/ppermute | solution.py:487
  8.5 4.8 %all-to-all-start = ((s32[16,1,32]{2,1,0:T(1,128)}), s32[16,1,32]{2,1,0:T(1,128)S(1)}, u32[]{:S(2)}, u32[]{:S(2)}) async-start(s32[16,1,32]{2,1,0:T(1,128)} %bitcast.28), calls=%async_computation | async-start | bytes 16384 | tf_op jit(solution)/shard_map/all_to_all | solution.py:484
  13.3 5.4 %all-to-all-done = s32[16,1,32]{2,1,0:T(1,128)S(1)} async-done(((s32[16,1,32]{2,1,0:T(1,128)}), s32[16,1,32]{2,1,0:T(1,128)S(1)}, u32[]{:S(2)}, u32[]{:S(2)}) %all-to-all-start) | async-done | bytes 2080 | tf_op jit(solution)/shard_map/all_to_all | solution.py:484
  18.8 0.0 collective-permute-done.other_ref
  18.8 0.9 %copy-done.4 = f32[4,8192]{1,0:T(4,128)S(1)} copy-done((f32[4,8192]{1,0:T(4,128)S(1)}, f32[4,8192]{1,0:T(4,128)}, u32[]{:S(2)}) %copy-start.4) | copy-done | bytes 131096
  19.7 2.6 %serve_windows.1 = f32[16,32,4,128]{3,2,1,0:T(4,128)} custom-call(s32[1]{0:T(128)} %bitcast.far_ref, s32[16,32]{1,0:T(8,128)S(1)} %bitcast.12, f32[4,8192]{1,0:T(4,128)S(1)} %copy-done.4, f32[4,8192]{1,0:T(4,128)S(1)} %collective-permute-done.other_ref), custom_call_target="tpu_custom_call" | custom-call | tf_op jit(solution)/shard_map/serve_windows/pallas_call | solution.py:508
  22.2 3.7 %all-to-all-start.1 = ((f32[16,32,4,128]{3,2,1,0:T(4,128)}), f32[16,32,4,128]{3,2,1,0:T(4,128)S(1)}, u32[]{:S(2)}, u32[]{:S(2)}) async-start(f32[16,32,4,128]{3,2,1,0:T(4,128)} %serve_windows.1), calls=%async_computation.1 | async-start | bytes 2097152 | tf_op jit(solution)/shard_map/all_to_all | solution.py:484
  25.9 4.7 %top_level.1 = (f32[4,8192]{1,0:T(4,128)}, f32[4,8192]{1,0:T(4,128)}) custom-call(f32[60,60]{1,0:T(8,128)} %mix_ref.7, f32[60,4,8192]{2,1,0:T(4,128)} %bitcast.18, f32[60,4,8192]{2,1,0:T(4,128)} %bitcast.19, f32[60,4,8192]{2,1,0:T(4,128)} %bitcast.20, f32[60,4,8192]{2,1,0:T(4,128)} %bitcast.21), custom_call_target="tpu_custom_call" | custom-call | flops 3932160 | bytes 7864320 | tf_op jit(solution)/shard_map/top_level/pallas_call | solution.py:169
  30.6 0.0 copy-start.1
  30.6 0.0 copy-start.5
  30.6 0.0 copy-start.6
  30.6 0.0 copy-start.7
  30.7 0.0 copy-start.8
  30.7 0.0 copy-start.9
  30.7 0.0 copy-start.11
  30.7 0.0 copy-start.12
  30.7 6.1 %diffuse_atmos.1 = bf16[4,72,8192]{2,1,0:T(8,128)(2,1)} custom-call(bf16[72,72]{1,0:T(8,128)(2,1)} %mix_ref.4, f32[4,8192]{1,0:T(4,128)} %get-tuple-element.28.tend_ref, bf16[4,72,8192]{2,1,0:T(8,128)(2,1)} %refs_3_.1, bf16[4,72,8192]{2,1,0:T(8,128)(2,1)} %refs_3_.1, bf16[4,72,8192]{2,1,0:T(8,128)(2,1)} %refs_3_.1, bf16[4,72,8192]{2,1,0:T(8,128)(2,1)} %refs_3_.1), custom_call_target="tpu_custom_call" | custom-call | flops 339738624 | bytes 9437184 | tf_op jit(solution)/shard_map/diffuse_atmos/pallas_call | solution.py:123
  36.8 5.3 %all-to-all-done.1 = f32[16,32,4,128]{3,2,1,0:T(4,128)S(1)} async-done(((f32[16,32,4,128]{3,2,1,0:T(4,128)}), f32[16,32,4,128]{3,2,1,0:T(4,128)S(1)}, u32[]{:S(2)}, u32[]{:S(2)}) %all-to-all-start.1) | async-done | bytes 1048608 | tf_op jit(solution)/shard_map/all_to_all | solution.py:484
  42.0 0.0 copy-done.6
  42.0 0.0 copy-done.7
  42.1 10.0 %forcing_and_windows.1 = (f32[4,8192]{1,0:T(4,128)S(1)}, f32[16,20,4,128]{3,2,1,0:T(4,128)S(1)}, f32[16,20,4,128]{3,2,1,0:T(4,128)}) custom-call(s32[1]{0:T(128)} %bitcast.far_ref, s32[4,64]{1,0:T(4,128)S(1)} %copy-done.11, s32[4,64]{1,0:T(4,128)S(1)} %copy-done.12, f32[60,60]{1,0:T(8,128)S(1)} %copy-done.1, f32[512,4,128]{2,1,0:T(4,128)S(1)} %bitcast.11, ...), custom_call_target="tpu_custom_call" | custom-call | tf_op jit(solution)/shard_map/forcing_and_windows/pallas_call | solution.py:527
  52.1 15.1 %all_to_all.26.back_ref = f32[16,20,4,128]{3,2,1,0:T(4,128)S(1)} all-to-all(f32[16,20,4,128]{3,2,1,0:T(4,128)S(1)} %get-tuple-element.40), channel_id=1, replica_groups=mesh['far'=2,'near'=2,'sub'=8] {'near','sub'}, dimensions={0} | all-to-all | bytes 1310720 | tf_op jit(solution)/shard_map/all_to_all | solution.py:484
  67.2 3.6 %all-to-all-start.2 = ((f32[16,20,4,128]{3,2,1,0:T(4,128)}), f32[16,20,4,128]{3,2,1,0:T(4,128)S(1)}, u32[]{:S(2)}, u32[]{:S(2)}) async-start(f32[16,20,4,128]{3,2,1,0:T(4,128)} %get-tuple-element.36), calls=%async_computation.2 | async-start | bytes 1310720 | tf_op jit(solution)/shard_map/all_to_all | solution.py:484
  70.8 1.4 %collect_away.1 = f32[4,10240]{1,0:T(4,128)S(1)} custom-call(s32[1]{0:T(128)} %bitcast.far_ref, s32[16,32]{1,0:T(8,128)S(1)} %bitcast.13, f32[16,20,4,128]{3,2,1,0:T(4,128)S(1)} %all_to_all.26.back_ref), custom_call_target="tpu_custom_call" | custom-call | tf_op jit(solution)/shard_map/collect_away/pallas_call | solution.py:432
  72.3 0.4 collective-permute-start.1
  72.7 12.3 %diffuse_ocean.1 = f32[60,4,8192]{2,1,0:T(4,128)} custom-call(f32[60,60]{1,0:T(8,128)} %mix_ref.7, f32[4,8192]{1,0:T(4,128)} %copy-done.2, s32[1,8192]{1,0:T(1,128)} %bitcast.15, f32[60,4,8192]{2,1,0:T(4,128)} %bitcast.22, f32[60,4,8192]{2,1,0:T(4,128)} %bitcast.23, f32[60,4,8192]{2,1,0:T(4,128)} %bitcast.24, f32[60,4,8192]{2,1,0:T(4,128)} %bitcast.25), custom_call_target="tpu_custom_call" | custom-call | flops 2831155200 | bytes 15728640 | tf_op jit(solution)/shard_map/diffuse_ocean/pallas_call | solution.py:377
  84.9 1.3 %all-to-all-done.2.back_ref = f32[16,20,4,128]{3,2,1,0:T(4,128)S(1)} async-done(((f32[16,20,4,128]{3,2,1,0:T(4,128)}), f32[16,20,4,128]{3,2,1,0:T(4,128)S(1)}, u32[]{:S(2)}, u32[]{:S(2)}) %all-to-all-start.2) | async-done | bytes 655392 | tf_op jit(solution)/shard_map/all_to_all | solution.py:484
  86.3 1.4 %collect_home.1.keep_ref = f32[4,10240]{1,0:T(4,128)S(1)} custom-call(s32[1]{0:T(128)} %bitcast.far_ref, s32[16,32]{1,0:T(8,128)S(1)} %bitcast.14, f32[16,20,4,128]{3,2,1,0:T(4,128)S(1)} %all-to-all-done.2.back_ref), custom_call_target="tpu_custom_call" | custom-call | tf_op jit(solution)/shard_map/collect_home/pallas_call | solution.py:432
  87.7 0.0 collective-permute-done.1.other_ref
  87.7 0.7 surface_state.1
  (15 shorter events, 0.0 us)
Async XLA Ops:
  4.5 14.3 %collective-permute-start = (f32[4,8192]{1,0:T(4,128)}, f32[4,8192]{1,0:T(4,128)S(1)}, u32[]{:S(2)}, u32[]{:S(2)}) collective-permute-start(f32[4,8192]{1,0:T(4,128)} %get-tuple-element.27.own_ref), channel_id=1, source_target_pairs={{0,16},{16,0},{1,17},{17,1},{2,18},{18,2},{3,19},{19,3},{4,20},{20... | collective-permute-start | bytes 393224 | tf_op jit(solution)/shard_map/ppermute | solution.py:487
  8.5 10.3 %all-to-all-start = ((s32[16,1,32]{2,1,0:T(1,128)}), s32[16,1,32]{2,1,0:T(1,128)S(1)}, u32[]{:S(2)}, u32[]{:S(2)}) async-start(s32[16,1,32]{2,1,0:T(1,128)} %bitcast.28), calls=%async_computation | async-start | bytes 16384 | tf_op jit(solution)/shard_map/all_to_all | solution.py:484
  18.8 0.9 %copy-start.4 = (f32[4,8192]{1,0:T(4,128)S(1)}, f32[4,8192]{1,0:T(4,128)}, u32[]{:S(2)}) copy-start(f32[4,8192]{1,0:T(4,128)} %get-tuple-element.27.own_ref) | copy-start | bytes 393220
  22.2 19.8 %all-to-all-start.1 = ((f32[16,32,4,128]{3,2,1,0:T(4,128)}), f32[16,32,4,128]{3,2,1,0:T(4,128)S(1)}, u32[]{:S(2)}, u32[]{:S(2)}) async-start(f32[16,32,4,128]{3,2,1,0:T(4,128)} %serve_windows.1), calls=%async_computation.1 | async-start | bytes 2097152 | tf_op jit(solution)/shard_map/all_to_all | solution.py:484
  30.6 11.4 %copy-start = (s32[4,8192]{1,0:T(4,128)S(1)}, s32[4,8192]{1,0:T(4,128)}, u32[]{:S(2)}) copy-start(s32[4,8192]{1,0:T(4,128)} %column_ref.3) | copy-start | bytes 393220
  30.6 11.4 %copy-start.1 = (f32[60,60]{1,0:T(8,128)S(1)}, f32[60,60]{1,0:T(8,128)}, u32[]{:S(2)}) copy-start(f32[60,60]{1,0:T(8,128)} %mix_ref.7) | copy-start | bytes 43204
  30.6 11.4 %copy-start.5 = (s32[8192]{0:T(1024)S(1)}, s32[8192]{0:T(1024)}, u32[]{:S(2)}) copy-start(s32[8192]{0:T(1024)} %param.23) | copy-start | bytes 98308
  30.6 11.4 %copy-start.6 = (f32[4,8192]{1,0:T(4,128)S(1)}, f32[4,8192]{1,0:T(4,128)}, u32[]{:S(2)}) copy-start(f32[4,8192]{1,0:T(4,128)} %ocean_weight_ref.1) | copy-start | bytes 393220
  30.6 11.4 %copy-start.7 = (f32[4,8192]{1,0:T(4,128)S(1)}, f32[4,8192]{1,0:T(4,128)}, u32[]{:S(2)}) copy-start(f32[4,8192]{1,0:T(4,128)} %atmos_weight_ref.1) | copy-start | bytes 393220
  30.7 11.4 %copy-start.8 = (f32[4,8192]{1,0:T(4,128)S(1)}, f32[4,8192]{1,0:T(4,128)}, u32[]{:S(2)}) copy-start(f32[4,8192]{1,0:T(4,128)} %get-tuple-element.34.base_ref) | copy-start | bytes 393220
  30.7 11.4 %copy-start.9 = (f32[4,8192]{1,0:T(4,128)S(1)}, f32[4,8192]{1,0:T(4,128)}, u32[]{:S(2)}) copy-start(f32[4,8192]{1,0:T(4,128)} %get-tuple-element.35.state_ref) | copy-start | bytes 393220
  30.7 11.4 %copy-start.11 = (s32[4,64]{1,0:T(4,128)S(1)}, s32[4,64]{1,0:T(4,128)}, u32[]{:S(2)}) copy-start(s32[4,64]{1,0:T(4,128)} %get-tuple-element.31.place_ref) | copy-start | bytes 3076
  30.7 11.4 %copy-start.12 = (s32[4,64]{1,0:T(4,128)S(1)}, s32[4,64]{1,0:T(4,128)}, u32[]{:S(2)}) copy-start(s32[4,64]{1,0:T(4,128)} %get-tuple-element.32.spot_ref) | copy-start | bytes 3076
  52.1 15.1 %copy-start.2 = (f32[4,8192]{1,0:T(4,128)}, f32[4,8192]{1,0:T(4,128)S(1)}, u32[]{:S(2)}) copy-start(f32[4,8192]{1,0:T(4,128)S(1)} %get-tuple-element.37.forcing_ref) | copy-start | bytes 393220
  67.2 19.0 %all-to-all-start.2 = ((f32[16,20,4,128]{3,2,1,0:T(4,128)}), f32[16,20,4,128]{3,2,1,0:T(4,128)S(1)}, u32[]{:S(2)}, u32[]{:S(2)}) async-start(f32[16,20,4,128]{3,2,1,0:T(4,128)} %get-tuple-element.36), calls=%async_computation.2 | async-start | bytes 1310720 | tf_op jit(solution)/shard_map/all_to_all | solution.py:484
  72.3 15.4 %collective-permute-start.1 = (f32[4,10240]{1,0:T(4,128)S(1)}, f32[4,10240]{1,0:T(4,128)S(1)}, u32[]{:S(2)}, u32[]{:S(2)}) collective-permute-start(f32[4,10240]{1,0:T(4,128)S(1)} %collect_away.1), channel_id=1, source_target_pairs={{0,16},{16,0},{1,17},{17,1},{2,18},{18,2},{3,19},{19,3},{4,20},{20... | collective-permute-start | bytes 491528 | tf_op jit(solution)/shard_map/ppermute | solution.py:487
  72.7 15.0 %copy-start.3 = (f32[4,8192]{1,0:T(4,128)S(1)}, f32[4,8192]{1,0:T(4,128)}, u32[]{:S(2)}) copy-start(f32[4,8192]{1,0:T(4,128)} %land_ref.1) | copy-start | bytes 393220
  72.7 15.0 %copy-start.10 = (f32[8192]{0:T(1024)S(1)}, f32[8192]{0:T(1024)}, u32[]{:S(2)}) copy-start(f32[8192]{0:T(1024)} %param.19) | copy-start | bytes 98308

commit v2 on v1

--- a/solution.py
+++ b/solution.py
@@ -10,7 +10,8 @@
 couple_rate = 0.5
 LANES = 128
 params = pltpu.CompilerParams(vmem_limit_bytes=24 * 1024 * 1024)
-stream_params = pltpu.CompilerParams(vmem_limit_bytes=56 * 1024 * 1024)
+stream_params = pltpu.CompilerParams(vmem_limit_bytes=52 * 1024 * 1024)
+first_params = pltpu.CompilerParams(vmem_limit_bytes=56 * 1024 * 1024)
 vmem = pl.BlockSpec(memory_space=pltpu.VMEM)
 smem = pl.BlockSpec(memory_space=pltpu.SMEM)
 AXES = ("far", "near", "sub")
@@ -20,7 +21,7 @@
     return pl.ds(pl.multiple_of(index * LANES, LANES), LANES)
 
 
-def request_kernel(per_owner, slot_ref, column_ref, place_ref, spot_ref, wanted_ref):
+def make_requests(per_owner, slot_ref, column_ref, place_ref, spot_ref, wanted_ref):
     intersections, cells = slot_ref.shape
     near, spots = wanted_ref.shape
     windows = cells // LANES
@@ -58,7 +59,25 @@
     wanted_ref[...] = wanted.astype(jnp.int32)
 
 
-def flux_kernel(last, x_ref, drag_ref, before_ref, down_ref, forcing_ref, tend_ref):
+def start_kernel(
+    last,
+    per_owner,
+    slot_ref,
+    column_ref,
+    x_ref,
+    drag_ref,
+    before_ref,
+    down_ref,
+    place_ref,
+    spot_ref,
+    wanted_ref,
+    forcing_ref,
+    tend_ref,
+):
+    @pl.when(pl.program_id(0) == 0)
+    def _():
+        make_requests(per_owner, slot_ref, column_ref, place_ref, spot_ref, wanted_ref)
+
     def row(ref, index):
         return ref[index : index + 1, :]
 
@@ -82,26 +101,41 @@
     tend_ref[3:4, :] = -north_stress
 
 
-def surface_rates(profiles, drag_factor, surface_before, downward):
+def start(near, per_owner, slots, parents, profiles, drag_factor, surface_before, downward):
     fields, levels, columns = profiles.shape
+    intersections, cells = slots.shape
     block = min(4096, columns)
     tall = 16
     at = (levels - 1) // tall
     rows = pl.BlockSpec((fields, block), lambda i: (0, i))
+    tiles = (intersections, cells // LANES)
+    asked = (near, 2 * per_owner)
+
+    def whole(shape):
+        return pl.BlockSpec(shape, lambda i: (0, 0))
+
     return pl.pallas_call(
-        functools.partial(flux_kernel, levels - 1 - at * tall),
+        functools.partial(start_kernel, levels - 1 - at * tall, per_owner),
         grid=(columns // block,),
         in_specs=[
+            whole(slots.shape),
+            whole(slots.shape),
             pl.BlockSpec((fields, tall, block), lambda i: (0, at, i)),
             pl.BlockSpec((1, block), lambda i: (0, i)),
             rows,
             rows,
         ],
-        out_specs=[rows, rows],
-        out_shape=[jax.ShapeDtypeStruct((fields, columns), jnp.float32)] * 2,
-        compiler_params=stream_params,
-        name="surface_rates",
-    )(profiles, drag_factor.reshape(1, columns), surface_before, downward)
+        out_specs=[whole(tiles), whole(tiles), whole(asked), rows, rows],
+        out_shape=[
+            jax.ShapeDtypeStruct(tiles, jnp.int32),
+            jax.ShapeDtypeStruct(tiles, jnp.int32),
+            jax.ShapeDtypeStruct(asked, jnp.int32),
+            jax.ShapeDtypeStruct((fields, columns), jnp.float32),
+            jax.ShapeDtypeStruct((fields, columns), jnp.float32),
+        ],
+        compiler_params=first_params,
+        name="requests_and_rates",
+    )(slots, parents, profiles, drag_factor.reshape(1, columns), surface_before, downward)
 
 
 def atmos_kernel(mix_ref, tend_ref, *refs):
@@ -486,23 +520,16 @@
     def to_far(values):
         return lax.ppermute(values, "far", ((0, 1), (1, 0)))
 
-    forcing_rows, tendency = surface_rates(
-        atmos_profiles, drag_factor, surface_before, downward_fluxes
-    )
-    exchange_slot, forcing_rows = lax.optimization_barrier((exchange_slot, forcing_rows))
-    place, spot, wanted = pl.pallas_call(
-        functools.partial(request_kernel, per_owner),
-        in_specs=[vmem] * 2,
-        out_specs=[vmem] * 3,
-        out_shape=[
-            jax.ShapeDtypeStruct((intersections, cells // LANES), jnp.int32),
-            jax.ShapeDtypeStruct((intersections, cells // LANES), jnp.int32),
-            jax.ShapeDtypeStruct((near, spots), jnp.int32),
-        ],
-        compiler_params=stream_params,
-        name="requests",
-    )(exchange_slot, parent_column)
-    forcing_rows, wanted = lax.optimization_barrier((forcing_rows, wanted))
+    place, spot, wanted, forcing_rows, tendency = start(
+        near,
+        per_owner,
+        exchange_slot,
+        parent_column,
+        atmos_profiles,
+        drag_factor,
+        surface_before,
+        downward_fluxes,
+    )
     asked = to_near(wanted)
     other_rows = to_far(forcing_rows)
     served = pl.pallas_call(
@@ -516,31 +543,14 @@
     )(far, asked, forcing_rows, other_rows)
     arrived = to_near(served)
     base, first_level = top_level(state, ocean_mixing)
-    atmos_updated = diffuse_atmos(atmos_profiles, atmos_mixing, tendency)
-    arrived, atmos_updated, base = lax.optimization_barrier((arrived, atmos_updated, base))
-
-    def whole(*shape):
-        return pl.BlockSpec(shape, lambda i: (0,) * len(shape))
+    arrived, base = lax.optimization_barrier((arrived, base))
 
     rows = per_owner // fields
     sent = (near, per_owner + rows, fields, LANES)
     forcing, away, home = pl.pallas_call(
         middle_kernel,
-        grid=(1,),
-        in_specs=[
-            smem,
-            smem,
-            smem,
-            smem,
-            whole(near * spots, fields, LANES),
-            whole(intersections, cells),
-            whole(intersections, cells),
-            whole(intersections, cells),
-            whole(1, cells),
-            whole(fields, cells),
-            whole(fields, cells),
-        ],
-        out_specs=[whole(fields, cells), whole(*sent), whole(*sent)],
+        in_specs=[smem] * 4 + [vmem] * 7,
+        out_specs=[vmem] * 3,
         out_shape=[
             jax.ShapeDtypeStruct((fields, cells), jnp.float32),
             jax.ShapeDtypeStruct(sent, jnp.float32),
@@ -566,7 +576,11 @@
         base,
         first_level,
     )
-    back_away = to_near(away)
+    tendency, forcing = lax.optimization_barrier((tendency, forcing))
+    atmos_updated = diffuse_atmos(atmos_profiles, atmos_mixing, tendency)
+    back_away, atmos_updated, home = lax.optimization_barrier(
+        (to_near(away), atmos_updated, home)
+    )
     back_home = to_near(home)
     sums_away = collect(asked, far, back_away, per_owner, columns, False)
     other_sums = to_far(sums_away)

time: 89.2 us -> 88.5 us (level)
  blocking collectives: 15.1 us -> 0 us
  waiting for transfers between devices: 12 us -> 24.7 us
  starting transfers between devices: 16.5 us -> 20.2 us
  Pallas kernels: 43 us -> 41.1 us
    all_to_all x1 -> x0, blocking collectives: 15.1 us -> none  [to_near(): lax.all_to_all(values, ('near', 'sub'), split_axis=0, concat_axis=0, tile...]
    all_to_all x3 -> x4, waiting for transfers between devices: 12 us -> 24.7 us  [to_near(): lax.all_to_all(values, ('near', 'sub'), split_axis=0, concat_axis=0, tile...]
    all_to_all x3 -> x4, starting transfers between devices: 12.1 us -> 15.7 us  [to_near(): lax.all_to_all(values, ('near', 'sub'), split_axis=0, concat_axis=0, tile...]
    pallas_call x3 -> x2, Pallas kernels: 13.9 us -> 12.7 us  [the longest x1 10.3 us: per_device(): pl.pallas_call(middle_kernel, in_specs=[smem] * 4 + [vmem] * 7, out_specs...]
  transfers between devices with their start and end apart: 5 -> 6, of which waited for: 3 -> 4; matrix products, arithmetic and copies ran while one was open for 0% -> 0% of each run, Pallas kernels for 29% -> 29%
where the time goes in v2:
time: 88.5 us; the launch traced here: 87.7 us
  Pallas kernels  41.1 us (46%)
  waiting for transfers between devices  24.7 us (28%)
  starting transfers between devices  20.2 us (23%)
  local copies, waits for them, and re-layouts  0.97 us (1%)
    all_to_all x4, waiting for transfers between devices, to_near(): lax.all_to_all(values, ('near', 'sub'), split_axis=0, concat_axis=0, tile...  24.7 us
    all_to_all x4, starting transfers between devices, to_near(): lax.all_to_all(values, ('near', 'sub'), split_axis=0, concat_axis=0, tile...  15.7 us
    pallas_call x1, Pallas kernels, diffuse_ocean(): pl.pallas_call(ocean_kernel, grid=(cells // block,), in_specs=[pl.BlockSp...  12.1 us
    pallas_call x1, Pallas kernels, per_device(): pl.pallas_call(middle_kernel, in_specs=[smem] * 4 + [vmem] * 7, out_specs...  10.3 us
    pallas_call x1, Pallas kernels, diffuse_atmos(): pl.pallas_call(atmos_kernel, grid=(columns // block,), in_specs=[pl.Block...  5.85 us
    ppermute x2, starting transfers between devices, to_far(): return lax.ppermute(values, 'far', ((0, 1), (1, 0)))  4.49 us
    pallas_call x1, Pallas kernels, top_level(): pl.pallas_call(top_kernel, grid=(cells // block,), in_specs=[smem] + spec...  4.26 us
    pallas_call x2, Pallas kernels, collect(): pl.pallas_call(functools.partial(collect_kernel, per_owner, home), in_spe...  2.84 us
  transfers between devices with their start and end apart: 6, of which 4 were waited for; matrix products, arithmetic and copies ran while one was open for 0% of the time, Pallas kernels for 29%

profile of v2, /device:TPU:0, one launch (start us, length us, event | category | flops | bytes accessed | tf_op | source)
XLA Modules:
  0.0 87.7 jit_solution(15057041697902963178)
XLA Ops:
  0.6 0.0 copy-start.1
  0.6 2.5 %requests_and_rates.1 = (s32[4,64]{1,0:T(4,128)}, s32[4,64]{1,0:T(4,128)}, s32[16,32]{1,0:T(8,128)}, f32[4,8192]{1,0:T(4,128)}, f32[4,8192]{1,0:T(4,128)}) custom-call(s32[4,8192]{1,0:T(4,128)} %slot_ref.1, s32[4,8192]{1,0:T(4,128)} %column_ref.3, bf16[4,72,8192]{2,1,0:T(8,128)(2,1)} %refs_3_.1, f32[1,8192]{1,0:T(1,128)} %bitcast.27, f32[4,8192]{1,0:T(4,128)} %before_ref.1, ...), custom_call_target="tpu_custom_call" | custom-call | tf_op jit(solution)/shard_map/requests_and_rates/pallas_call | solution.py:117
  3.1 4.1 %collective-permute-start = (f32[4,8192]{1,0:T(4,128)}, f32[4,8192]{1,0:T(4,128)S(1)}, u32[]{:S(2)}, u32[]{:S(2)}) collective-permute-start(f32[4,8192]{1,0:T(4,128)} %get-tuple-element.25.own_ref), channel_id=1, source_target_pairs={{0,16},{16,0},{1,17},{17,1},{2,18},{18,2},{3,19},{19,3},{4,20},{20... | collective-permute-start | bytes 393224 | tf_op jit(solution)/shard_map/ppermute | solution.py:521
  7.2 4.8 %all-to-all-start = ((s32[16,1,32]{2,1,0:T(1,128)}), s32[16,1,32]{2,1,0:T(1,128)S(1)}, u32[]{:S(2)}, u32[]{:S(2)}) async-start(s32[16,1,32]{2,1,0:T(1,128)} %bitcast.28), calls=%async_computation | async-start | bytes 16384 | tf_op jit(solution)/shard_map/all_to_all | solution.py:518
  12.0 5.4 %all-to-all-done = s32[16,1,32]{2,1,0:T(1,128)S(1)} async-done(((s32[16,1,32]{2,1,0:T(1,128)}), s32[16,1,32]{2,1,0:T(1,128)S(1)}, u32[]{:S(2)}, u32[]{:S(2)}) %all-to-all-start) | async-done | bytes 2080 | tf_op jit(solution)/shard_map/all_to_all | solution.py:518
  17.4 0.0 collective-permute-done.other_ref
  17.4 0.9 %copy-done.4 = f32[4,8192]{1,0:T(4,128)S(1)} copy-done((f32[4,8192]{1,0:T(4,128)S(1)}, f32[4,8192]{1,0:T(4,128)}, u32[]{:S(2)}) %copy-start.4) | copy-done | bytes 131096
  18.4 2.6 %serve_windows.1 = f32[16,32,4,128]{3,2,1,0:T(4,128)} custom-call(s32[1]{0:T(128)} %bitcast.far_ref, s32[16,32]{1,0:T(8,128)S(1)} %bitcast.12, f32[4,8192]{1,0:T(4,128)S(1)} %copy-done.4, f32[4,8192]{1,0:T(4,128)S(1)} %collective-permute-done.other_ref), custom_call_target="tpu_custom_call" | custom-call | tf_op jit(solution)/shard_map/serve_windows/pallas_call | solution.py:535
  20.9 3.7 %all-to-all-start.1 = ((f32[16,32,4,128]{3,2,1,0:T(4,128)}), f32[16,32,4,128]{3,2,1,0:T(4,128)S(1)}, u32[]{:S(2)}, u32[]{:S(2)}) async-start(f32[16,32,4,128]{3,2,1,0:T(4,128)} %serve_windows.1), calls=%async_computation.1 | async-start | bytes 2097152 | tf_op jit(solution)/shard_map/all_to_all | solution.py:518
  24.6 0.0 copy-start
  24.6 0.0 copy-start.5
  24.6 0.0 copy-start.6
  24.6 0.0 copy-start.7
  24.6 0.0 copy-start.10
  24.7 0.0 copy-start.9
  24.7 4.3 %top_level.1 = (f32[4,8192]{1,0:T(4,128)S(1)}, f32[4,8192]{1,0:T(4,128)S(1)}) custom-call(f32[60,60]{1,0:T(8,128)S(1)} %copy-done.1, f32[60,4,8192]{2,1,0:T(4,128)} %bitcast.18, f32[60,4,8192]{2,1,0:T(4,128)} %bitcast.19, f32[60,4,8192]{2,1,0:T(4,128)} %bitcast.20, f32[60,4,8192]{2,1,0:T(4,128)} %bitcast.21), custom_call_target="tpu_custom_call" | custom-call | flops 3932160 | bytes 7864320 | tf_op jit(solution)/shard_map/top_level/pallas_call | solution.py:203
  28.9 11.8 %all-to-all-done.1 = f32[16,32,4,128]{3,2,1,0:T(4,128)S(1)} async-done(((f32[16,32,4,128]{3,2,1,0:T(4,128)}), f32[16,32,4,128]{3,2,1,0:T(4,128)S(1)}, u32[]{:S(2)}, u32[]{:S(2)}) %all-to-all-start.1) | async-done | bytes 1048608 | tf_op jit(solution)/shard_map/all_to_all | solution.py:518
  40.7 0.0 copy-done
  40.7 10.3 %forcing_and_windows.1 = (f32[4,8192]{1,0:T(4,128)S(1)}, f32[16,20,4,128]{3,2,1,0:T(4,128)}, f32[16,20,4,128]{3,2,1,0:T(4,128)}) custom-call(s32[1]{0:T(128)} %bitcast.far_ref, s32[4,64]{1,0:T(4,128)S(1)} %copy-done.10, s32[4,64]{1,0:T(4,128)S(1)} %copy-done.11, f32[60,60]{1,0:T(8,128)S(1)} %copy-done.1, f32[512,4,128]{2,1,0:T(4,128)S(1)} %bitcast.11, ...), custom_call_target="tpu_custom_call" | custom-call | tf_op jit(solution)/shard_map/forcing_and_windows/pallas_call | solution.py:550
  51.0 3.6 %all-to-all-start.2 = ((f32[16,20,4,128]{3,2,1,0:T(4,128)}), f32[16,20,4,128]{3,2,1,0:T(4,128)S(1)}, u32[]{:S(2)}, u32[]{:S(2)}) async-start(f32[16,20,4,128]{3,2,1,0:T(4,128)} %get-tuple-element.30), calls=%async_computation.2 | async-start | bytes 1310720 | tf_op jit(solution)/shard_map/all_to_all | solution.py:518
  54.6 5.8 %diffuse_atmos.1 = bf16[4,72,8192]{2,1,0:T(8,128)(2,1)} custom-call(bf16[72,72]{1,0:T(8,128)(2,1)S(1)} %copy-done.9, f32[4,8192]{1,0:T(4,128)S(1)} %copy-done.2, bf16[4,72,8192]{2,1,0:T(8,128)(2,1)} %refs_3_.1, bf16[4,72,8192]{2,1,0:T(8,128)(2,1)} %refs_3_.1, bf16[4,72,8192]{2,1,0:T(8,128)(2,1)} %refs_3_.1, bf16[4,72,8192]{2,1,0:T(8,128)(2,1)} %refs_3_.1), custom_call_target="tpu_custom_call" | custom-call | flops 339738624 | bytes 9437184 | tf_op jit(solution)/shard_map/diffuse_atmos/pallas_call | solution.py:157
  60.5 6.0 %all-to-all-done.2.back_ref = f32[16,20,4,128]{3,2,1,0:T(4,128)S(1)} async-done(((f32[16,20,4,128]{3,2,1,0:T(4,128)}), f32[16,20,4,128]{3,2,1,0:T(4,128)S(1)}, u32[]{:S(2)}, u32[]{:S(2)}) %all-to-all-start.2) | async-done | bytes 655392 | tf_op jit(solution)/shard_map/all_to_all | solution.py:518
  66.5 3.6 %all-to-all-start.3 = ((f32[16,20,4,128]{3,2,1,0:T(4,128)}), f32[16,20,4,128]{3,2,1,0:T(4,128)S(1)}, u32[]{:S(2)}, u32[]{:S(2)}) async-start(f32[16,20,4,128]{3,2,1,0:T(4,128)} %get-tuple-element.36), calls=%async_computation.3 | async-start | bytes 1310720 | tf_op jit(solution)/shard_map/all_to_all | solution.py:518
  70.1 1.4 %collect_away.1 = f32[4,10240]{1,0:T(4,128)S(1)} custom-call(s32[1]{0:T(128)} %bitcast.far_ref, s32[16,32]{1,0:T(8,128)S(1)} %bitcast.13, f32[16,20,4,128]{3,2,1,0:T(4,128)S(1)} %all-to-all-done.2.back_ref), custom_call_target="tpu_custom_call" | custom-call | tf_op jit(solution)/shard_map/collect_away/pallas_call | solution.py:466
  71.5 0.0 copy-start.3
  71.6 0.0 copy-start.8
  71.6 0.4 collective-permute-start.1
  72.0 12.1 %diffuse_ocean.1 = f32[60,4,8192]{2,1,0:T(4,128)} custom-call(f32[60,60]{1,0:T(8,128)S(1)} %copy-done.1, f32[4,8192]{1,0:T(4,128)S(1)} %get-tuple-element.37.forcing_ref, s32[1,8192]{1,0:T(1,128)S(1)} %bitcast.16, f32[60,4,8192]{2,1,0:T(4,128)} %bitcast.22, f32[60,4,8192]{2,1,0:T(4,128)} %bitcast.23, f32[60,4,8192]{2,1,0:T(4,128)} %bitcast.24, ...), custom_call_target="tpu_custom_call" | custom-call | flops 2831155200 | bytes 15728640 | tf_op jit(solution)/shard_map/diffuse_ocean/pallas_call | solution.py:411
  84.1 1.5 %all-to-all-done.3.back_ref = f32[16,20,4,128]{3,2,1,0:T(4,128)S(1)} async-done(((f32[16,20,4,128]{3,2,1,0:T(4,128)}), f32[16,20,4,128]{3,2,1,0:T(4,128)S(1)}, u32[]{:S(2)}, u32[]{:S(2)}) %all-to-all-start.3) | async-done | bytes 655392 | tf_op jit(solution)/shard_map/all_to_all | solution.py:518
  85.5 1.4 %collect_home.1.keep_ref = f32[4,10240]{1,0:T(4,128)S(1)} custom-call(s32[1]{0:T(128)} %bitcast.far_ref, s32[16,32]{1,0:T(8,128)S(1)} %bitcast.14, f32[16,20,4,128]{3,2,1,0:T(4,128)S(1)} %all-to-all-done.3.back_ref), custom_call_target="tpu_custom_call" | custom-call | tf_op jit(solution)/shard_map/collect_home/pallas_call | solution.py:466
  87.0 0.0 collective-permute-done.1.other_ref
  87.0 0.7 surface_state.1
  (13 shorter events, 0.0 us)
Async XLA Ops:
  0.6 23.9 %copy-start.1 = (f32[60,60]{1,0:T(8,128)S(1)}, f32[60,60]{1,0:T(8,128)}, u32[]{:S(2)}) copy-start(f32[60,60]{1,0:T(8,128)} %mix_ref.7) | copy-start | bytes 43204
  3.1 14.3 %collective-permute-start = (f32[4,8192]{1,0:T(4,128)}, f32[4,8192]{1,0:T(4,128)S(1)}, u32[]{:S(2)}, u32[]{:S(2)}) collective-permute-start(f32[4,8192]{1,0:T(4,128)} %get-tuple-element.25.own_ref), channel_id=1, source_target_pairs={{0,16},{16,0},{1,17},{17,1},{2,18},{18,2},{3,19},{19,3},{4,20},{20... | collective-permute-start | bytes 393224 | tf_op jit(solution)/shard_map/ppermute | solution.py:521
  7.2 10.3 %all-to-all-start = ((s32[16,1,32]{2,1,0:T(1,128)}), s32[16,1,32]{2,1,0:T(1,128)S(1)}, u32[]{:S(2)}, u32[]{:S(2)}) async-start(s32[16,1,32]{2,1,0:T(1,128)} %bitcast.28), calls=%async_computation | async-start | bytes 16384 | tf_op jit(solution)/shard_map/all_to_all | solution.py:518
  17.4 0.9 %copy-start.4 = (f32[4,8192]{1,0:T(4,128)S(1)}, f32[4,8192]{1,0:T(4,128)}, u32[]{:S(2)}) copy-start(f32[4,8192]{1,0:T(4,128)} %get-tuple-element.25.own_ref) | copy-start | bytes 393220
  20.9 19.8 %all-to-all-start.1 = ((f32[16,32,4,128]{3,2,1,0:T(4,128)}), f32[16,32,4,128]{3,2,1,0:T(4,128)S(1)}, u32[]{:S(2)}, u32[]{:S(2)}) async-start(f32[16,32,4,128]{3,2,1,0:T(4,128)} %serve_windows.1), calls=%async_computation.1 | async-start | bytes 2097152 | tf_op jit(solution)/shard_map/all_to_all | solution.py:518
  24.6 16.1 %copy-start = (s32[4,8192]{1,0:T(4,128)S(1)}, s32[4,8192]{1,0:T(4,128)}, u32[]{:S(2)}) copy-start(s32[4,8192]{1,0:T(4,128)} %column_ref.3) | copy-start | bytes 393220
  24.6 16.1 %copy-start.5 = (s32[8192]{0:T(1024)S(1)}, s32[8192]{0:T(1024)}, u32[]{:S(2)}) copy-start(s32[8192]{0:T(1024)} %param.23) | copy-start | bytes 98308
  24.6 16.1 %copy-start.6 = (f32[4,8192]{1,0:T(4,128)S(1)}, f32[4,8192]{1,0:T(4,128)}, u32[]{:S(2)}) copy-start(f32[4,8192]{1,0:T(4,128)} %ocean_weight_ref.1) | copy-start | bytes 393220
  24.6 16.1 %copy-start.7 = (f32[4,8192]{1,0:T(4,128)S(1)}, f32[4,8192]{1,0:T(4,128)}, u32[]{:S(2)}) copy-start(f32[4,8192]{1,0:T(4,128)} %atmos_weight_ref.1) | copy-start | bytes 393220
  24.6 16.1 %copy-start.10 = (s32[4,64]{1,0:T(4,128)S(1)}, s32[4,64]{1,0:T(4,128)}, u32[]{:S(2)}) copy-start(s32[4,64]{1,0:T(4,128)} %get-tuple-element.22.place_ref) | copy-start | bytes 3076
  24.6 16.1 %copy-start.11 = (s32[4,64]{1,0:T(4,128)S(1)}, s32[4,64]{1,0:T(4,128)}, u32[]{:S(2)}) copy-start(s32[4,64]{1,0:T(4,128)} %get-tuple-element.23.spot_ref) | copy-start | bytes 3076
  24.6 30.0 %copy-start.2 = (f32[4,8192]{1,0:T(4,128)S(1)}, f32[4,8192]{1,0:T(4,128)}, u32[]{:S(2)}) copy-start(f32[4,8192]{1,0:T(4,128)} %get-tuple-element.33.tend_ref) | copy-start | bytes 393220
  24.7 30.0 %copy-start.9 = (bf16[72,72]{1,0:T(8,128)(2,1)S(1)}, bf16[72,72]{1,0:T(8,128)(2,1)}, u32[]{:S(2)}) copy-start(bf16[72,72]{1,0:T(8,128)(2,1)} %mix_ref.6) | copy-start | bytes 31108
  51.0 15.5 %all-to-all-start.2 = ((f32[16,20,4,128]{3,2,1,0:T(4,128)}), f32[16,20,4,128]{3,2,1,0:T(4,128)S(1)}, u32[]{:S(2)}, u32[]{:S(2)}) async-start(f32[16,20,4,128]{3,2,1,0:T(4,128)} %get-tuple-element.30), calls=%async_computation.2 | async-start | bytes 1310720 | tf_op jit(solution)/shard_map/all_to_all | solution.py:518
  66.5 19.0 %all-to-all-start.3 = ((f32[16,20,4,128]{3,2,1,0:T(4,128)}), f32[16,20,4,128]{3,2,1,0:T(4,128)S(1)}, u32[]{:S(2)}, u32[]{:S(2)}) async-start(f32[16,20,4,128]{3,2,1,0:T(4,128)} %get-tuple-element.36), calls=%async_computation.3 | async-start | bytes 1310720 | tf_op jit(solution)/shard_map/all_to_all | solution.py:518
  71.5 15.4 %copy-start.3 = (f32[4,8192]{1,0:T(4,128)S(1)}, f32[4,8192]{1,0:T(4,128)}, u32[]{:S(2)}) copy-start(f32[4,8192]{1,0:T(4,128)} %land_ref.1) | copy-start | bytes 393220
  71.6 15.4 %copy-start.8 = (f32[8192]{0:T(1024)S(1)}, f32[8192]{0:T(1024)}, u32[]{:S(2)}) copy-start(f32[8192]{0:T(1024)} %param.19) | copy-start | bytes 98308
  71.6 15.4 %collective-permute-start.1 = (f32[4,10240]{1,0:T(4,128)S(1)}, f32[4,10240]{1,0:T(4,128)S(1)}, u32[]{:S(2)}, u32[]{:S(2)}) collective-permute-start(f32[4,10240]{1,0:T(4,128)S(1)} %collect_away.1), channel_id=1, source_target_pairs={{0,16},{16,0},{1,17},{17,1},{2,18},{18,2},{3,19},{19,3},{4,20},{20... | collective-permute-start | bytes 491528 | tf_op jit(solution)/shard_map/ppermute | solution.py:521

commit v3 on v2

--- a/solution.py
+++ b/solution.py
@@ -216,16 +216,26 @@
     )(mixing, *[state] * len(specs))
 
 
-def serve_kernel(per_owner, far_ref, asked_ref, own_ref, other_ref, out_ref, blocks_ref):
+def serve_kernel(
+    per_owner, far_ref, asked_ref, own_ref, other_ref, out_ref, blocks_ref, arrived_sem
+):
+    copies = [
+        pltpu.make_async_copy(ref, blocks_ref.at[index], arrived_sem.at[index])
+        for index, ref in enumerate((own_ref, other_ref))
+    ]
+    for copy in copies:
+        copy.start()
+    for copy in copies:
+        copy.wait()
     far = far_ref[0]
-    blocks_ref[far] = own_ref[...]
-    blocks_ref[1 - far] = other_ref[...]
 
     def body(peer, carry):
         for shard in range(2):
             for slot in range(per_owner):
                 spot = shard * per_owner + slot
-                out_ref[peer, spot] = blocks_ref[shard, :, window(asked_ref[peer, spot])]
+                out_ref[peer, spot] = blocks_ref[
+                    shard ^ far, :, window(asked_ref[peer, spot])
+                ]
         return carry
 
     lax.fori_loop(0, out_ref.shape[0], body, 0)
@@ -239,33 +249,21 @@
 GROUP = 8
 
 
-def middle_kernel(
-    far_ref,
+def hot_kernel(
     place_ref,
-    spot_ref,
-    mix_ref,
-    arrived_ref,
     column_ref,
-    ocean_weight_ref,
     atmos_weight_ref,
     mask_ref,
-    base_ref,
-    state_ref,
-    forcing_ref,
-    away_ref,
-    home_ref,
+    hot_ref,
+    share_ref,
     lanes_ref,
-    value_ref,
-    *share_refs,
+    *sums,
 ):
     intersections, cells = column_ref.shape
     windows = cells // LANES
-    fields = base_ref.shape[0]
-    near, packed = away_ref.shape[:2]
-    per_owner = packed * fields // (fields + 1)
-    for ref in (value_ref, *share_refs):
+    fields = share_ref.shape[1]
+    for ref in sums:
         ref[...] = jnp.zeros(ref.shape, jnp.float32)
-    corner = mix_ref[0, 0]
     group_tiles = GROUP * intersections
     steps = LANES // intersections
     for first in range(0, windows, steps):
@@ -287,11 +285,77 @@
     field_ids = lax.broadcasted_iota(jnp.int32, (fields, LANES), 0)
     share_rows = lax.broadcasted_iota(jnp.int32, (2 * intersections, LANES), 0)
     first_half = share_rows % intersections < 2
-    blank = jnp.zeros((2 * fields, LANES), jnp.float32)
-    top = 2 * fields * intersections
 
     def body(group, carry):
         turned = lanes_ref[group]
+        for inner in range(GROUP):
+            step = group * GROUP + inner
+            here = window(step)
+            share = atmos_weight_ref[:, here] * mask_ref[:, here].astype(jnp.float32)
+            hot = []
+            for k in range(intersections):
+                tile = inner * intersections + k
+                lane_of = jnp.broadcast_to(turned[:, tile : tile + 1], (LANES, LANES))
+                hot.append(jnp.where(lane_of == column_ids, one, zero))
+            hot = jnp.concatenate(
+                [
+                    jnp.concatenate([hot[0], hot[1]], axis=1),
+                    jnp.concatenate([hot[2], hot[3]], axis=1),
+                ],
+                axis=0,
+            )
+            hot_ref[step] = hot
+            parts = split_high(share)
+            rows = jnp.concatenate(
+                [jnp.where(first_half, parts, 0.0), jnp.where(first_half, 0.0, parts)], axis=1
+            ).astype(jnp.bfloat16)
+            spread = jnp.dot(rows, hot, preferred_element_type=jnp.float32)
+            for k in range(intersections):
+                side = slice((k % 2) * LANES, (k % 2 + 1) * LANES)
+                low = intersections + k
+                shared = spread[k : k + 1, side] + spread[low : low + 1, side]
+                place = place_ref[k, step]
+                sums[k][lax.div(place, fields)] += jnp.where(
+                    field_ids == lax.rem(place, fields), shared, 0.0
+                )
+        return carry
+
+    lax.fori_loop(0, windows // GROUP, body, 0)
+    total = sums[0][...]
+    for ref in sums[1:]:
+        total = total + ref[...]
+    share_ref[...] = total
+
+
+def middle_kernel(
+    far_ref,
+    place_ref,
+    spot_ref,
+    mix_ref,
+    arrived_ref,
+    column_ref,
+    ocean_weight_ref,
+    atmos_weight_ref,
+    mask_ref,
+    base_ref,
+    state_ref,
+    hot_ref,
+    share_ref,
+    forcing_ref,
+    away_ref,
+    home_ref,
+    value_ref,
+):
+    intersections, cells = column_ref.shape
+    windows = cells // LANES
+    fields = base_ref.shape[0]
+    near, packed = away_ref.shape[:2]
+    per_owner = packed * fields // (fields + 1)
+    value_ref[...] = jnp.zeros(value_ref.shape, jnp.float32)
+    corner = mix_ref[0, 0]
+    blank = jnp.zeros((2 * fields, LANES), jnp.float32)
+
+    def body(group, carry):
         for inner in range(GROUP):
             step = group * GROUP + inner
             here = window(step)
@@ -299,9 +363,7 @@
             ocean_weight = ocean_weight_ref[:, here]
             total = jnp.zeros((fields, LANES), jnp.float32)
             weight = jnp.zeros((1, LANES), jnp.float32)
-            where = []
             for k in range(intersections):
-                where.append(place_ref[k, step])
                 picked = jnp.take_along_axis(
                     arrived_ref[spot_ref[k, step]],
                     jnp.broadcast_to(lanes[k : k + 1], (fields, LANES)),
@@ -317,39 +379,18 @@
                 mask == 1, base_ref[:, here] + corner * forcing, state_ref[:, here]
             )
             share = atmos_weight_ref[:, here] * mask.astype(jnp.float32)
-            hot = []
-            for k in range(intersections):
-                tile = inner * intersections + k
-                lane_of = jnp.broadcast_to(turned[:, tile : tile + 1], (LANES, LANES))
-                hot.append(jnp.where(lane_of == column_ids, one, zero))
-            hot = jnp.concatenate(
-                [
-                    jnp.concatenate([hot[0], hot[1]], axis=1),
-                    jnp.concatenate([hot[2], hot[3]], axis=1),
-                ],
-                axis=0,
-            )
             parts = [split_high(share[k : k + 1] * surface) for k in range(intersections)]
-            share_parts = split_high(share)
-            left = [parts[0], parts[1], blank, blank, jnp.where(first_half, share_parts, 0.0)]
-            right = [blank, blank, parts[2], parts[3], jnp.where(first_half, 0.0, share_parts)]
+            left = [parts[0], parts[1], blank, blank]
+            right = [blank, blank, parts[2], parts[3]]
             rows = jnp.concatenate(
                 [jnp.concatenate(left, axis=0), jnp.concatenate(right, axis=0)], axis=1
             ).astype(jnp.bfloat16)
-            spread = jnp.dot(rows, hot, preferred_element_type=jnp.float32)
+            spread = jnp.dot(rows, hot_ref[step], preferred_element_type=jnp.float32)
             for k in range(intersections):
-                place = where[k]
                 side = slice((k % 2) * LANES, (k % 2 + 1) * LANES)
                 at = 2 * fields * k
-                value_ref[place] = (
+                value_ref[place_ref[k, step]] = (
                     spread[at : at + fields, side] + spread[at + fields : at + 2 * fields, side]
-                )
-                shared = (
-                    spread[top + k : top + k + 1, side]
-                    + spread[top + intersections + k : top + intersections + k + 1, side]
-                )
-                share_refs[k][lax.div(place, fields)] += jnp.where(
-                    field_ids == lax.rem(place, fields), shared, 0.0
                 )
         return carry
 
@@ -359,10 +400,7 @@
     for ref, shard in ((away_ref, 1 - far), (home_ref, far)):
         values = value_ref[pl.ds(shard * near * per_owner, near * per_owner)]
         ref[:, :per_owner] = values.reshape(near, per_owner, fields, LANES)
-        at = pl.ds(shard * near * rows, near * rows)
-        shares = share_refs[0][at]
-        for share_ref in share_refs[1:]:
-            shares = shares + share_ref[at]
+        shares = share_ref[pl.ds(shard * near * rows, near * rows)]
         ref[:, per_owner:] = shares.reshape(near, rows, fields, LANES)
 
 
@@ -532,35 +570,49 @@
     )
     asked = to_near(wanted)
     other_rows = to_far(forcing_rows)
+    base, first_level = top_level(state, ocean_mixing)
+    asked, base, first_level = lax.optimization_barrier((asked, base, first_level))
     served = pl.pallas_call(
         functools.partial(serve_kernel, per_owner),
-        in_specs=[smem, smem, vmem, vmem],
+        in_specs=[smem, smem] + [pl.BlockSpec(memory_space=pl.ANY)] * 2,
         out_specs=vmem,
         out_shape=jax.ShapeDtypeStruct((near, spots, fields, LANES), jnp.float32),
-        scratch_shapes=[pltpu.VMEM((2, fields, columns), jnp.float32)],
+        scratch_shapes=[
+            pltpu.VMEM((2, fields, columns), jnp.float32),
+            pltpu.SemaphoreType.DMA((2,)),
+        ],
         compiler_params=params,
         name="serve_windows",
     )(far, asked, forcing_rows, other_rows)
+    served, columns_asked = lax.optimization_barrier((served, parent_column))
     arrived = to_near(served)
-    base, first_level = top_level(state, ocean_mixing)
-    arrived, base = lax.optimization_barrier((arrived, base))
-
     rows = per_owner // fields
+    windows = cells // LANES
+    hot, shares = pl.pallas_call(
+        hot_kernel,
+        in_specs=[smem] + [vmem] * 3,
+        out_specs=[vmem] * 2,
+        out_shape=[
+            jax.ShapeDtypeStruct((windows, 2 * LANES, 2 * LANES), jnp.bfloat16),
+            jax.ShapeDtypeStruct((2 * near * rows, fields, LANES), jnp.float32),
+        ],
+        scratch_shapes=[pltpu.VMEM((windows // GROUP, LANES, LANES), jnp.bfloat16)]
+        + [pltpu.VMEM((2 * near * rows, fields, LANES), jnp.float32)] * intersections,
+        compiler_params=params,
+        name="one_hot_and_shares",
+    )(place, columns_asked, atmos_weight, mask)
+    arrived, hot, shares = lax.optimization_barrier((arrived, hot, shares))
     sent = (near, per_owner + rows, fields, LANES)
     forcing, away, home = pl.pallas_call(
         middle_kernel,
-        in_specs=[smem] * 4 + [vmem] * 7,
+        in_specs=[smem] * 4 + [vmem] * 9,
         out_specs=[vmem] * 3,
         out_shape=[
             jax.ShapeDtypeStruct((fields, cells), jnp.float32),
             jax.ShapeDtypeStruct(sent, jnp.float32),
             jax.ShapeDtypeStruct(sent, jnp.float32),
         ],
-        scratch_shapes=[
-            pltpu.VMEM((cells // LANES // GROUP, LANES, LANES), jnp.bfloat16),
-            pltpu.VMEM((near * spots, fields, LANES), jnp.float32),
-        ]
-        + [pltpu.VMEM((2 * near * rows, fields, LANES), jnp.float32)] * intersections,
+        scratch_shapes=[pltpu.VMEM((near * spots, fields, LANES), jnp.float32)],
         compiler_params=params,
         name="forcing_and_windows",
     )(
@@ -575,6 +627,8 @@
         mask,
         base,
         first_level,
+        hot,
+        shares,
     )
     tendency, forcing = lax.optimization_barrier((tendency, forcing))
     atmos_updated = diffuse_atmos(atmos_profiles, atmos_mixing, tendency)

time: 88.5 us -> 87.5 us (0.989)
  waiting for transfers between devices: 24.7 us -> 13.1 us
  local copies, waits for them, and re-layouts: 0.97 us -> 7.46 us
  Pallas kernels: 41.1 us -> 44 us
  starting transfers between devices: 20.2 us -> 21.3 us
    all_to_all x4, waiting for transfers between devices: 24.7 us -> 13.1 us  [to_near(): lax.all_to_all(values, ('near', 'sub'), split_axis=0, concat_axis=0, tile...]
    unnamed x24 -> x30, local copies, waits for them, and re-layouts: 0.97 us -> 7.46 us
    pallas_call x1 -> x2, Pallas kernels: 10.3 us -> 12.7 us  [the longest x1 7.64 us: per_device(): pl.pallas_call(hot_kernel, in_specs=[smem] + [vmem] * 3, out_specs=[vmem]...]
    all_to_all x4, starting transfers between devices: 15.7 us -> 16.8 us  [to_near(): lax.all_to_all(values, ('near', 'sub'), split_axis=0, concat_axis=0, tile...]
  transfers between devices with their start and end apart: 6 -> 6, of which waited for: 4 -> 4; matrix products, arithmetic and copies ran while one was open for 0% -> 0% of each run, Pallas kernels for 29% -> 38%
where the time goes in v3:
time: 87.5 us; the launch traced here: 86.7 us
  Pallas kernels  44 us (50%)
  starting transfers between devices  21.3 us (24%)
  waiting for transfers between devices  13.1 us (15%)
  local copies, waits for them, and re-layouts  7.46 us (9%)
    all_to_all x4, starting transfers between devices, to_near(): lax.all_to_all(values, ('near', 'sub'), split_axis=0, concat_axis=0, tile...  16.8 us
    all_to_all x4, waiting for transfers between devices, to_near(): lax.all_to_all(values, ('near', 'sub'), split_axis=0, concat_axis=0, tile...  13.1 us
    pallas_call x1, Pallas kernels, diffuse_ocean(): pl.pallas_call(ocean_kernel, grid=(cells // block,), in_specs=[pl.BlockSp...  12.1 us
    pallas_call x1, Pallas kernels, per_device(): pl.pallas_call(hot_kernel, in_specs=[smem] + [vmem] * 3, out_specs=[vmem]...  7.64 us
    unnamed x30, local copies, waits for them, and re-layouts  7.46 us
    pallas_call x1, Pallas kernels, diffuse_atmos(): pl.pallas_call(atmos_kernel, grid=(columns // block,), in_specs=[pl.Block...  5.85 us
    pallas_call x1, Pallas kernels, per_device(): pl.pallas_call(middle_kernel, in_specs=[smem] * 4 + [vmem] * 9, out_specs...  5.1 us
    ppermute x2, starting transfers between devices, to_far(): return lax.ppermute(values, 'far', ((0, 1), (1, 0)))  4.48 us
  transfers between devices with their start and end apart: 6, of which 4 were waited for; matrix products, arithmetic and copies ran while one was open for 0% of the time, Pallas kernels for 38%

profile of v3, /device:TPU:0, one launch (start us, length us, event | category | flops | bytes accessed | tf_op | source)
XLA Modules:
  0.0 86.7 jit_solution(8334411220028912913)
XLA Ops:
  0.6 2.5 %requests_and_rates.1 = (s32[4,64]{1,0:T(4,128)}, s32[4,64]{1,0:T(4,128)}, s32[16,32]{1,0:T(8,128)}, f32[4,8192]{1,0:T(4,128)}, f32[4,8192]{1,0:T(4,128)}) custom-call(s32[4,8192]{1,0:T(4,128)} %slot_ref.1, s32[4,8192]{1,0:T(4,128)} %column_ref.4, bf16[4,72,8192]{2,1,0:T(8,128)(2,1)} %refs_3_.1, f32[1,8192]{1,0:T(1,128)} %bitcast.28, f32[4,8192]{1,0:T(4,128)} %before_ref.1, ...), custom_call_target="tpu_custom_call" | custom-call | tf_op jit(solution)/shard_map/requests_and_rates/pallas_call | solution.py:117
  3.1 4.1 %collective-permute-start = (f32[4,8192]{1,0:T(4,128)}, f32[4,8192]{1,0:T(4,128)S(1)}, u32[]{:S(2)}, u32[]{:S(2)}) collective-permute-start(f32[4,8192]{1,0:T(4,128)} %get-tuple-element.36.own_ref), channel_id=1, source_target_pairs={{0,16},{16,0},{1,17},{17,1},{2,18},{18,2},{3,19},{19,3},{4,20},{20... | collective-permute-start | bytes 393224 | tf_op jit(solution)/shard_map/ppermute | solution.py:559
  7.2 4.8 %all-to-all-start = ((s32[16,1,32]{2,1,0:T(1,128)}), s32[16,1,32]{2,1,0:T(1,128)S(1)}, u32[]{:S(2)}, u32[]{:S(2)}) async-start(s32[16,1,32]{2,1,0:T(1,128)} %bitcast.29), calls=%async_computation | async-start | bytes 16384 | tf_op jit(solution)/shard_map/all_to_all | solution.py:556
  12.0 0.0 copy-start.4
  12.0 0.7 copy-done.4
  12.8 0.0 copy-start.13
  12.8 0.0 copy-start.5
  12.8 0.0 copy-start.7
  12.8 4.2 %top_level.1 = (f32[4,8192]{1,0:T(4,128)S(1)}, f32[4,8192]{1,0:T(4,128)S(1)}) custom-call(f32[60,60]{1,0:T(8,128)S(1)} %copy-done.4, f32[60,4,8192]{2,1,0:T(4,128)} %bitcast.19, f32[60,4,8192]{2,1,0:T(4,128)} %bitcast.20, f32[60,4,8192]{2,1,0:T(4,128)} %bitcast.21, f32[60,4,8192]{2,1,0:T(4,128)} %bitcast.22), custom_call_target="tpu_custom_call" | custom-call | flops 3932160 | bytes 7864320 | tf_op jit(solution)/shard_map/top_level/pallas_call | solution.py:203
  17.1 0.0 copy-start.12
  17.1 0.4 all-to-all-done
  17.4 0.0 collective-permute-done.other_ref
  17.4 3.0 %serve_windows.1 = f32[16,32,4,128]{3,2,1,0:T(4,128)} custom-call(s32[1]{0:T(128)} %bitcast.far_ref, s32[16,32]{1,0:T(8,128)S(1)} %bitcast.15, f32[4,8192]{1,0:T(4,128)S(1)} %copy-done.10, f32[4,8192]{1,0:T(4,128)S(1)} %collective-permute-done.other_ref), custom_call_target="tpu_custom_call" | custom-call | tf_op jit(solution)/shard_map/serve_windows/pallas_call | solution.py:575
  20.5 4.8 %all-to-all-start.1 = ((f32[16,32,4,128]{3,2,1,0:T(4,128)}), f32[16,32,4,128]{3,2,1,0:T(4,128)S(1)}, u32[]{:S(2)}, u32[]{:S(2)}) async-start(f32[16,32,4,128]{3,2,1,0:T(4,128)} %serve_windows.1), calls=%async_computation.1 | async-start | bytes 2097152 | tf_op jit(solution)/shard_map/all_to_all | solution.py:556
  25.3 7.6 %one_hot_and_shares.1 = (bf16[64,256,256]{2,1,0:T(8,128)(2,1)S(1)}, f32[128,4,128]{2,1,0:T(4,128)S(1)}) custom-call(s32[4,64]{1,0:T(4,128)S(1)} %copy-done.13, s32[4,8192]{1,0:T(4,128)S(1)} %copy-done.2, f32[4,8192]{1,0:T(4,128)S(1)} %copy-done.3, s32[1,8192]{1,0:T(1,128)S(1)} %bitcast.12), custom_call_target="tpu_custom_call" | custom-call | tf_op jit(solution)/shard_map/one_hot_and_shares/pallas_call | solution.py:591
  33.0 3.3 %copy-done = bf16[64,256,256]{2,1,0:T(8,128)(2,1)} copy-done((bf16[64,256,256]{2,1,0:T(8,128)(2,1)}, bf16[64,256,256]{2,1,0:T(8,128)(2,1)S(1)}, u32[]{:S(2)}) %copy-start) | copy-done | bytes 8388632
  36.3 5.2 %all-to-all-done.1 = f32[16,32,4,128]{3,2,1,0:T(4,128)S(1)} async-done(((f32[16,32,4,128]{3,2,1,0:T(4,128)}), f32[16,32,4,128]{3,2,1,0:T(4,128)S(1)}, u32[]{:S(2)}, u32[]{:S(2)}) %all-to-all-start.1) | async-done | bytes 1048608 | tf_op jit(solution)/shard_map/all_to_all | solution.py:556
  41.5 3.4 %copy-done.1 = bf16[64,256,256]{2,1,0:T(8,128)(2,1)S(1)} copy-done((bf16[64,256,256]{2,1,0:T(8,128)(2,1)S(1)}, bf16[64,256,256]{2,1,0:T(8,128)(2,1)}, u32[]{:S(2)}) %copy-start.1) | copy-done | bytes 8388632
  44.9 5.1 %forcing_and_windows.1 = (f32[4,8192]{1,0:T(4,128)S(1)}, f32[16,20,4,128]{3,2,1,0:T(4,128)}, f32[16,20,4,128]{3,2,1,0:T(4,128)}) custom-call(s32[1]{0:T(128)} %bitcast.far_ref, s32[4,64]{1,0:T(4,128)S(1)} %copy-done.13, s32[4,64]{1,0:T(4,128)S(1)} %copy-done.14, f32[60,60]{1,0:T(8,128)S(1)} %copy-done.5, f32[512,4,128]{2,1,0:T(4,128)S(1)} %bitcast.11, ...), custom_call_target="tpu_custom_call" | custom-call | tf_op jit(solution)/shard_map/forcing_and_windows/pallas_call | solution.py:606
  50.0 3.6 %all-to-all-start.2 = ((f32[16,20,4,128]{3,2,1,0:T(4,128)}), f32[16,20,4,128]{3,2,1,0:T(4,128)S(1)}, u32[]{:S(2)}, u32[]{:S(2)}) async-start(f32[16,20,4,128]{3,2,1,0:T(4,128)} %get-tuple-element.46), calls=%async_computation.2 | async-start | bytes 1310720 | tf_op jit(solution)/shard_map/all_to_all | solution.py:556
  53.6 5.8 %diffuse_atmos.1 = bf16[4,72,8192]{2,1,0:T(8,128)(2,1)} custom-call(bf16[72,72]{1,0:T(8,128)(2,1)S(1)} %copy-done.12, f32[4,8192]{1,0:T(4,128)S(1)} %copy-done.8, bf16[4,72,8192]{2,1,0:T(8,128)(2,1)} %refs_3_.1, bf16[4,72,8192]{2,1,0:T(8,128)(2,1)} %refs_3_.1, bf16[4,72,8192]{2,1,0:T(8,128)(2,1)} %refs_3_.1, bf16[4,72,8192]{2,1,0:T(8,128)(2,1)} %refs_3_.1), custom_call_target="tpu_custom_call" | custom-call | flops 339738624 | bytes 9437184 | tf_op jit(solution)/shard_map/diffuse_atmos/pallas_call | solution.py:157
  59.4 6.0 %all-to-all-done.2.back_ref = f32[16,20,4,128]{3,2,1,0:T(4,128)S(1)} async-done(((f32[16,20,4,128]{3,2,1,0:T(4,128)}), f32[16,20,4,128]{3,2,1,0:T(4,128)S(1)}, u32[]{:S(2)}, u32[]{:S(2)}) %all-to-all-start.2) | async-done | bytes 655392 | tf_op jit(solution)/shard_map/all_to_all | solution.py:556
  65.5 3.6 %all-to-all-start.3 = ((f32[16,20,4,128]{3,2,1,0:T(4,128)}), f32[16,20,4,128]{3,2,1,0:T(4,128)S(1)}, u32[]{:S(2)}, u32[]{:S(2)}) async-start(f32[16,20,4,128]{3,2,1,0:T(4,128)} %get-tuple-element.52), calls=%async_computation.3 | async-start | bytes 1310720 | tf_op jit(solution)/shard_map/all_to_all | solution.py:556
  69.1 1.4 %collect_away.1 = f32[4,10240]{1,0:T(4,128)S(1)} custom-call(s32[1]{0:T(128)} %bitcast.far_ref, s32[16,32]{1,0:T(8,128)S(1)} %bitcast.16, f32[16,20,4,128]{3,2,1,0:T(4,128)S(1)} %all-to-all-done.2.back_ref), custom_call_target="tpu_custom_call" | custom-call | tf_op jit(solution)/shard_map/collect_away/pallas_call | solution.py:504
  70.5 0.0 copy-start.9
  70.5 0.0 copy-start.11
  70.5 0.4 collective-permute-start.1
  70.9 12.1 %diffuse_ocean.1 = f32[60,4,8192]{2,1,0:T(4,128)} custom-call(f32[60,60]{1,0:T(8,128)S(1)} %copy-done.5, f32[4,8192]{1,0:T(4,128)S(1)} %get-tuple-element.53.forcing_ref, s32[1,8192]{1,0:T(1,128)S(1)} %bitcast.14, f32[60,4,8192]{2,1,0:T(4,128)} %bitcast.23, f32[60,4,8192]{2,1,0:T(4,128)} %bitcast.24, f32[60,4,8192]{2,1,0:T(4,128)} %bitcast.25, ...), custom_call_target="tpu_custom_call" | custom-call | flops 2831155200 | bytes 15728640 | tf_op jit(solution)/shard_map/diffuse_ocean/pallas_call | solution.py:449
  83.0 1.5 %all-to-all-done.3.back_ref = f32[16,20,4,128]{3,2,1,0:T(4,128)S(1)} async-done(((f32[16,20,4,128]{3,2,1,0:T(4,128)}), f32[16,20,4,128]{3,2,1,0:T(4,128)S(1)}, u32[]{:S(2)}, u32[]{:S(2)}) %all-to-all-start.3) | async-done | bytes 655392 | tf_op jit(solution)/shard_map/all_to_all | solution.py:556
  84.5 1.4 %collect_home.1.keep_ref = f32[4,10240]{1,0:T(4,128)S(1)} custom-call(s32[1]{0:T(128)} %bitcast.far_ref, s32[16,32]{1,0:T(8,128)S(1)} %bitcast.17, f32[16,20,4,128]{3,2,1,0:T(4,128)S(1)} %all-to-all-done.3.back_ref), custom_call_target="tpu_custom_call" | custom-call | tf_op jit(solution)/shard_map/collect_home/pallas_call | solution.py:504
  85.9 0.0 collective-permute-done.1.other_ref
  86.0 0.7 surface_state.1
  (20 shorter events, 0.0 us)
Async XLA Ops:
  3.1 14.3 %collective-permute-start = (f32[4,8192]{1,0:T(4,128)}, f32[4,8192]{1,0:T(4,128)S(1)}, u32[]{:S(2)}, u32[]{:S(2)}) collective-permute-start(f32[4,8192]{1,0:T(4,128)} %get-tuple-element.36.own_ref), channel_id=1, source_target_pairs={{0,16},{16,0},{1,17},{17,1},{2,18},{18,2},{3,19},{19,3},{4,20},{20... | collective-permute-start | bytes 393224 | tf_op jit(solution)/shard_map/ppermute | solution.py:559
  7.2 10.3 %all-to-all-start = ((s32[16,1,32]{2,1,0:T(1,128)}), s32[16,1,32]{2,1,0:T(1,128)S(1)}, u32[]{:S(2)}, u32[]{:S(2)}) async-start(s32[16,1,32]{2,1,0:T(1,128)} %bitcast.29), calls=%async_computation | async-start | bytes 16384 | tf_op jit(solution)/shard_map/all_to_all | solution.py:556
  12.0 0.8 copy-start.4
  12.8 4.6 %copy-start.10 = (f32[4,8192]{1,0:T(4,128)S(1)}, f32[4,8192]{1,0:T(4,128)}, u32[]{:S(2)}) copy-start(f32[4,8192]{1,0:T(4,128)} %get-tuple-element.36.own_ref) | copy-start | bytes 393220
  12.8 12.5 %copy-start.2 = (s32[4,8192]{1,0:T(4,128)S(1)}, s32[4,8192]{1,0:T(4,128)}, u32[]{:S(2)}) copy-start(s32[4,8192]{1,0:T(4,128)} %column_ref.4) | copy-start | bytes 393220
  12.8 12.5 %copy-start.3 = (f32[4,8192]{1,0:T(4,128)S(1)}, f32[4,8192]{1,0:T(4,128)}, u32[]{:S(2)}) copy-start(f32[4,8192]{1,0:T(4,128)} %atmos_weight_ref.3) | copy-start | bytes 393220
  12.8 12.5 %copy-start.6 = (s32[8192]{0:T(1024)S(1)}, s32[8192]{0:T(1024)}, u32[]{:S(2)}) copy-start(s32[8192]{0:T(1024)} %param.23) | copy-start | bytes 98308
  12.8 12.5 %copy-start.13 = (s32[4,64]{1,0:T(4,128)S(1)}, s32[4,64]{1,0:T(4,128)}, u32[]{:S(2)}) copy-start(s32[4,64]{1,0:T(4,128)} %get-tuple-element.30.place_ref) | copy-start | bytes 3076
  12.8 28.7 %copy-start.5 = (f32[60,60]{1,0:T(8,128)S(1)}, f32[60,60]{1,0:T(8,128)}, u32[]{:S(2)}) copy-start(f32[60,60]{1,0:T(8,128)} %mix_ref.7) | copy-start | bytes 43204
  12.8 28.6 %copy-start.7 = (f32[4,8192]{1,0:T(4,128)S(1)}, f32[4,8192]{1,0:T(4,128)}, u32[]{:S(2)}) copy-start(f32[4,8192]{1,0:T(4,128)} %ocean_weight_ref.1) | copy-start | bytes 393220
  12.8 28.6 %copy-start.14 = (s32[4,64]{1,0:T(4,128)S(1)}, s32[4,64]{1,0:T(4,128)}, u32[]{:S(2)}) copy-start(s32[4,64]{1,0:T(4,128)} %get-tuple-element.31.spot_ref) | copy-start | bytes 3076
  17.1 36.5 %copy-start.8 = (f32[4,8192]{1,0:T(4,128)S(1)}, f32[4,8192]{1,0:T(4,128)}, u32[]{:S(2)}) copy-start(f32[4,8192]{1,0:T(4,128)} %get-tuple-element.49.tend_ref) | copy-start | bytes 393220
  17.1 36.5 %copy-start.12 = (bf16[72,72]{1,0:T(8,128)(2,1)S(1)}, bf16[72,72]{1,0:T(8,128)(2,1)}, u32[]{:S(2)}) copy-start(bf16[72,72]{1,0:T(8,128)(2,1)} %mix_ref.6) | copy-start | bytes 31108
  20.5 21.0 %all-to-all-start.1 = ((f32[16,32,4,128]{3,2,1,0:T(4,128)}), f32[16,32,4,128]{3,2,1,0:T(4,128)S(1)}, u32[]{:S(2)}, u32[]{:S(2)}) async-start(f32[16,32,4,128]{3,2,1,0:T(4,128)} %serve_windows.1), calls=%async_computation.1 | async-start | bytes 2097152 | tf_op jit(solution)/shard_map/all_to_all | solution.py:556
  33.0 3.3 %copy-start = (bf16[64,256,256]{2,1,0:T(8,128)(2,1)}, bf16[64,256,256]{2,1,0:T(8,128)(2,1)S(1)}, u32[]{:S(2)}) copy-start(bf16[64,256,256]{2,1,0:T(8,128)(2,1)S(1)} %get-tuple-element.44.hot_ref) | copy-start | bytes 25165828
  41.5 3.4 %copy-start.1 = (bf16[64,256,256]{2,1,0:T(8,128)(2,1)S(1)}, bf16[64,256,256]{2,1,0:T(8,128)(2,1)}, u32[]{:S(2)}) copy-start(bf16[64,256,256]{2,1,0:T(8,128)(2,1)} %copy-done) | copy-start | bytes 25165828
  50.0 15.5 %all-to-all-start.2 = ((f32[16,20,4,128]{3,2,1,0:T(4,128)}), f32[16,20,4,128]{3,2,1,0:T(4,128)S(1)}, u32[]{:S(2)}, u32[]{:S(2)}) async-start(f32[16,20,4,128]{3,2,1,0:T(4,128)} %get-tuple-element.46), calls=%async_computation.2 | async-start | bytes 1310720 | tf_op jit(solution)/shard_map/all_to_all | solution.py:556
  65.5 19.0 %all-to-all-start.3 = ((f32[16,20,4,128]{3,2,1,0:T(4,128)}), f32[16,20,4,128]{3,2,1,0:T(4,128)S(1)}, u32[]{:S(2)}, u32[]{:S(2)}) async-start(f32[16,20,4,128]{3,2,1,0:T(4,128)} %get-tuple-element.52), calls=%async_computation.3 | async-start | bytes 1310720 | tf_op jit(solution)/shard_map/all_to_all | solution.py:556
  70.5 15.4 %copy-start.9 = (f32[4,8192]{1,0:T(4,128)S(1)}, f32[4,8192]{1,0:T(4,128)}, u32[]{:S(2)}) copy-start(f32[4,8192]{1,0:T(4,128)} %land_ref.1) | copy-start | bytes 393220
  70.5 15.4 %copy-start.11 = (f32[8192]{0:T(1024)S(1)}, f32[8192]{0:T(1024)}, u32[]{:S(2)}) copy-start(f32[8192]{0:T(1024)} %param.19) | copy-start | bytes 98308
  70.5 15.4 %collective-permute-start.1 = (f32[4,10240]{1,0:T(4,128)S(1)}, f32[4,10240]{1,0:T(4,128)S(1)}, u32[]{:S(2)}, u32[]{:S(2)}) collective-permute-start(f32[4,10240]{1,0:T(4,128)S(1)} %collect_away.1), channel_id=1, source_target_pairs={{0,16},{16,0},{1,17},{17,1},{2,18},{18,2},{3,19},{19,3},{4,20},{20... | collective-permute-start | bytes 491528 | tf_op jit(solution)/shard_map/ppermute | solution.py:559

commit v4 on v3

--- a/solution.py
+++ b/solution.py
@@ -11,9 +11,11 @@
 LANES = 128
 params = pltpu.CompilerParams(vmem_limit_bytes=24 * 1024 * 1024)
 stream_params = pltpu.CompilerParams(vmem_limit_bytes=52 * 1024 * 1024)
+middle_params = pltpu.CompilerParams(vmem_limit_bytes=48 * 1024 * 1024)
 first_params = pltpu.CompilerParams(vmem_limit_bytes=56 * 1024 * 1024)
 vmem = pl.BlockSpec(memory_space=pltpu.VMEM)
 smem = pl.BlockSpec(memory_space=pltpu.SMEM)
+hbm = pl.BlockSpec(memory_space=pl.ANY)
 AXES = ("far", "near", "sub")
 
 
@@ -219,26 +221,31 @@
 def serve_kernel(
     per_owner, far_ref, asked_ref, own_ref, other_ref, out_ref, blocks_ref, arrived_sem
 ):
-    copies = [
-        pltpu.make_async_copy(ref, blocks_ref.at[index], arrived_sem.at[index])
-        for index, ref in enumerate((own_ref, other_ref))
-    ]
-    for copy in copies:
-        copy.start()
-    for copy in copies:
-        copy.wait()
+    @pl.when(pl.program_id(0) == 0)
+    def _():
+        copies = [
+            pltpu.make_async_copy(ref, blocks_ref.at[index], arrived_sem.at[index])
+            for index, ref in enumerate((own_ref, other_ref))
+        ]
+        for copy in copies:
+            copy.start()
+        for copy in copies:
+            copy.wait()
+
     far = far_ref[0]
+    peers = out_ref.shape[0]
+    first = pl.program_id(0) * peers
 
     def body(peer, carry):
         for shard in range(2):
             for slot in range(per_owner):
                 spot = shard * per_owner + slot
                 out_ref[peer, spot] = blocks_ref[
-                    shard ^ far, :, window(asked_ref[peer, spot])
+                    shard ^ far, :, window(asked_ref[first + peer, spot])
                 ]
         return carry
 
-    lax.fori_loop(0, out_ref.shape[0], body, 0)
+    lax.fori_loop(0, peers, body, 0)
 
 
 def split_high(values):
@@ -262,23 +269,27 @@
     intersections, cells = column_ref.shape
     windows = cells // LANES
     fields = share_ref.shape[1]
-    for ref in sums:
-        ref[...] = jnp.zeros(ref.shape, jnp.float32)
     group_tiles = GROUP * intersections
     steps = LANES // intersections
-    for first in range(0, windows, steps):
-        tall = jnp.concatenate(
-            [
-                column_ref[:, (first + step) * LANES : (first + step + 1) * LANES] & (LANES - 1)
-                for step in range(steps)
-            ],
-            axis=0,
-        )
-        turned = tall.astype(jnp.float32).T.astype(jnp.bfloat16)
-        for part in range(steps // GROUP):
-            lanes_ref[first // GROUP + part, :, :group_tiles] = turned[
-                :, part * group_tiles : (part + 1) * group_tiles
-            ]
+    group = pl.program_id(0)
+    @pl.when(group == 0)
+    def _():
+        for ref in sums:
+            ref[...] = jnp.zeros(ref.shape, jnp.float32)
+        for first in range(0, windows, steps):
+            tall = jnp.concatenate(
+                [
+                    column_ref[:, (first + step) * LANES : (first + step + 1) * LANES] & (LANES - 1)
+                    for step in range(steps)
+                ],
+                axis=0,
+            )
+            turned = tall.astype(jnp.float32).T.astype(jnp.bfloat16)
+            for part in range(steps // GROUP):
+                lanes_ref[first // GROUP + part, :, :group_tiles] = turned[
+                    :, part * group_tiles : (part + 1) * group_tiles
+                ]
+
     column_ids = lax.broadcasted_iota(jnp.int32, (LANES, LANES), 1)
     column_ids = column_ids.astype(jnp.float32).astype(jnp.bfloat16)
     one, zero = jnp.bfloat16(1.0), jnp.bfloat16(0.0)
@@ -286,45 +297,44 @@
     share_rows = lax.broadcasted_iota(jnp.int32, (2 * intersections, LANES), 0)
     first_half = share_rows % intersections < 2
 
-    def body(group, carry):
-        turned = lanes_ref[group]
-        for inner in range(GROUP):
-            step = group * GROUP + inner
-            here = window(step)
-            share = atmos_weight_ref[:, here] * mask_ref[:, here].astype(jnp.float32)
-            hot = []
-            for k in range(intersections):
-                tile = inner * intersections + k
-                lane_of = jnp.broadcast_to(turned[:, tile : tile + 1], (LANES, LANES))
-                hot.append(jnp.where(lane_of == column_ids, one, zero))
-            hot = jnp.concatenate(
-                [
-                    jnp.concatenate([hot[0], hot[1]], axis=1),
-                    jnp.concatenate([hot[2], hot[3]], axis=1),
-                ],
-                axis=0,
+    turned = lanes_ref[group]
+    for inner in range(GROUP):
+        step = group * GROUP + inner
+        here = window(step)
+        share = atmos_weight_ref[:, here] * mask_ref[:, here].astype(jnp.float32)
+        hot = []
+        for k in range(intersections):
+            tile = inner * intersections + k
+            lane_of = jnp.broadcast_to(turned[:, tile : tile + 1], (LANES, LANES))
+            hot.append(jnp.where(lane_of == column_ids, one, zero))
+        hot = jnp.concatenate(
+            [
+                jnp.concatenate([hot[0], hot[1]], axis=1),
+                jnp.concatenate([hot[2], hot[3]], axis=1),
+            ],
+            axis=0,
+        )
+        hot_ref[inner] = hot
+        parts = split_high(share)
+        rows = jnp.concatenate(
+            [jnp.where(first_half, parts, 0.0), jnp.where(first_half, 0.0, parts)], axis=1
+        ).astype(jnp.bfloat16)
+        spread = jnp.dot(rows, hot, preferred_element_type=jnp.float32)
+        for k in range(intersections):
+            side = slice((k % 2) * LANES, (k % 2 + 1) * LANES)
+            low = intersections + k
+            shared = spread[k : k + 1, side] + spread[low : low + 1, side]
+            place = place_ref[k, step]
+            sums[k][lax.div(place, fields)] += jnp.where(
+                field_ids == lax.rem(place, fields), shared, 0.0
             )
-            hot_ref[step] = hot
-            parts = split_high(share)
-            rows = jnp.concatenate(
-                [jnp.where(first_half, parts, 0.0), jnp.where(first_half, 0.0, parts)], axis=1
-            ).astype(jnp.bfloat16)
-            spread = jnp.dot(rows, hot, preferred_element_type=jnp.float32)
-            for k in range(intersections):
-                side = slice((k % 2) * LANES, (k % 2 + 1) * LANES)
-                low = intersections + k
-                shared = spread[k : k + 1, side] + spread[low : low + 1, side]
-                place = place_ref[k, step]
-                sums[k][lax.div(place, fields)] += jnp.where(
-                    field_ids == lax.rem(place, fields), shared, 0.0
-                )
-        return carry
-
-    lax.fori_loop(0, windows // GROUP, body, 0)
-    total = sums[0][...]
-    for ref in sums[1:]:
-        total = total + ref[...]
-    share_ref[...] = total
+
+    @pl.when(group == pl.num_programs(0) - 1)
+    def _():
+        total = sums[0][...]
+        for ref in sums[1:]:
+            total = total + ref[...]
+        share_ref[...] = total
 
 
 def middle_kernel(
@@ -345,17 +355,29 @@
     away_ref,
     home_ref,
     value_ref,
+    held_ref,
+    held_sem,
+    sent_sem,
 ):
     intersections, cells = column_ref.shape
     windows = cells // LANES
     fields = base_ref.shape[0]
     near, packed = away_ref.shape[:2]
     per_owner = packed * fields // (fields + 1)
+    rows = per_owner // fields
+
+    def fetch(group):
+        part = pl.ds(group * GROUP, GROUP)
+        return pltpu.make_async_copy(hot_ref.at[part], held_ref.at[part], held_sem.at[group])
+
+    for group in range(windows // GROUP):
+        fetch(group).start()
     value_ref[...] = jnp.zeros(value_ref.shape, jnp.float32)
     corner = mix_ref[0, 0]
     blank = jnp.zeros((2 * fields, LANES), jnp.float32)
 
     def body(group, carry):
+        fetch(group).wait()
         for inner in range(GROUP):
             step = group * GROUP + inner
             here = window(step)
@@ -382,10 +404,10 @@
             parts = [split_high(share[k : k + 1] * surface) for k in range(intersections)]
             left = [parts[0], parts[1], blank, blank]
             right = [blank, blank, parts[2], parts[3]]
-            rows = jnp.concatenate(
+            parts = jnp.concatenate(
                 [jnp.concatenate(left, axis=0), jnp.concatenate(right, axis=0)], axis=1
             ).astype(jnp.bfloat16)
-            spread = jnp.dot(rows, hot_ref[step], preferred_element_type=jnp.float32)
+            spread = jnp.dot(parts, held_ref[step], preferred_element_type=jnp.float32)
             for k in range(intersections):
                 side = slice((k % 2) * LANES, (k % 2 + 1) * LANES)
                 at = 2 * fields * k
@@ -396,12 +418,25 @@
 
     lax.fori_loop(0, windows // GROUP, body, 0)
     far = far_ref[0]
-    rows = per_owner // fields
-    for ref, shard in ((away_ref, 1 - far), (home_ref, far)):
-        values = value_ref[pl.ds(shard * near * per_owner, near * per_owner)]
-        ref[:, :per_owner] = values.reshape(near, per_owner, fields, LANES)
-        shares = share_ref[pl.ds(shard * near * rows, near * rows)]
-        ref[:, per_owner:] = shares.reshape(near, rows, fields, LANES)
+    shards = value_ref.reshape(2, near, per_owner, fields, LANES)
+    copies = []
+    for index, (ref, shard) in enumerate(((away_ref, 1 - far), (home_ref, far))):
+        copies.append(
+            pltpu.make_async_copy(
+                shards.at[shard], ref.at[:, pl.ds(0, per_owner)], sent_sem.at[2 * index]
+            )
+        )
+        copies.append(
+            pltpu.make_async_copy(
+                share_ref.at[shard],
+                ref.at[:, pl.ds(per_owner, rows)],
+                sent_sem.at[2 * index + 1],
+            )
+        )
+    for copy in copies:
+        copy.start()
+    for copy in copies:
+        copy.wait()
 
 
 def ocean_kernel(mix_ref, forcing_ref, mask_ref, *refs):
@@ -468,11 +503,14 @@
     )(mixing, forcing, mask, *[state] * len(specs))
 
 
-def collect_kernel(per_owner, home, far_ref, asked_ref, back_ref, out_ref, *sums):
-    near, packed, fields, _ = back_ref.shape
+def collect_kernel(per_owner, far_ref, asked_ref, back_ref, *refs):
+    near, _, fields, _ = back_ref.shape
+    chains = 4
+    sums = refs[-2 * chains :]
+    rest = refs[: -2 * chains]
+    home = len(rest) > 1
     columns = sums[0].shape[1]
     quarter = columns // fields
-    chains = len(sums) // 2
     far = far_ref[0]
     first = (far if home else 1 - far) * per_owner
     for ref in sums:
@@ -493,36 +531,36 @@
     for chain in range(1, chains):
         values = values + sums[chain][...]
         shares = shares + sums[chains + chain][...]
-    out_ref[:, :columns] = values
-    for row in range(fields):
-        out_ref[row : row + 1, columns:] = shares[:, row * quarter : (row + 1) * quarter]
-
-
-def collect(asked, far, back, per_owner, columns, home):
+    out_ref = rest[-1]
+    if home:
+        other_ref, land_weight_ref, land_ref = rest[:3]
+        land_weight = land_weight_ref[...]
+        total = values + other_ref[:, :columns] + land_weight * land_ref[...]
+        weight = shares + land_weight
+        for row in range(fields):
+            part = slice(row * quarter, (row + 1) * quarter)
+            other_shares = other_ref[row : row + 1, columns:]
+            out_ref[:, part] = total[:, part] / (weight[:, part] + other_shares)
+    else:
+        out_ref[:, :columns] = values
+        for row in range(fields):
+            out_ref[row : row + 1, columns:] = shares[:, row * quarter : (row + 1) * quarter]
+
+
+def collect(asked, far, back, per_owner, columns, rest):
     fields = back.shape[2]
     chains = 4
+    width = columns if rest else columns + columns // fields
     return pl.pallas_call(
-        functools.partial(collect_kernel, per_owner, home),
-        in_specs=[smem, smem, vmem],
+        functools.partial(collect_kernel, per_owner),
+        in_specs=[smem, smem, vmem] + [vmem] * len(rest),
         out_specs=vmem,
-        out_shape=jax.ShapeDtypeStruct((fields, columns + columns // fields), jnp.float32),
+        out_shape=jax.ShapeDtypeStruct((fields, width), jnp.float32),
         scratch_shapes=[pltpu.VMEM((fields, columns), jnp.float32)] * chains
         + [pltpu.VMEM((1, columns), jnp.float32)] * chains,
         compiler_params=params,
-        name="collect_home" if home else "collect_away",
-    )(far, asked, back)
-
-
-def final_kernel(keep_ref, other_ref, land_weight_ref, land_ref, out_ref):
-    fields, columns = out_ref.shape
-    quarter = columns // fields
-    both = keep_ref[:, :columns] + other_ref[:, :columns]
-    shares = keep_ref[:, columns:] + other_ref[:, columns:]
-    land_weight = land_weight_ref[...]
-    total = both + land_weight * land_ref[...]
-    for row in range(fields):
-        part = slice(row * quarter, (row + 1) * quarter)
-        out_ref[:, part] = total[:, part] / (shares[row : row + 1] + land_weight[:, part])
+        name="surface_state" if rest else "collect_away",
+    )(far, asked, back, *rest)
 
 
 def per_device(
@@ -574,8 +612,9 @@
     asked, base, first_level = lax.optimization_barrier((asked, base, first_level))
     served = pl.pallas_call(
         functools.partial(serve_kernel, per_owner),
-        in_specs=[smem, smem] + [pl.BlockSpec(memory_space=pl.ANY)] * 2,
-        out_specs=vmem,
+        grid=(4,),
+        in_specs=[smem, smem, hbm, hbm],
+        out_specs=pl.BlockSpec((near // 4, spots, fields, LANES), lambda i: (i, 0, 0, 0)),
         out_shape=jax.ShapeDtypeStruct((near, spots, fields, LANES), jnp.float32),
         scratch_shapes=[
             pltpu.VMEM((2, fields, columns), jnp.float32),
@@ -590,30 +629,39 @@
     windows = cells // LANES
     hot, shares = pl.pallas_call(
         hot_kernel,
+        grid=(windows // GROUP,),
         in_specs=[smem] + [vmem] * 3,
-        out_specs=[vmem] * 2,
+        out_specs=[
+            pl.BlockSpec((GROUP, 2 * LANES, 2 * LANES), lambda i: (i, 0, 0)),
+            pl.BlockSpec((2 * near * rows, fields, LANES), lambda i: (0, 0, 0)),
+        ],
         out_shape=[
             jax.ShapeDtypeStruct((windows, 2 * LANES, 2 * LANES), jnp.bfloat16),
             jax.ShapeDtypeStruct((2 * near * rows, fields, LANES), jnp.float32),
         ],
         scratch_shapes=[pltpu.VMEM((windows // GROUP, LANES, LANES), jnp.bfloat16)]
         + [pltpu.VMEM((2 * near * rows, fields, LANES), jnp.float32)] * intersections,
-        compiler_params=params,
+        compiler_params=middle_params,
         name="one_hot_and_shares",
     )(place, columns_asked, atmos_weight, mask)
     arrived, hot, shares = lax.optimization_barrier((arrived, hot, shares))
     sent = (near, per_owner + rows, fields, LANES)
     forcing, away, home = pl.pallas_call(
         middle_kernel,
-        in_specs=[smem] * 4 + [vmem] * 9,
-        out_specs=[vmem] * 3,
+        in_specs=[smem] * 4 + [vmem] * 7 + [hbm, vmem],
+        out_specs=[vmem, hbm, hbm],
         out_shape=[
             jax.ShapeDtypeStruct((fields, cells), jnp.float32),
             jax.ShapeDtypeStruct(sent, jnp.float32),
             jax.ShapeDtypeStruct(sent, jnp.float32),
         ],
-        scratch_shapes=[pltpu.VMEM((near * spots, fields, LANES), jnp.float32)],
-        compiler_params=params,
+        scratch_shapes=[
+            pltpu.VMEM((near * spots, fields, LANES), jnp.float32),
+            pltpu.VMEM((windows, 2 * LANES, 2 * LANES), jnp.bfloat16),
+            pltpu.SemaphoreType.DMA((windows // GROUP,)),
+            pltpu.SemaphoreType.DMA((4,)),
+        ],
+        compiler_params=middle_params,
         name="forcing_and_windows",
     )(
         far,
@@ -628,7 +676,7 @@
         base,
         first_level,
         hot,
-        shares,
+        shares.reshape(2, near, rows, fields, LANES),
     )
     tendency, forcing = lax.optimization_barrier((tendency, forcing))
     atmos_updated = diffuse_atmos(atmos_profiles, atmos_mixing, tendency)
@@ -636,19 +684,18 @@
         (to_near(away), atmos_updated, home)
     )
     back_home = to_near(home)
-    sums_away = collect(asked, far, back_away, per_owner, columns, False)
+    sums_away = collect(asked, far, back_away, per_owner, columns, ())
     other_sums = to_far(sums_away)
     ocean_updated = diffuse_ocean(state, ocean_mixing, forcing, mask).transpose(1, 0, 2)
     back_home, ocean_updated = lax.optimization_barrier((back_home, ocean_updated))
-    sums_home = collect(asked, far, back_home, per_owner, columns, True)
-    surface_state = pl.pallas_call(
-        final_kernel,
-        in_specs=[vmem] * 4,
-        out_specs=vmem,
-        out_shape=jax.ShapeDtypeStruct((fields, columns), jnp.float32),
-        compiler_params=params,
-        name="surface_state",
-    )(sums_home, other_sums, land_weight.reshape(1, columns), land_surface)
+    surface_state = collect(
+        asked,
+        far,
+        back_home,
+        per_owner,
+        columns,
+        (other_sums, land_weight.reshape(1, columns), land_surface),
+    )
     return (atmos_updated, ocean_updated, surface_state)
 
 

time: 87.5 us -> 85.6 us (0.978)
  local copies, waits for them, and re-layouts: 7.46 us -> 0.81 us
  Pallas kernels: 44 us -> 47.1 us
  waiting for transfers between devices: 13.1 us -> 14.8 us
    unnamed x30 -> x26, local copies, waits for them, and re-layouts: 7.46 us -> 0.81 us
    pallas_call x6 -> x5, Pallas kernels: 19.4 us -> 22.4 us  [the longest x1 9.25 us: per_device(): pl.pallas_call(hot_kernel, grid=(windows // GROUP,), in_specs=[smem] + [v...]
    all_to_all x4, waiting for transfers between devices: 13.1 us -> 14.7 us  [to_near(): lax.all_to_all(values, ('near', 'sub'), split_axis=0, concat_axis=0, tile...]
  transfers between devices with their start and end apart: 6 -> 6, of which waited for: 4 -> 4; matrix products, arithmetic and copies ran while one was open for 0% -> 0% of each run, Pallas kernels for 38% -> 39%
where the time goes in v4:
time: 85.6 us; the launch traced here: 84.8 us
  Pallas kernels  47.1 us (55%)
  starting transfers between devices  21.3 us (25%)
  waiting for transfers between devices  14.8 us (17%)
    all_to_all x4, starting transfers between devices, to_near(): lax.all_to_all(values, ('near', 'sub'), split_axis=0, concat_axis=0, tile...  16.8 us
    all_to_all x4, waiting for transfers between devices, to_near(): lax.all_to_all(values, ('near', 'sub'), split_axis=0, concat_axis=0, tile...  14.7 us
    pallas_call x1, Pallas kernels, diffuse_ocean(): pl.pallas_call(ocean_kernel, grid=(cells // block,), in_specs=[pl.BlockSp...  12.1 us
    pallas_call x1, Pallas kernels, per_device(): pl.pallas_call(hot_kernel, grid=(windows // GROUP,), in_specs=[smem] + [v...  9.25 us
    pallas_call x1, Pallas kernels, per_device(): pl.pallas_call(middle_kernel, in_specs=[smem] * 4 + [vmem] * 7 + [hbm, vm...  6.25 us
    pallas_call x1, Pallas kernels, diffuse_atmos(): pl.pallas_call(atmos_kernel, grid=(columns // block,), in_specs=[pl.Block...  5.86 us
    ppermute x2, starting transfers between devices, to_far(): return lax.ppermute(values, 'far', ((0, 1), (1, 0)))  4.49 us
    pallas_call x1, Pallas kernels, top_level(): pl.pallas_call(top_kernel, grid=(cells // block,), in_specs=[smem] + spec...  4.2 us
  transfers between devices with their start and end apart: 6, of which 4 were waited for; matrix products, arithmetic and copies ran while one was open for 0% of the time, Pallas kernels for 39%

profile of v4, /device:TPU:0, one launch (start us, length us, event | category | flops | bytes accessed | tf_op | source)
XLA Modules:
  0.0 84.8 jit_solution(15297794801326508890)
XLA Ops:
  0.6 2.5 %requests_and_rates.1 = (s32[4,64]{1,0:T(4,128)}, s32[4,64]{1,0:T(4,128)}, s32[16,32]{1,0:T(8,128)}, f32[4,8192]{1,0:T(4,128)}, f32[4,8192]{1,0:T(4,128)}) custom-call(s32[4,8192]{1,0:T(4,128)} %slot_ref.1, s32[4,8192]{1,0:T(4,128)} %column_ref.4, bf16[4,72,8192]{2,1,0:T(8,128)(2,1)} %refs_3_.1, f32[1,8192]{1,0:T(1,128)} %bitcast.30, f32[4,8192]{1,0:T(4,128)} %before_ref.1, ...), custom_call_target="tpu_custom_call" | custom-call | tf_op jit(solution)/shard_map/requests_and_rates/pallas_call | solution.py:119
  3.1 4.1 %collective-permute-start = (f32[4,8192]{1,0:T(4,128)}, f32[4,8192]{1,0:T(4,128)S(1)}, u32[]{:S(2)}, u32[]{:S(2)}) collective-permute-start(f32[4,8192]{1,0:T(4,128)} %get-tuple-element.36.own_ref), channel_id=1, source_target_pairs={{0,16},{16,0},{1,17},{17,1},{2,18},{18,2},{3,19},{19,3},{4,20},{20... | collective-permute-start | bytes 393224 | tf_op jit(solution)/shard_map/ppermute | solution.py:597
  7.2 4.8 %all-to-all-start = ((s32[16,1,32]{2,1,0:T(1,128)}), s32[16,1,32]{2,1,0:T(1,128)S(1)}, u32[]{:S(2)}, u32[]{:S(2)}) async-start(s32[16,1,32]{2,1,0:T(1,128)} %bitcast.31), calls=%async_computation | async-start | bytes 16384 | tf_op jit(solution)/shard_map/all_to_all | solution.py:594
  12.0 0.0 copy-start.2
  12.0 0.7 copy-done.2
  12.8 0.0 copy-start.11
  12.8 0.0 copy-start.5
  12.8 0.0 copy-start.12
  12.8 4.2 %top_level.1 = (f32[4,8192]{1,0:T(4,128)S(1)}, f32[4,8192]{1,0:T(4,128)S(1)}) custom-call(f32[60,60]{1,0:T(8,128)S(1)} %copy-done.2, f32[60,4,8192]{2,1,0:T(4,128)} %bitcast.21, f32[60,4,8192]{2,1,0:T(4,128)} %bitcast.22, f32[60,4,8192]{2,1,0:T(4,128)} %bitcast.23, f32[60,4,8192]{2,1,0:T(4,128)} %bitcast.24), custom_call_target="tpu_custom_call" | custom-call | flops 3932160 | bytes 7864320 | tf_op jit(solution)/shard_map/top_level/pallas_call | solution.py:205
  17.1 0.0 copy-start.10
  17.1 0.4 all-to-all-done
  17.4 0.0 collective-permute-done.other_ref
  17.4 3.4 %serve_windows.1 = f32[16,32,4,128]{3,2,1,0:T(4,128)} custom-call(s32[1]{0:T(128)} %bitcast.far_ref, s32[16,32]{1,0:T(8,128)S(1)} %bitcast.17, f32[4,8192]{1,0:T(4,128)S(1)} %copy-done.7, f32[4,8192]{1,0:T(4,128)S(1)} %collective-permute-done.other_ref), custom_call_target="tpu_custom_call" | custom-call | tf_op jit(solution)/shard_map/serve_windows/pallas_call | solution.py:613
  20.8 4.8 %all-to-all-start.1 = ((f32[16,32,4,128]{3,2,1,0:T(4,128)}), f32[16,32,4,128]{3,2,1,0:T(4,128)S(1)}, u32[]{:S(2)}, u32[]{:S(2)}) async-start(f32[16,32,4,128]{3,2,1,0:T(4,128)} %serve_windows.1), calls=%async_computation.1 | async-start | bytes 2097152 | tf_op jit(solution)/shard_map/all_to_all | solution.py:594
  25.6 0.0 copy-done
  25.6 0.0 copy-done.1
  25.6 0.0 copy-done.4
  25.6 9.3 %one_hot_and_shares.1 = (bf16[64,256,256]{2,1,0:T(8,128)(2,1)}, f32[128,4,128]{2,1,0:T(4,128)S(1)}) custom-call(s32[4,64]{1,0:T(4,128)S(1)} %copy-done.11, s32[4,8192]{1,0:T(4,128)S(1)} %copy-done, f32[4,8192]{1,0:T(4,128)S(1)} %copy-done.1, s32[1,8192]{1,0:T(1,128)S(1)} %bitcast.13), custom_call_target="tpu_custom_call" | custom-call | tf_op jit(solution)/shard_map/one_hot_and_shares/pallas_call | solution.py:630
  34.9 6.9 %all-to-all-done.1 = f32[16,32,4,128]{3,2,1,0:T(4,128)S(1)} async-done(((f32[16,32,4,128]{3,2,1,0:T(4,128)}), f32[16,32,4,128]{3,2,1,0:T(4,128)S(1)}, u32[]{:S(2)}, u32[]{:S(2)}) %all-to-all-start.1) | async-done | bytes 1048608 | tf_op jit(solution)/shard_map/all_to_all | solution.py:594
  41.8 6.3 %forcing_and_windows.1 = (f32[4,8192]{1,0:T(4,128)S(1)}, f32[16,20,4,128]{3,2,1,0:T(4,128)}, f32[16,20,4,128]{3,2,1,0:T(4,128)}) custom-call(s32[1]{0:T(128)} %bitcast.far_ref, s32[4,64]{1,0:T(4,128)S(1)} %copy-done.11, s32[4,64]{1,0:T(4,128)S(1)} %copy-done.12, f32[60,60]{1,0:T(8,128)S(1)} %copy-done.3, f32[512,4,128]{2,1,0:T(4,128)S(1)} %bitcast.12, ...), custom_call_target="tpu_custom_call" | custom-call | tf_op jit(solution)/shard_map/forcing_and_windows/pallas_call | solution.py:649
  48.1 3.6 %all-to-all-start.2 = ((f32[16,20,4,128]{3,2,1,0:T(4,128)}), f32[16,20,4,128]{3,2,1,0:T(4,128)S(1)}, u32[]{:S(2)}, u32[]{:S(2)}) async-start(f32[16,20,4,128]{3,2,1,0:T(4,128)} %get-tuple-element.46), calls=%async_computation.2 | async-start | bytes 1310720 | tf_op jit(solution)/shard_map/all_to_all | solution.py:594
  51.7 5.9 %diffuse_atmos.1 = bf16[4,72,8192]{2,1,0:T(8,128)(2,1)} custom-call(bf16[72,72]{1,0:T(8,128)(2,1)S(1)} %copy-done.10, f32[4,8192]{1,0:T(4,128)S(1)} %copy-done.6, bf16[4,72,8192]{2,1,0:T(8,128)(2,1)} %refs_3_.1, bf16[4,72,8192]{2,1,0:T(8,128)(2,1)} %refs_3_.1, bf16[4,72,8192]{2,1,0:T(8,128)(2,1)} %refs_3_.1, bf16[4,72,8192]{2,1,0:T(8,128)(2,1)} %refs_3_.1), custom_call_target="tpu_custom_call" | custom-call | flops 339738624 | bytes 9437184 | tf_op jit(solution)/shard_map/diffuse_atmos/pallas_call | solution.py:159
  57.6 6.0 %all-to-all-done.2.back_ref = f32[16,20,4,128]{3,2,1,0:T(4,128)S(1)} async-done(((f32[16,20,4,128]{3,2,1,0:T(4,128)}), f32[16,20,4,128]{3,2,1,0:T(4,128)S(1)}, u32[]{:S(2)}, u32[]{:S(2)}) %all-to-all-start.2) | async-done | bytes 655392 | tf_op jit(solution)/shard_map/all_to_all | solution.py:594
  63.6 3.6 %all-to-all-start.3 = ((f32[16,20,4,128]{3,2,1,0:T(4,128)}), f32[16,20,4,128]{3,2,1,0:T(4,128)S(1)}, u32[]{:S(2)}, u32[]{:S(2)}) async-start(f32[16,20,4,128]{3,2,1,0:T(4,128)} %get-tuple-element.52), calls=%async_computation.3 | async-start | bytes 1310720 | tf_op jit(solution)/shard_map/all_to_all | solution.py:594
  67.2 1.4 %collect_away.1 = f32[4,10240]{1,0:T(4,128)S(1)} custom-call(s32[1]{0:T(128)} %bitcast.far_ref, s32[16,32]{1,0:T(8,128)S(1)} %bitcast.18, f32[16,20,4,128]{3,2,1,0:T(4,128)S(1)} %all-to-all-done.2.back_ref), custom_call_target="tpu_custom_call" | custom-call | tf_op jit(solution)/shard_map/collect_away/pallas_call | solution.py:554
  68.6 0.0 copy-start.8
  68.6 0.0 copy-start.9
  68.6 0.4 collective-permute-start.1
  69.0 12.1 %diffuse_ocean.1 = f32[60,4,8192]{2,1,0:T(4,128)} custom-call(f32[60,60]{1,0:T(8,128)S(1)} %copy-done.3, f32[4,8192]{1,0:T(4,128)S(1)} %get-tuple-element.53.forcing_ref, s32[1,8192]{1,0:T(1,128)S(1)} %bitcast.15, f32[60,4,8192]{2,1,0:T(4,128)} %bitcast.25, f32[60,4,8192]{2,1,0:T(4,128)} %bitcast.26, f32[60,4,8192]{2,1,0:T(4,128)} %bitcast.27, ...), custom_call_target="tpu_custom_call" | custom-call | flops 2831155200 | bytes 15728640 | tf_op jit(solution)/shard_map/diffuse_ocean/pallas_call | solution.py:484
  81.2 1.5 %all-to-all-done.3.back_ref = f32[16,20,4,128]{3,2,1,0:T(4,128)S(1)} async-done(((f32[16,20,4,128]{3,2,1,0:T(4,128)}), f32[16,20,4,128]{3,2,1,0:T(4,128)S(1)}, u32[]{:S(2)}, u32[]{:S(2)}) %all-to-all-start.3) | async-done | bytes 655392 | tf_op jit(solution)/shard_map/all_to_all | solution.py:594
  82.6 0.0 collective-permute-done.1.refs_0_
  82.6 2.1 %surface_state.1 = f32[4,8192]{1,0:T(4,128)} custom-call(s32[1]{0:T(128)} %bitcast.far_ref, s32[16,32]{1,0:T(8,128)S(1)} %bitcast.19, f32[16,20,4,128]{3,2,1,0:T(4,128)S(1)} %all-to-all-done.3.back_ref, f32[4,10240]{1,0:T(4,128)S(1)} %collective-permute-done.1.refs_0_, f32[1,8192]{1,0:T(1,128)S(1)} %bitcast.20, f32[4,8192]{1,0:T(4,128)S(1)} %copy-done.8), custom_call_target="tpu_custom_call" | custom-call | tf_op jit(solution)/shard_map/surface_state/pallas_call | solution.py:554
  (15 shorter events, 0.0 us)
Async XLA Ops:
  3.1 14.3 %collective-permute-start = (f32[4,8192]{1,0:T(4,128)}, f32[4,8192]{1,0:T(4,128)S(1)}, u32[]{:S(2)}, u32[]{:S(2)}) collective-permute-start(f32[4,8192]{1,0:T(4,128)} %get-tuple-element.36.own_ref), channel_id=1, source_target_pairs={{0,16},{16,0},{1,17},{17,1},{2,18},{18,2},{3,19},{19,3},{4,20},{20... | collective-permute-start | bytes 393224 | tf_op jit(solution)/shard_map/ppermute | solution.py:597
  7.2 10.3 %all-to-all-start = ((s32[16,1,32]{2,1,0:T(1,128)}), s32[16,1,32]{2,1,0:T(1,128)S(1)}, u32[]{:S(2)}, u32[]{:S(2)}) async-start(s32[16,1,32]{2,1,0:T(1,128)} %bitcast.31), calls=%async_computation | async-start | bytes 16384 | tf_op jit(solution)/shard_map/all_to_all | solution.py:594
  12.0 0.8 copy-start.2
  12.8 4.6 %copy-start.7 = (f32[4,8192]{1,0:T(4,128)S(1)}, f32[4,8192]{1,0:T(4,128)}, u32[]{:S(2)}) copy-start(f32[4,8192]{1,0:T(4,128)} %get-tuple-element.36.own_ref) | copy-start | bytes 393220
  12.8 12.8 %copy-start = (s32[4,8192]{1,0:T(4,128)S(1)}, s32[4,8192]{1,0:T(4,128)}, u32[]{:S(2)}) copy-start(s32[4,8192]{1,0:T(4,128)} %column_ref.4) | copy-start | bytes 393220
  12.8 12.8 %copy-start.1 = (f32[4,8192]{1,0:T(4,128)S(1)}, f32[4,8192]{1,0:T(4,128)}, u32[]{:S(2)}) copy-start(f32[4,8192]{1,0:T(4,128)} %atmos_weight_ref.3) | copy-start | bytes 393220
  12.8 12.8 %copy-start.4 = (s32[8192]{0:T(1024)S(1)}, s32[8192]{0:T(1024)}, u32[]{:S(2)}) copy-start(s32[8192]{0:T(1024)} %param.23) | copy-start | bytes 98308
  12.8 12.8 %copy-start.11 = (s32[4,64]{1,0:T(4,128)S(1)}, s32[4,64]{1,0:T(4,128)}, u32[]{:S(2)}) copy-start(s32[4,64]{1,0:T(4,128)} %get-tuple-element.30.place_ref) | copy-start | bytes 3076
  12.8 29.0 %copy-start.3 = (f32[60,60]{1,0:T(8,128)S(1)}, f32[60,60]{1,0:T(8,128)}, u32[]{:S(2)}) copy-start(f32[60,60]{1,0:T(8,128)} %mix_ref.7) | copy-start | bytes 43204
  12.8 29.0 %copy-start.5 = (f32[4,8192]{1,0:T(4,128)S(1)}, f32[4,8192]{1,0:T(4,128)}, u32[]{:S(2)}) copy-start(f32[4,8192]{1,0:T(4,128)} %ocean_weight_ref.1) | copy-start | bytes 393220
  12.8 29.0 %copy-start.12 = (s32[4,64]{1,0:T(4,128)S(1)}, s32[4,64]{1,0:T(4,128)}, u32[]{:S(2)}) copy-start(s32[4,64]{1,0:T(4,128)} %get-tuple-element.31.spot_ref) | copy-start | bytes 3076
  17.1 34.6 %copy-start.6 = (f32[4,8192]{1,0:T(4,128)S(1)}, f32[4,8192]{1,0:T(4,128)}, u32[]{:S(2)}) copy-start(f32[4,8192]{1,0:T(4,128)} %get-tuple-element.49.tend_ref) | copy-start | bytes 393220
  17.1 34.6 %copy-start.10 = (bf16[72,72]{1,0:T(8,128)(2,1)S(1)}, bf16[72,72]{1,0:T(8,128)(2,1)}, u32[]{:S(2)}) copy-start(bf16[72,72]{1,0:T(8,128)(2,1)} %mix_ref.6) | copy-start | bytes 31108
  20.8 21.0 %all-to-all-start.1 = ((f32[16,32,4,128]{3,2,1,0:T(4,128)}), f32[16,32,4,128]{3,2,1,0:T(4,128)S(1)}, u32[]{:S(2)}, u32[]{:S(2)}) async-start(f32[16,32,4,128]{3,2,1,0:T(4,128)} %serve_windows.1), calls=%async_computation.1 | async-start | bytes 2097152 | tf_op jit(solution)/shard_map/all_to_all | solution.py:594
  48.1 15.5 %all-to-all-start.2 = ((f32[16,20,4,128]{3,2,1,0:T(4,128)}), f32[16,20,4,128]{3,2,1,0:T(4,128)S(1)}, u32[]{:S(2)}, u32[]{:S(2)}) async-start(f32[16,20,4,128]{3,2,1,0:T(4,128)} %get-tuple-element.46), calls=%async_computation.2 | async-start | bytes 1310720 | tf_op jit(solution)/shard_map/all_to_all | solution.py:594
  63.6 19.0 %all-to-all-start.3 = ((f32[16,20,4,128]{3,2,1,0:T(4,128)}), f32[16,20,4,128]{3,2,1,0:T(4,128)S(1)}, u32[]{:S(2)}, u32[]{:S(2)}) async-start(f32[16,20,4,128]{3,2,1,0:T(4,128)} %get-tuple-element.52), calls=%async_computation.3 | async-start | bytes 1310720 | tf_op jit(solution)/shard_map/all_to_all | solution.py:594
  68.6 14.0 %copy-start.8 = (f32[4,8192]{1,0:T(4,128)S(1)}, f32[4,8192]{1,0:T(4,128)}, u32[]{:S(2)}) copy-start(f32[4,8192]{1,0:T(4,128)} %refs_2_.3) | copy-start | bytes 393220
  68.6 14.0 %copy-start.9 = (f32[8192]{0:T(1024)S(1)}, f32[8192]{0:T(1024)}, u32[]{:S(2)}) copy-start(f32[8192]{0:T(1024)} %param.19) | copy-start | bytes 98308
  68.6 14.0 %collective-permute-start.1 = (f32[4,10240]{1,0:T(4,128)S(1)}, f32[4,10240]{1,0:T(4,128)S(1)}, u32[]{:S(2)}, u32[]{:S(2)}) collective-permute-start(f32[4,10240]{1,0:T(4,128)S(1)} %collect_away.1), channel_id=1, source_target_pairs={{0,16},{16,0},{1,17},{17,1},{2,18},{18,2},{3,19},{19,3},{4,20},{20... | collective-permute-start | bytes 491528 | tf_op jit(solution)/shard_map/ppermute | solution.py:597

commit v5 on v4

--- a/solution.py
+++ b/solution.py
@@ -219,33 +219,47 @@
 
 
 def serve_kernel(
-    per_owner, far_ref, asked_ref, own_ref, other_ref, out_ref, blocks_ref, arrived_sem
+    per_owner,
+    far_ref,
+    asked_ref,
+    own_ref,
+    other_ref,
+    out_ref,
+    blocks_ref,
+    filled_ref,
+    arrived_sem,
+    sent_sem,
 ):
-    @pl.when(pl.program_id(0) == 0)
-    def _():
-        copies = [
-            pltpu.make_async_copy(ref, blocks_ref.at[index], arrived_sem.at[index])
-            for index, ref in enumerate((own_ref, other_ref))
-        ]
-        for copy in copies:
-            copy.start()
-        for copy in copies:
-            copy.wait()
-
+    copies = [
+        pltpu.make_async_copy(ref, blocks_ref.at[index], arrived_sem.at[index])
+        for index, ref in enumerate((own_ref, other_ref))
+    ]
+    for copy in copies:
+        copy.start()
+    for copy in copies:
+        copy.wait()
     far = far_ref[0]
-    peers = out_ref.shape[0]
-    first = pl.program_id(0) * peers
 
     def body(peer, carry):
         for shard in range(2):
             for slot in range(per_owner):
                 spot = shard * per_owner + slot
-                out_ref[peer, spot] = blocks_ref[
-                    shard ^ far, :, window(asked_ref[first + peer, spot])
+                filled_ref[peer, spot] = blocks_ref[
+                    shard ^ far, :, window(asked_ref[peer, spot])
                 ]
         return carry
 
-    lax.fori_loop(0, peers, body, 0)
+    sends = []
+    parts = sent_sem.shape[0]
+    peers = filled_ref.shape[0] // parts
+    for part in range(parts):
+        lax.fori_loop(part * peers, (part + 1) * peers, body, 0)
+        at = pl.ds(part * peers, peers)
+        send = pltpu.make_async_copy(filled_ref.at[at], out_ref.at[at], sent_sem.at[part])
+        send.start()
+        sends.append(send)
+    for send in sends:
+        send.wait()
 
 
 def split_high(values):
@@ -370,7 +384,9 @@
         part = pl.ds(group * GROUP, GROUP)
         return pltpu.make_async_copy(hot_ref.at[part], held_ref.at[part], held_sem.at[group])
 
-    for group in range(windows // GROUP):
+    groups = windows // GROUP
+    ahead = min(3, groups)
+    for group in range(ahead):
         fetch(group).start()
     value_ref[...] = jnp.zeros(value_ref.shape, jnp.float32)
     corner = mix_ref[0, 0]
@@ -378,6 +394,11 @@
 
     def body(group, carry):
         fetch(group).wait()
+
+        @pl.when(group + ahead < groups)
+        def _():
+            fetch(group + ahead).start()
+
         for inner in range(GROUP):
             step = group * GROUP + inner
             here = window(step)
@@ -612,13 +633,14 @@
     asked, base, first_level = lax.optimization_barrier((asked, base, first_level))
     served = pl.pallas_call(
         functools.partial(serve_kernel, per_owner),
-        grid=(4,),
         in_specs=[smem, smem, hbm, hbm],
-        out_specs=pl.BlockSpec((near // 4, spots, fields, LANES), lambda i: (i, 0, 0, 0)),
+        out_specs=hbm,
         out_shape=jax.ShapeDtypeStruct((near, spots, fields, LANES), jnp.float32),
         scratch_shapes=[
             pltpu.VMEM((2, fields, columns), jnp.float32),
+            pltpu.VMEM((near, spots, fields, LANES), jnp.float32),
             pltpu.SemaphoreType.DMA((2,)),
+            pltpu.SemaphoreType.DMA((4,)),
         ],
         compiler_params=params,
         name="serve_windows",

time: 85.6 us -> 85.8 us (level)
  no operation moved by 1% of the time
where the time goes in v5:
time: 85.8 us; the launch traced here: 85 us
  Pallas kernels  47.3 us (55%)
  starting transfers between devices  21.3 us (25%)
  waiting for transfers between devices  14.8 us (17%)
    all_to_all x4, starting transfers between devices, to_near(): lax.all_to_all(values, ('near', 'sub'), split_axis=0, concat_axis=0, tile...  16.8 us
    all_to_all x4, waiting for transfers between devices, to_near(): lax.all_to_all(values, ('near', 'sub'), split_axis=0, concat_axis=0, tile...  14.8 us
    pallas_call x1, Pallas kernels, diffuse_ocean(): pl.pallas_call(ocean_kernel, grid=(cells // block,), in_specs=[pl.BlockSp...  12.1 us
    pallas_call x1, Pallas kernels, per_device(): pl.pallas_call(hot_kernel, grid=(windows // GROUP,), in_specs=[smem] + [v...  9.25 us
    pallas_call x1, Pallas kernels, per_device(): pl.pallas_call(middle_kernel, in_specs=[smem] * 4 + [vmem] * 7 + [hbm, vm...  7.02 us
    pallas_call x1, Pallas kernels, diffuse_atmos(): pl.pallas_call(atmos_kernel, grid=(columns // block,), in_specs=[pl.Block...  5.85 us
    ppermute x2, starting transfers between devices, to_far(): return lax.ppermute(values, 'far', ((0, 1), (1, 0)))  4.49 us
    pallas_call x1, Pallas kernels, top_level(): pl.pallas_call(top_kernel, grid=(cells // block,), in_specs=[smem] + spec...  4.2 us
  transfers between devices with their start and end apart: 6, of which 4 were waited for; matrix products, arithmetic and copies ran while one was open for 0% of the time, Pallas kernels for 39%

profile of v5, /device:TPU:0, one launch (start us, length us, event | category | flops | bytes accessed | tf_op | source)
XLA Modules:
  0.0 85.0 jit_solution(18251602057828938541)
XLA Ops:
  0.6 2.5 %requests_and_rates.1 = (s32[4,64]{1,0:T(4,128)}, s32[4,64]{1,0:T(4,128)}, s32[16,32]{1,0:T(8,128)}, f32[4,8192]{1,0:T(4,128)}, f32[4,8192]{1,0:T(4,128)}) custom-call(s32[4,8192]{1,0:T(4,128)} %slot_ref.1, s32[4,8192]{1,0:T(4,128)} %column_ref.4, bf16[4,72,8192]{2,1,0:T(8,128)(2,1)} %refs_3_.1, f32[1,8192]{1,0:T(1,128)} %bitcast.30, f32[4,8192]{1,0:T(4,128)} %before_ref.1, ...), custom_call_target="tpu_custom_call" | custom-call | tf_op jit(solution)/shard_map/requests_and_rates/pallas_call | solution.py:119
  3.1 4.1 %collective-permute-start = (f32[4,8192]{1,0:T(4,128)}, f32[4,8192]{1,0:T(4,128)S(1)}, u32[]{:S(2)}, u32[]{:S(2)}) collective-permute-start(f32[4,8192]{1,0:T(4,128)} %get-tuple-element.36.own_ref), channel_id=1, source_target_pairs={{0,16},{16,0},{1,17},{17,1},{2,18},{18,2},{3,19},{19,3},{4,20},{20... | collective-permute-start | bytes 393224 | tf_op jit(solution)/shard_map/ppermute | solution.py:618
  7.2 4.8 %all-to-all-start = ((s32[16,1,32]{2,1,0:T(1,128)}), s32[16,1,32]{2,1,0:T(1,128)S(1)}, u32[]{:S(2)}, u32[]{:S(2)}) async-start(s32[16,1,32]{2,1,0:T(1,128)} %bitcast.31), calls=%async_computation | async-start | bytes 16384 | tf_op jit(solution)/shard_map/all_to_all | solution.py:615
  12.0 0.0 copy-start.2
  12.0 0.7 copy-done.2
  12.8 0.0 copy-start.11
  12.8 0.0 copy-start.3
  12.8 0.0 copy-start.5
  12.8 0.0 copy-start.12
  12.8 4.2 %top_level.1 = (f32[4,8192]{1,0:T(4,128)S(1)}, f32[4,8192]{1,0:T(4,128)S(1)}) custom-call(f32[60,60]{1,0:T(8,128)S(1)} %copy-done.2, f32[60,4,8192]{2,1,0:T(4,128)} %bitcast.21, f32[60,4,8192]{2,1,0:T(4,128)} %bitcast.22, f32[60,4,8192]{2,1,0:T(4,128)} %bitcast.23, f32[60,4,8192]{2,1,0:T(4,128)} %bitcast.24), custom_call_target="tpu_custom_call" | custom-call | flops 3932160 | bytes 7864320 | tf_op jit(solution)/shard_map/top_level/pallas_call | solution.py:205
  17.1 0.0 copy-start.6
  17.1 0.0 copy-start.10
  17.1 0.4 all-to-all-done
  17.4 0.0 collective-permute-done.other_ref
  17.4 2.8 %serve_windows.1 = f32[16,32,4,128]{3,2,1,0:T(4,128)} custom-call(s32[1]{0:T(128)} %bitcast.far_ref, s32[16,32]{1,0:T(8,128)S(1)} %bitcast.17, f32[4,8192]{1,0:T(4,128)S(1)} %copy-done.7, f32[4,8192]{1,0:T(4,128)S(1)} %collective-permute-done.other_ref), custom_call_target="tpu_custom_call" | custom-call | tf_op jit(solution)/shard_map/serve_windows/pallas_call | solution.py:634
  20.2 4.8 %all-to-all-start.1 = ((f32[16,32,4,128]{3,2,1,0:T(4,128)}), f32[16,32,4,128]{3,2,1,0:T(4,128)S(1)}, u32[]{:S(2)}, u32[]{:S(2)}) async-start(f32[16,32,4,128]{3,2,1,0:T(4,128)} %serve_windows.1), calls=%async_computation.1 | async-start | bytes 2097152 | tf_op jit(solution)/shard_map/all_to_all | solution.py:615
  25.1 9.3 %one_hot_and_shares.1 = (bf16[64,256,256]{2,1,0:T(8,128)(2,1)}, f32[128,4,128]{2,1,0:T(4,128)S(1)}) custom-call(s32[4,64]{1,0:T(4,128)S(1)} %copy-done.11, s32[4,8192]{1,0:T(4,128)S(1)} %copy-done, f32[4,8192]{1,0:T(4,128)S(1)} %copy-done.1, s32[1,8192]{1,0:T(1,128)S(1)} %bitcast.13), custom_call_target="tpu_custom_call" | custom-call | tf_op jit(solution)/shard_map/one_hot_and_shares/pallas_call | solution.py:652
  34.3 6.9 %all-to-all-done.1 = f32[16,32,4,128]{3,2,1,0:T(4,128)S(1)} async-done(((f32[16,32,4,128]{3,2,1,0:T(4,128)}), f32[16,32,4,128]{3,2,1,0:T(4,128)S(1)}, u32[]{:S(2)}, u32[]{:S(2)}) %all-to-all-start.1) | async-done | bytes 1048608 | tf_op jit(solution)/shard_map/all_to_all | solution.py:615
  41.2 0.0 copy-done.3
  41.2 7.0 %forcing_and_windows.1 = (f32[4,8192]{1,0:T(4,128)S(1)}, f32[16,20,4,128]{3,2,1,0:T(4,128)}, f32[16,20,4,128]{3,2,1,0:T(4,128)}) custom-call(s32[1]{0:T(128)} %bitcast.far_ref, s32[4,64]{1,0:T(4,128)S(1)} %copy-done.11, s32[4,64]{1,0:T(4,128)S(1)} %copy-done.12, f32[60,60]{1,0:T(8,128)S(1)} %copy-done.3, f32[512,4,128]{2,1,0:T(4,128)S(1)} %bitcast.12, ...), custom_call_target="tpu_custom_call" | custom-call | tf_op jit(solution)/shard_map/forcing_and_windows/pallas_call | solution.py:671
  48.3 3.6 %all-to-all-start.2 = ((f32[16,20,4,128]{3,2,1,0:T(4,128)}), f32[16,20,4,128]{3,2,1,0:T(4,128)S(1)}, u32[]{:S(2)}, u32[]{:S(2)}) async-start(f32[16,20,4,128]{3,2,1,0:T(4,128)} %get-tuple-element.46), calls=%async_computation.2 | async-start | bytes 1310720 | tf_op jit(solution)/shard_map/all_to_all | solution.py:615
  51.9 5.8 %diffuse_atmos.1 = bf16[4,72,8192]{2,1,0:T(8,128)(2,1)} custom-call(bf16[72,72]{1,0:T(8,128)(2,1)S(1)} %copy-done.10, f32[4,8192]{1,0:T(4,128)S(1)} %copy-done.6, bf16[4,72,8192]{2,1,0:T(8,128)(2,1)} %refs_3_.1, bf16[4,72,8192]{2,1,0:T(8,128)(2,1)} %refs_3_.1, bf16[4,72,8192]{2,1,0:T(8,128)(2,1)} %refs_3_.1, bf16[4,72,8192]{2,1,0:T(8,128)(2,1)} %refs_3_.1), custom_call_target="tpu_custom_call" | custom-call | flops 339738624 | bytes 9437184 | tf_op jit(solution)/shard_map/diffuse_atmos/pallas_call | solution.py:159
  57.7 6.0 %all-to-all-done.2.back_ref = f32[16,20,4,128]{3,2,1,0:T(4,128)S(1)} async-done(((f32[16,20,4,128]{3,2,1,0:T(4,128)}), f32[16,20,4,128]{3,2,1,0:T(4,128)S(1)}, u32[]{:S(2)}, u32[]{:S(2)}) %all-to-all-start.2) | async-done | bytes 655392 | tf_op jit(solution)/shard_map/all_to_all | solution.py:615
  63.8 3.6 %all-to-all-start.3 = ((f32[16,20,4,128]{3,2,1,0:T(4,128)}), f32[16,20,4,128]{3,2,1,0:T(4,128)S(1)}, u32[]{:S(2)}, u32[]{:S(2)}) async-start(f32[16,20,4,128]{3,2,1,0:T(4,128)} %get-tuple-element.52), calls=%async_computation.3 | async-start | bytes 1310720 | tf_op jit(solution)/shard_map/all_to_all | solution.py:615
  67.4 1.4 %collect_away.1 = f32[4,10240]{1,0:T(4,128)S(1)} custom-call(s32[1]{0:T(128)} %bitcast.far_ref, s32[16,32]{1,0:T(8,128)S(1)} %bitcast.18, f32[16,20,4,128]{3,2,1,0:T(4,128)S(1)} %all-to-all-done.2.back_ref), custom_call_target="tpu_custom_call" | custom-call | tf_op jit(solution)/shard_map/collect_away/pallas_call | solution.py:575
  68.8 0.0 copy-start.8
  68.8 0.0 copy-start.9
  68.8 0.4 collective-permute-start.1
  69.2 12.1 %diffuse_ocean.1 = f32[60,4,8192]{2,1,0:T(4,128)} custom-call(f32[60,60]{1,0:T(8,128)S(1)} %copy-done.3, f32[4,8192]{1,0:T(4,128)S(1)} %get-tuple-element.53.forcing_ref, s32[1,8192]{1,0:T(1,128)S(1)} %bitcast.15, f32[60,4,8192]{2,1,0:T(4,128)} %bitcast.25, f32[60,4,8192]{2,1,0:T(4,128)} %bitcast.26, f32[60,4,8192]{2,1,0:T(4,128)} %bitcast.27, ...), custom_call_target="tpu_custom_call" | custom-call | flops 2831155200 | bytes 15728640 | tf_op jit(solution)/shard_map/diffuse_ocean/pallas_call | solution.py:505
  81.4 1.5 %all-to-all-done.3.back_ref = f32[16,20,4,128]{3,2,1,0:T(4,128)S(1)} async-done(((f32[16,20,4,128]{3,2,1,0:T(4,128)}), f32[16,20,4,128]{3,2,1,0:T(4,128)S(1)}, u32[]{:S(2)}, u32[]{:S(2)}) %all-to-all-start.3) | async-done | bytes 655392 | tf_op jit(solution)/shard_map/all_to_all | solution.py:615
  82.8 0.0 collective-permute-done.1.refs_0_
  82.8 2.1 %surface_state.1 = f32[4,8192]{1,0:T(4,128)} custom-call(s32[1]{0:T(128)} %bitcast.far_ref, s32[16,32]{1,0:T(8,128)S(1)} %bitcast.19, f32[16,20,4,128]{3,2,1,0:T(4,128)S(1)} %all-to-all-done.3.back_ref, f32[4,10240]{1,0:T(4,128)S(1)} %collective-permute-done.1.refs_0_, f32[1,8192]{1,0:T(1,128)S(1)} %bitcast.20, f32[4,8192]{1,0:T(4,128)S(1)} %copy-done.8), custom_call_target="tpu_custom_call" | custom-call | tf_op jit(solution)/shard_map/surface_state/pallas_call | solution.py:575
  (15 shorter events, 0.0 us)
Async XLA Ops:
  3.1 14.3 %collective-permute-start = (f32[4,8192]{1,0:T(4,128)}, f32[4,8192]{1,0:T(4,128)S(1)}, u32[]{:S(2)}, u32[]{:S(2)}) collective-permute-start(f32[4,8192]{1,0:T(4,128)} %get-tuple-element.36.own_ref), channel_id=1, source_target_pairs={{0,16},{16,0},{1,17},{17,1},{2,18},{18,2},{3,19},{19,3},{4,20},{20... | collective-permute-start | bytes 393224 | tf_op jit(solution)/shard_map/ppermute | solution.py:618
  7.2 10.3 %all-to-all-start = ((s32[16,1,32]{2,1,0:T(1,128)}), s32[16,1,32]{2,1,0:T(1,128)S(1)}, u32[]{:S(2)}, u32[]{:S(2)}) async-start(s32[16,1,32]{2,1,0:T(1,128)} %bitcast.31), calls=%async_computation | async-start | bytes 16384 | tf_op jit(solution)/shard_map/all_to_all | solution.py:615
  12.0 0.8 copy-start.2
  12.8 4.6 %copy-start.7 = (f32[4,8192]{1,0:T(4,128)S(1)}, f32[4,8192]{1,0:T(4,128)}, u32[]{:S(2)}) copy-start(f32[4,8192]{1,0:T(4,128)} %get-tuple-element.36.own_ref) | copy-start | bytes 393220
  12.8 12.2 %copy-start = (s32[4,8192]{1,0:T(4,128)S(1)}, s32[4,8192]{1,0:T(4,128)}, u32[]{:S(2)}) copy-start(s32[4,8192]{1,0:T(4,128)} %column_ref.4) | copy-start | bytes 393220
  12.8 12.3 %copy-start.1 = (f32[4,8192]{1,0:T(4,128)S(1)}, f32[4,8192]{1,0:T(4,128)}, u32[]{:S(2)}) copy-start(f32[4,8192]{1,0:T(4,128)} %atmos_weight_ref.3) | copy-start | bytes 393220
  12.8 12.3 %copy-start.4 = (s32[8192]{0:T(1024)S(1)}, s32[8192]{0:T(1024)}, u32[]{:S(2)}) copy-start(s32[8192]{0:T(1024)} %param.23) | copy-start | bytes 98308
  12.8 12.3 %copy-start.11 = (s32[4,64]{1,0:T(4,128)S(1)}, s32[4,64]{1,0:T(4,128)}, u32[]{:S(2)}) copy-start(s32[4,64]{1,0:T(4,128)} %get-tuple-element.30.place_ref) | copy-start | bytes 3076
  12.8 28.4 %copy-start.3 = (f32[60,60]{1,0:T(8,128)S(1)}, f32[60,60]{1,0:T(8,128)}, u32[]{:S(2)}) copy-start(f32[60,60]{1,0:T(8,128)} %mix_ref.7) | copy-start | bytes 43204
  12.8 28.4 %copy-start.5 = (f32[4,8192]{1,0:T(4,128)S(1)}, f32[4,8192]{1,0:T(4,128)}, u32[]{:S(2)}) copy-start(f32[4,8192]{1,0:T(4,128)} %ocean_weight_ref.1) | copy-start | bytes 393220
  12.8 28.4 %copy-start.12 = (s32[4,64]{1,0:T(4,128)S(1)}, s32[4,64]{1,0:T(4,128)}, u32[]{:S(2)}) copy-start(s32[4,64]{1,0:T(4,128)} %get-tuple-element.31.spot_ref) | copy-start | bytes 3076
  17.1 34.8 %copy-start.6 = (f32[4,8192]{1,0:T(4,128)S(1)}, f32[4,8192]{1,0:T(4,128)}, u32[]{:S(2)}) copy-start(f32[4,8192]{1,0:T(4,128)} %get-tuple-element.49.tend_ref) | copy-start | bytes 393220
  17.1 34.8 %copy-start.10 = (bf16[72,72]{1,0:T(8,128)(2,1)S(1)}, bf16[72,72]{1,0:T(8,128)(2,1)}, u32[]{:S(2)}) copy-start(bf16[72,72]{1,0:T(8,128)(2,1)} %mix_ref.6) | copy-start | bytes 31108
  20.2 21.0 %all-to-all-start.1 = ((f32[16,32,4,128]{3,2,1,0:T(4,128)}), f32[16,32,4,128]{3,2,1,0:T(4,128)S(1)}, u32[]{:S(2)}, u32[]{:S(2)}) async-start(f32[16,32,4,128]{3,2,1,0:T(4,128)} %serve_windows.1), calls=%async_computation.1 | async-start | bytes 2097152 | tf_op jit(solution)/shard_map/all_to_all | solution.py:615
  48.3 15.5 %all-to-all-start.2 = ((f32[16,20,4,128]{3,2,1,0:T(4,128)}), f32[16,20,4,128]{3,2,1,0:T(4,128)S(1)}, u32[]{:S(2)}, u32[]{:S(2)}) async-start(f32[16,20,4,128]{3,2,1,0:T(4,128)} %get-tuple-element.46), calls=%async_computation.2 | async-start | bytes 1310720 | tf_op jit(solution)/shard_map/all_to_all | solution.py:615
  63.8 19.0 %all-to-all-start.3 = ((f32[16,20,4,128]{3,2,1,0:T(4,128)}), f32[16,20,4,128]{3,2,1,0:T(4,128)S(1)}, u32[]{:S(2)}, u32[]{:S(2)}) async-start(f32[16,20,4,128]{3,2,1,0:T(4,128)} %get-tuple-element.52), calls=%async_computation.3 | async-start | bytes 1310720 | tf_op jit(solution)/shard_map/all_to_all | solution.py:615
  68.8 14.0 %copy-start.8 = (f32[4,8192]{1,0:T(4,128)S(1)}, f32[4,8192]{1,0:T(4,128)}, u32[]{:S(2)}) copy-start(f32[4,8192]{1,0:T(4,128)} %refs_2_.3) | copy-start | bytes 393220
  68.8 14.0 %copy-start.9 = (f32[8192]{0:T(1024)S(1)}, f32[8192]{0:T(1024)}, u32[]{:S(2)}) copy-start(f32[8192]{0:T(1024)} %param.19) | copy-start | bytes 98308
  68.8 14.0 %collective-permute-start.1 = (f32[4,10240]{1,0:T(4,128)S(1)}, f32[4,10240]{1,0:T(4,128)S(1)}, u32[]{:S(2)}, u32[]{:S(2)}) collective-permute-start(f32[4,10240]{1,0:T(4,128)S(1)} %collect_away.1), channel_id=1, source_target_pairs={{0,16},{16,0},{1,17},{17,1},{2,18},{18,2},{3,19},{19,3},{4,20},{20... | collective-permute-start | bytes 491528 | tf_op jit(solution)/shard_map/ppermute | solution.py:618

commit v6 on v5

--- a/solution.py
+++ b/solution.py
@@ -369,6 +369,7 @@
     away_ref,
     home_ref,
     value_ref,
+    parts_ref,
     held_ref,
     held_sem,
     sent_sem,
@@ -385,20 +386,13 @@
         return pltpu.make_async_copy(hot_ref.at[part], held_ref.at[part], held_sem.at[group])
 
     groups = windows // GROUP
-    ahead = min(3, groups)
-    for group in range(ahead):
+    for group in range(groups):
         fetch(group).start()
     value_ref[...] = jnp.zeros(value_ref.shape, jnp.float32)
     corner = mix_ref[0, 0]
     blank = jnp.zeros((2 * fields, LANES), jnp.float32)
 
     def body(group, carry):
-        fetch(group).wait()
-
-        @pl.when(group + ahead < groups)
-        def _():
-            fetch(group + ahead).start()
-
         for inner in range(GROUP):
             step = group * GROUP + inner
             here = window(step)
@@ -428,7 +422,18 @@
             parts = jnp.concatenate(
                 [jnp.concatenate(left, axis=0), jnp.concatenate(right, axis=0)], axis=1
             ).astype(jnp.bfloat16)
-            spread = jnp.dot(parts, held_ref[step], preferred_element_type=jnp.float32)
+            parts_ref[step] = parts
+        return carry
+
+    lax.fori_loop(0, groups, body, 0)
+
+    def multiply(group, carry):
+        fetch(group).wait()
+        for inner in range(GROUP):
+            step = group * GROUP + inner
+            spread = jnp.dot(
+                parts_ref[step], held_ref[step], preferred_element_type=jnp.float32
+            )
             for k in range(intersections):
                 side = slice((k % 2) * LANES, (k % 2 + 1) * LANES)
                 at = 2 * fields * k
@@ -437,7 +442,7 @@
                 )
         return carry
 
-    lax.fori_loop(0, windows // GROUP, body, 0)
+    lax.fori_loop(0, groups, multiply, 0)
     far = far_ref[0]
     shards = value_ref.reshape(2, near, per_owner, fields, LANES)
     copies = []
@@ -679,6 +684,7 @@
         ],
         scratch_shapes=[
             pltpu.VMEM((near * spots, fields, LANES), jnp.float32),
+            pltpu.VMEM((windows, 2 * fields * intersections, 2 * LANES), jnp.bfloat16),
             pltpu.VMEM((windows, 2 * LANES, 2 * LANES), jnp.bfloat16),
             pltpu.SemaphoreType.DMA((windows // GROUP,)),
             pltpu.SemaphoreType.DMA((4,)),
@@ -700,16 +706,16 @@
         hot,
         shares.reshape(2, near, rows, fields, LANES),
     )
-    tendency, forcing = lax.optimization_barrier((tendency, forcing))
-    atmos_updated = diffuse_atmos(atmos_profiles, atmos_mixing, tendency)
-    back_away, atmos_updated, home = lax.optimization_barrier(
-        (to_near(away), atmos_updated, home)
+    ocean_updated = diffuse_ocean(state, ocean_mixing, forcing, mask).transpose(1, 0, 2)
+    back_away, ocean_updated, home = lax.optimization_barrier(
+        (to_near(away), ocean_updated, home)
     )
     back_home = to_near(home)
     sums_away = collect(asked, far, back_away, per_owner, columns, ())
+    tendency, sums_away = lax.optimization_barrier((tendency, sums_away))
     other_sums = to_far(sums_away)
-    ocean_updated = diffuse_ocean(state, ocean_mixing, forcing, mask).transpose(1, 0, 2)
-    back_home, ocean_updated = lax.optimization_barrier((back_home, ocean_updated))
+    atmos_updated = diffuse_atmos(atmos_profiles, atmos_mixing, tendency)
+    back_home, atmos_updated = lax.optimization_barrier((back_home, atmos_updated))
     surface_state = collect(
         asked,
         far,

time: 85.8 us -> 86.7 us (1.010)
  starting transfers between devices: 21.3 us -> 22.8 us
    all_to_all x4, starting transfers between devices: 16.8 us -> 18.3 us  [to_near(): lax.all_to_all(values, ('near', 'sub'), split_axis=0, concat_axis=0, tile...]
  transfers between devices with their start and end apart: 6 -> 6, of which waited for: 4 -> 3; matrix products, arithmetic and copies ran while one was open for 0% -> 0% of each run, Pallas kernels for 39% -> 38%
where the time goes in v6:
time: 86.7 us; the launch traced here: 85.9 us
  Pallas kernels  46.5 us (54%)
  starting transfers between devices  22.8 us (26%)
  waiting for transfers between devices  15 us (17%)
    all_to_all x4, starting transfers between devices, to_near(): lax.all_to_all(values, ('near', 'sub'), split_axis=0, concat_axis=0, tile...  18.3 us
    all_to_all x4, waiting for transfers between devices, to_near(): lax.all_to_all(values, ('near', 'sub'), split_axis=0, concat_axis=0, tile...  15 us
    pallas_call x1, Pallas kernels, diffuse_ocean(): pl.pallas_call(ocean_kernel, grid=(cells // block,), in_specs=[pl.BlockSp...  12.2 us
    pallas_call x1, Pallas kernels, per_device(): pl.pallas_call(hot_kernel, grid=(windows // GROUP,), in_specs=[smem] + [v...  9.25 us
    pallas_call x1, Pallas kernels, per_device(): pl.pallas_call(middle_kernel, in_specs=[smem] * 4 + [vmem] * 7 + [hbm, vm...  6.2 us
    pallas_call x1, Pallas kernels, diffuse_atmos(): pl.pallas_call(atmos_kernel, grid=(columns // block,), in_specs=[pl.Block...  5.85 us
    ppermute x2, starting transfers between devices, to_far(): return lax.ppermute(values, 'far', ((0, 1), (1, 0)))  4.48 us
    pallas_call x1, Pallas kernels, top_level(): pl.pallas_call(top_kernel, grid=(cells // block,), in_specs=[smem] + spec...  4.2 us
  transfers between devices with their start and end apart: 6, of which 3 were waited for; matrix products, arithmetic and copies ran while one was open for 0% of the time, Pallas kernels for 38%

profile of v6, /device:TPU:0, one launch (start us, length us, event | category | flops | bytes accessed | tf_op | source)
XLA Modules:
  0.0 85.9 jit_solution(14167237939937217749)
XLA Ops:
  0.6 2.5 %requests_and_rates.1 = (s32[4,64]{1,0:T(4,128)}, s32[4,64]{1,0:T(4,128)}, s32[16,32]{1,0:T(8,128)}, f32[4,8192]{1,0:T(4,128)}, f32[4,8192]{1,0:T(4,128)}) custom-call(s32[4,8192]{1,0:T(4,128)} %slot_ref.1, s32[4,8192]{1,0:T(4,128)} %column_ref.4, bf16[4,72,8192]{2,1,0:T(8,128)(2,1)} %refs_3_.1, f32[1,8192]{1,0:T(1,128)} %bitcast.30, f32[4,8192]{1,0:T(4,128)} %before_ref.1, ...), custom_call_target="tpu_custom_call" | custom-call | tf_op jit(solution)/shard_map/requests_and_rates/pallas_call | solution.py:119
  3.1 4.1 %collective-permute-start = (f32[4,8192]{1,0:T(4,128)}, f32[4,8192]{1,0:T(4,128)S(1)}, u32[]{:S(2)}, u32[]{:S(2)}) collective-permute-start(f32[4,8192]{1,0:T(4,128)} %get-tuple-element.36.own_ref), channel_id=1, source_target_pairs={{0,16},{16,0},{1,17},{17,1},{2,18},{18,2},{3,19},{19,3},{4,20},{20... | collective-permute-start | bytes 393224 | tf_op jit(solution)/shard_map/ppermute | solution.py:623
  7.2 4.8 %all-to-all-start = ((s32[16,1,32]{2,1,0:T(1,128)}), s32[16,1,32]{2,1,0:T(1,128)S(1)}, u32[]{:S(2)}, u32[]{:S(2)}) async-start(s32[16,1,32]{2,1,0:T(1,128)} %bitcast.31), calls=%async_computation | async-start | bytes 16384 | tf_op jit(solution)/shard_map/all_to_all | solution.py:620
  12.0 0.0 copy-start.2
  12.0 0.7 copy-done.2
  12.8 0.0 copy-start.11
  12.8 0.0 copy-start.3
  12.8 0.0 copy-start.5
  12.8 4.2 %top_level.1 = (f32[4,8192]{1,0:T(4,128)S(1)}, f32[4,8192]{1,0:T(4,128)S(1)}) custom-call(f32[60,60]{1,0:T(8,128)S(1)} %copy-done.2, f32[60,4,8192]{2,1,0:T(4,128)} %bitcast.21, f32[60,4,8192]{2,1,0:T(4,128)} %bitcast.22, f32[60,4,8192]{2,1,0:T(4,128)} %bitcast.23, f32[60,4,8192]{2,1,0:T(4,128)} %bitcast.24), custom_call_target="tpu_custom_call" | custom-call | flops 3932160 | bytes 7864320 | tf_op jit(solution)/shard_map/top_level/pallas_call | solution.py:205
  17.1 0.4 all-to-all-done
  17.4 0.0 collective-permute-done.other_ref
  17.4 0.0 copy-done.7
  17.4 2.8 %serve_windows.1 = f32[16,32,4,128]{3,2,1,0:T(4,128)} custom-call(s32[1]{0:T(128)} %bitcast.far_ref, s32[16,32]{1,0:T(8,128)S(1)} %bitcast.17, f32[4,8192]{1,0:T(4,128)S(1)} %copy-done.7, f32[4,8192]{1,0:T(4,128)S(1)} %collective-permute-done.other_ref), custom_call_target="tpu_custom_call" | custom-call | tf_op jit(solution)/shard_map/serve_windows/pallas_call | solution.py:639
  20.2 4.8 %all-to-all-start.1 = ((f32[16,32,4,128]{3,2,1,0:T(4,128)}), f32[16,32,4,128]{3,2,1,0:T(4,128)S(1)}, u32[]{:S(2)}, u32[]{:S(2)}) async-start(f32[16,32,4,128]{3,2,1,0:T(4,128)} %serve_windows.1), calls=%async_computation.1 | async-start | bytes 2097152 | tf_op jit(solution)/shard_map/all_to_all | solution.py:620
  25.1 9.3 %one_hot_and_shares.1 = (bf16[64,256,256]{2,1,0:T(8,128)(2,1)}, f32[128,4,128]{2,1,0:T(4,128)S(1)}) custom-call(s32[4,64]{1,0:T(4,128)S(1)} %copy-done.11, s32[4,8192]{1,0:T(4,128)S(1)} %copy-done, f32[4,8192]{1,0:T(4,128)S(1)} %copy-done.1, s32[1,8192]{1,0:T(1,128)S(1)} %bitcast.13), custom_call_target="tpu_custom_call" | custom-call | tf_op jit(solution)/shard_map/one_hot_and_shares/pallas_call | solution.py:657
  34.3 6.9 %all-to-all-done.1 = f32[16,32,4,128]{3,2,1,0:T(4,128)S(1)} async-done(((f32[16,32,4,128]{3,2,1,0:T(4,128)}), f32[16,32,4,128]{3,2,1,0:T(4,128)S(1)}, u32[]{:S(2)}, u32[]{:S(2)}) %all-to-all-start.1) | async-done | bytes 1048608 | tf_op jit(solution)/shard_map/all_to_all | solution.py:620
  41.2 0.0 copy-done.3
  41.2 6.2 %forcing_and_windows.1 = (f32[4,8192]{1,0:T(4,128)S(1)}, f32[16,20,4,128]{3,2,1,0:T(4,128)}, f32[16,20,4,128]{3,2,1,0:T(4,128)}) custom-call(s32[1]{0:T(128)} %bitcast.far_ref, s32[4,64]{1,0:T(4,128)S(1)} %copy-done.11, s32[4,64]{1,0:T(4,128)S(1)} %copy-done.12, f32[60,60]{1,0:T(8,128)S(1)} %copy-done.3, f32[512,4,128]{2,1,0:T(4,128)S(1)} %bitcast.12, ...), custom_call_target="tpu_custom_call" | custom-call | tf_op jit(solution)/shard_map/forcing_and_windows/pallas_call | solution.py:676
  47.4 3.6 %all-to-all-start.2 = ((f32[16,20,4,128]{3,2,1,0:T(4,128)}), f32[16,20,4,128]{3,2,1,0:T(4,128)S(1)}, u32[]{:S(2)}, u32[]{:S(2)}) async-start(f32[16,20,4,128]{3,2,1,0:T(4,128)} %get-tuple-element.46), calls=%async_computation.2 | async-start | bytes 1310720 | tf_op jit(solution)/shard_map/all_to_all | solution.py:620
  51.0 0.0 copy-start.10
  51.1 12.2 %diffuse_ocean.1 = f32[60,4,8192]{2,1,0:T(4,128)} custom-call(f32[60,60]{1,0:T(8,128)S(1)} %copy-done.3, f32[4,8192]{1,0:T(4,128)S(1)} %get-tuple-element.47.forcing_ref, s32[1,8192]{1,0:T(1,128)S(1)} %bitcast.15, f32[60,4,8192]{2,1,0:T(4,128)} %bitcast.25, f32[60,4,8192]{2,1,0:T(4,128)} %bitcast.26, f32[60,4,8192]{2,1,0:T(4,128)} %bitcast.27, ...), custom_call_target="tpu_custom_call" | custom-call | flops 2831155200 | bytes 15728640 | tf_op jit(solution)/shard_map/diffuse_ocean/pallas_call | solution.py:510
  63.2 0.0 all-to-all-done.2.back_ref
  63.2 5.1 %all-to-all-start.3 = ((f32[16,20,4,128]{3,2,1,0:T(4,128)}), f32[16,20,4,128]{3,2,1,0:T(4,128)S(1)}, u32[]{:S(2)}, u32[]{:S(2)}) async-start(f32[16,20,4,128]{3,2,1,0:T(4,128)} %get-tuple-element.49), calls=%async_computation.3 | async-start | bytes 1310720 | tf_op jit(solution)/shard_map/all_to_all | solution.py:620
  68.3 1.4 %collect_away.1 = f32[4,10240]{1,0:T(4,128)S(1)} custom-call(s32[1]{0:T(128)} %bitcast.far_ref, s32[16,32]{1,0:T(8,128)S(1)} %bitcast.18, f32[16,20,4,128]{3,2,1,0:T(4,128)S(1)} %all-to-all-done.2.back_ref), custom_call_target="tpu_custom_call" | custom-call | tf_op jit(solution)/shard_map/collect_away/pallas_call | solution.py:580
  69.7 0.0 copy-start.8
  69.7 0.0 copy-start.9
  69.7 0.4 collective-permute-start.1
  70.1 5.8 %diffuse_atmos.1 = bf16[4,72,8192]{2,1,0:T(8,128)(2,1)} custom-call(bf16[72,72]{1,0:T(8,128)(2,1)S(1)} %copy-done.10, f32[4,8192]{1,0:T(4,128)S(1)} %copy-done.6, bf16[4,72,8192]{2,1,0:T(8,128)(2,1)} %refs_3_.1, bf16[4,72,8192]{2,1,0:T(8,128)(2,1)} %refs_3_.1, bf16[4,72,8192]{2,1,0:T(8,128)(2,1)} %refs_3_.1, bf16[4,72,8192]{2,1,0:T(8,128)(2,1)} %refs_3_.1), custom_call_target="tpu_custom_call" | custom-call | flops 339738624 | bytes 9437184 | tf_op jit(solution)/shard_map/diffuse_atmos/pallas_call | solution.py:159
  76.0 7.8 %all-to-all-done.3.back_ref = f32[16,20,4,128]{3,2,1,0:T(4,128)S(1)} async-done(((f32[16,20,4,128]{3,2,1,0:T(4,128)}), f32[16,20,4,128]{3,2,1,0:T(4,128)S(1)}, u32[]{:S(2)}, u32[]{:S(2)}) %all-to-all-start.3) | async-done | bytes 655392 | tf_op jit(solution)/shard_map/all_to_all | solution.py:620
  83.8 0.0 collective-permute-done.1.refs_0_
  83.8 0.0 copy-done.8
  83.8 2.1 %surface_state.1 = f32[4,8192]{1,0:T(4,128)} custom-call(s32[1]{0:T(128)} %bitcast.far_ref, s32[16,32]{1,0:T(8,128)S(1)} %bitcast.19, f32[16,20,4,128]{3,2,1,0:T(4,128)S(1)} %all-to-all-done.3.back_ref, f32[4,10240]{1,0:T(4,128)S(1)} %collective-permute-done.1.refs_0_, f32[1,8192]{1,0:T(1,128)S(1)} %bitcast.20, f32[4,8192]{1,0:T(4,128)S(1)} %copy-done.8), custom_call_target="tpu_custom_call" | custom-call | tf_op jit(solution)/shard_map/surface_state/pallas_call | solution.py:580
  (15 shorter events, 0.0 us)
Async XLA Ops:
  3.1 14.3 %collective-permute-start = (f32[4,8192]{1,0:T(4,128)}, f32[4,8192]{1,0:T(4,128)S(1)}, u32[]{:S(2)}, u32[]{:S(2)}) collective-permute-start(f32[4,8192]{1,0:T(4,128)} %get-tuple-element.36.own_ref), channel_id=1, source_target_pairs={{0,16},{16,0},{1,17},{17,1},{2,18},{18,2},{3,19},{19,3},{4,20},{20... | collective-permute-start | bytes 393224 | tf_op jit(solution)/shard_map/ppermute | solution.py:623
  7.2 10.3 %all-to-all-start = ((s32[16,1,32]{2,1,0:T(1,128)}), s32[16,1,32]{2,1,0:T(1,128)S(1)}, u32[]{:S(2)}, u32[]{:S(2)}) async-start(s32[16,1,32]{2,1,0:T(1,128)} %bitcast.31), calls=%async_computation | async-start | bytes 16384 | tf_op jit(solution)/shard_map/all_to_all | solution.py:620
  12.0 0.8 copy-start.2
  12.8 4.6 %copy-start.7 = (f32[4,8192]{1,0:T(4,128)S(1)}, f32[4,8192]{1,0:T(4,128)}, u32[]{:S(2)}) copy-start(f32[4,8192]{1,0:T(4,128)} %get-tuple-element.36.own_ref) | copy-start | bytes 393220
  12.8 12.2 %copy-start = (s32[4,8192]{1,0:T(4,128)S(1)}, s32[4,8192]{1,0:T(4,128)}, u32[]{:S(2)}) copy-start(s32[4,8192]{1,0:T(4,128)} %column_ref.4) | copy-start | bytes 393220
  12.8 12.2 %copy-start.1 = (f32[4,8192]{1,0:T(4,128)S(1)}, f32[4,8192]{1,0:T(4,128)}, u32[]{:S(2)}) copy-start(f32[4,8192]{1,0:T(4,128)} %atmos_weight_ref.3) | copy-start | bytes 393220
  12.8 12.2 %copy-start.4 = (s32[8192]{0:T(1024)S(1)}, s32[8192]{0:T(1024)}, u32[]{:S(2)}) copy-start(s32[8192]{0:T(1024)} %param.23) | copy-start | bytes 98308
  12.8 12.2 %copy-start.11 = (s32[4,64]{1,0:T(4,128)S(1)}, s32[4,64]{1,0:T(4,128)}, u32[]{:S(2)}) copy-start(s32[4,64]{1,0:T(4,128)} %get-tuple-element.30.place_ref) | copy-start | bytes 3076
  12.8 28.4 %copy-start.3 = (f32[60,60]{1,0:T(8,128)S(1)}, f32[60,60]{1,0:T(8,128)}, u32[]{:S(2)}) copy-start(f32[60,60]{1,0:T(8,128)} %mix_ref.6) | copy-start | bytes 43204
  12.8 28.4 %copy-start.5 = (f32[4,8192]{1,0:T(4,128)S(1)}, f32[4,8192]{1,0:T(4,128)}, u32[]{:S(2)}) copy-start(f32[4,8192]{1,0:T(4,128)} %ocean_weight_ref.1) | copy-start | bytes 393220
  12.8 28.4 %copy-start.12 = (s32[4,64]{1,0:T(4,128)S(1)}, s32[4,64]{1,0:T(4,128)}, u32[]{:S(2)}) copy-start(s32[4,64]{1,0:T(4,128)} %get-tuple-element.31.spot_ref) | copy-start | bytes 3076
  20.2 21.0 %all-to-all-start.1 = ((f32[16,32,4,128]{3,2,1,0:T(4,128)}), f32[16,32,4,128]{3,2,1,0:T(4,128)S(1)}, u32[]{:S(2)}, u32[]{:S(2)}) async-start(f32[16,32,4,128]{3,2,1,0:T(4,128)} %serve_windows.1), calls=%async_computation.1 | async-start | bytes 2097152 | tf_op jit(solution)/shard_map/all_to_all | solution.py:620
  47.4 15.8 %all-to-all-start.2 = ((f32[16,20,4,128]{3,2,1,0:T(4,128)}), f32[16,20,4,128]{3,2,1,0:T(4,128)S(1)}, u32[]{:S(2)}, u32[]{:S(2)}) async-start(f32[16,20,4,128]{3,2,1,0:T(4,128)} %get-tuple-element.46), calls=%async_computation.2 | async-start | bytes 1310720 | tf_op jit(solution)/shard_map/all_to_all | solution.py:620
  51.0 19.1 %copy-start.6 = (f32[4,8192]{1,0:T(4,128)S(1)}, f32[4,8192]{1,0:T(4,128)}, u32[]{:S(2)}) copy-start(f32[4,8192]{1,0:T(4,128)} %get-tuple-element.52.tend_ref) | copy-start | bytes 393220
  51.0 19.1 %copy-start.10 = (bf16[72,72]{1,0:T(8,128)(2,1)S(1)}, bf16[72,72]{1,0:T(8,128)(2,1)}, u32[]{:S(2)}) copy-start(bf16[72,72]{1,0:T(8,128)(2,1)} %mix_ref.7) | copy-start | bytes 31108
  63.2 20.6 %all-to-all-start.3 = ((f32[16,20,4,128]{3,2,1,0:T(4,128)}), f32[16,20,4,128]{3,2,1,0:T(4,128)S(1)}, u32[]{:S(2)}, u32[]{:S(2)}) async-start(f32[16,20,4,128]{3,2,1,0:T(4,128)} %get-tuple-element.49), calls=%async_computation.3 | async-start | bytes 1310720 | tf_op jit(solution)/shard_map/all_to_all | solution.py:620
  69.7 14.0 %copy-start.8 = (f32[4,8192]{1,0:T(4,128)S(1)}, f32[4,8192]{1,0:T(4,128)}, u32[]{:S(2)}) copy-start(f32[4,8192]{1,0:T(4,128)} %refs_2_.3) | copy-start | bytes 393220
  69.7 14.0 %copy-start.9 = (f32[8192]{0:T(1024)S(1)}, f32[8192]{0:T(1024)}, u32[]{:S(2)}) copy-start(f32[8192]{0:T(1024)} %param.19) | copy-start | bytes 98308
  69.7 14.0 %collective-permute-start.1 = (f32[4,10240]{1,0:T(4,128)S(1)}, f32[4,10240]{1,0:T(4,128)S(1)}, u32[]{:S(2)}, u32[]{:S(2)}) collective-permute-start(f32[4,10240]{1,0:T(4,128)S(1)} %collect_away.1), channel_id=1, source_target_pairs={{0,16},{16,0},{1,17},{17,1},{2,18},{18,2},{3,19},{19,3},{4,20},{20... | collective-permute-start | bytes 491528 | tf_op jit(solution)/shard_map/ppermute | solution.py:623

commit v7 on v6

--- a/solution.py
+++ b/solution.py
@@ -268,6 +268,7 @@
 
 
 GROUP = 8
+hot_type = jnp.float8_e4m3fn
 
 
 def hot_kernel(
@@ -328,7 +329,7 @@
             ],
             axis=0,
         )
-        hot_ref[inner] = hot
+        hot_ref[inner] = hot.astype(hot_type)
         parts = split_high(share)
         rows = jnp.concatenate(
             [jnp.where(first_half, parts, 0.0), jnp.where(first_half, 0.0, parts)], axis=1
@@ -432,7 +433,9 @@
         for inner in range(GROUP):
             step = group * GROUP + inner
             spread = jnp.dot(
-                parts_ref[step], held_ref[step], preferred_element_type=jnp.float32
+                parts_ref[step],
+                held_ref[step].astype(jnp.bfloat16),
+                preferred_element_type=jnp.float32,
             )
             for k in range(intersections):
                 side = slice((k % 2) * LANES, (k % 2 + 1) * LANES)
@@ -529,14 +532,14 @@
     )(mixing, forcing, mask, *[state] * len(specs))
 
 
-def collect_kernel(per_owner, far_ref, asked_ref, back_ref, *refs):
+def collect_kernel(per_owner, columns, far_ref, asked_ref, back_ref, *refs):
     near, _, fields, _ = back_ref.shape
-    chains = 4
-    sums = refs[-2 * chains :]
-    rest = refs[: -2 * chains]
+    chains = 2
+    sums = refs[-chains:]
+    rest = refs[:-chains]
     home = len(rest) > 1
-    columns = sums[0].shape[1]
-    quarter = columns // fields
+    windows = columns // LANES
+    quarter = windows // fields
     far = far_ref[0]
     first = (far if home else 1 - far) * per_owner
     for ref in sums:
@@ -546,44 +549,43 @@
         for slot in range(per_owner):
             for chain in range(chains):
                 peer = step * chains + chain
-                at = window(asked_ref[peer, first + slot])
                 tile, row = per_owner + slot // fields, slot % fields
-                sums[chain][:, at] += back_ref[peer, slot]
-                sums[chains + chain][:, at] += back_ref[peer, tile, row : row + 1]
+                share = back_ref[peer, tile, row : row + 1]
+                block = jnp.concatenate(
+                    [back_ref[peer, slot], jnp.broadcast_to(share, (fields, LANES))], axis=0
+                )
+                sums[chain][asked_ref[peer, first + slot]] += block
         return carry
 
     lax.fori_loop(0, near // chains, body, 0)
-    values, shares = sums[0][...], sums[chains][...]
-    for chain in range(1, chains):
-        values = values + sums[chain][...]
-        shares = shares + sums[chains + chain][...]
     out_ref = rest[-1]
-    if home:
-        other_ref, land_weight_ref, land_ref = rest[:3]
-        land_weight = land_weight_ref[...]
-        total = values + other_ref[:, :columns] + land_weight * land_ref[...]
-        weight = shares + land_weight
-        for row in range(fields):
-            part = slice(row * quarter, (row + 1) * quarter)
-            other_shares = other_ref[row : row + 1, columns:]
-            out_ref[:, part] = total[:, part] / (weight[:, part] + other_shares)
-    else:
-        out_ref[:, :columns] = values
-        for row in range(fields):
-            out_ref[row : row + 1, columns:] = shares[:, row * quarter : (row + 1) * quarter]
+    for spot in range(windows):
+        block = sums[0][spot]
+        for ref in sums[1:]:
+            block = block + ref[spot]
+        here = slice(spot * LANES, (spot + 1) * LANES)
+        row = slice(spot // quarter, spot // quarter + 1)
+        side = spot % quarter * LANES
+        beside = slice(columns + side, columns + side + LANES)
+        if home:
+            other_ref, land_weight_ref, land_ref = rest[:3]
+            land_weight = land_weight_ref[:, here]
+            total = block[:fields] + other_ref[:, here] + land_weight * land_ref[:, here]
+            out_ref[:, here] = total / (block[fields:] + (other_ref[row, beside] + land_weight))
+        else:
+            out_ref[:, here] = block[:fields]
+            out_ref[row, beside] = block[fields : fields + 1]
 
 
 def collect(asked, far, back, per_owner, columns, rest):
     fields = back.shape[2]
-    chains = 4
     width = columns if rest else columns + columns // fields
     return pl.pallas_call(
-        functools.partial(collect_kernel, per_owner),
+        functools.partial(collect_kernel, per_owner, columns),
         in_specs=[smem, smem, vmem] + [vmem] * len(rest),
         out_specs=vmem,
         out_shape=jax.ShapeDtypeStruct((fields, width), jnp.float32),
-        scratch_shapes=[pltpu.VMEM((fields, columns), jnp.float32)] * chains
-        + [pltpu.VMEM((1, columns), jnp.float32)] * chains,
+        scratch_shapes=[pltpu.VMEM((columns // LANES, 2 * fields, LANES), jnp.float32)] * 2,
         compiler_params=params,
         name="surface_state" if rest else "collect_away",
     )(far, asked, back, *rest)
@@ -663,7 +665,7 @@
             pl.BlockSpec((2 * near * rows, fields, LANES), lambda i: (0, 0, 0)),
         ],
         out_shape=[
-            jax.ShapeDtypeStruct((windows, 2 * LANES, 2 * LANES), jnp.bfloat16),
+            jax.ShapeDtypeStruct((windows, 2 * LANES, 2 * LANES), hot_type),
             jax.ShapeDtypeStruct((2 * near * rows, fields, LANES), jnp.float32),
         ],
         scratch_shapes=[pltpu.VMEM((windows // GROUP, LANES, LANES), jnp.bfloat16)]
@@ -685,7 +687,7 @@
         scratch_shapes=[
             pltpu.VMEM((near * spots, fields, LANES), jnp.float32),
             pltpu.VMEM((windows, 2 * fields * intersections, 2 * LANES), jnp.bfloat16),
-            pltpu.VMEM((windows, 2 * LANES, 2 * LANES), jnp.bfloat16),
+            pltpu.VMEM((windows, 2 * LANES, 2 * LANES), hot_type),
             pltpu.SemaphoreType.DMA((windows // GROUP,)),
             pltpu.SemaphoreType.DMA((4,)),
         ],
@@ -706,16 +708,16 @@
         hot,
         shares.reshape(2, near, rows, fields, LANES),
     )
-    ocean_updated = diffuse_ocean(state, ocean_mixing, forcing, mask).transpose(1, 0, 2)
-    back_away, ocean_updated, home = lax.optimization_barrier(
-        (to_near(away), ocean_updated, home)
+    tendency, forcing = lax.optimization_barrier((tendency, forcing))
+    atmos_updated = diffuse_atmos(atmos_profiles, atmos_mixing, tendency)
+    back_away, atmos_updated, home = lax.optimization_barrier(
+        (to_near(away), atmos_updated, home)
     )
     back_home = to_near(home)
     sums_away = collect(asked, far, back_away, per_owner, columns, ())
-    tendency, sums_away = lax.optimization_barrier((tendency, sums_away))
     other_sums = to_far(sums_away)
-    atmos_updated = diffuse_atmos(atmos_profiles, atmos_mixing, tendency)
-    back_home, atmos_updated = lax.optimization_barrier((back_home, atmos_updated))
+    ocean_updated = diffuse_ocean(state, ocean_mixing, forcing, mask).transpose(1, 0, 2)
+    back_home, ocean_updated = lax.optimization_barrier((back_home, ocean_updated))
     surface_state = collect(
         asked,
         far,

time: 86.7 us -> 84.5 us (0.975)
  starting transfers between devices: 22.8 us -> 20.8 us
  Pallas kernels: 46.5 us -> 45.1 us
  local copies, waits for them, and re-layouts: 0.81 us -> 2.08 us
    all_to_all x4, starting transfers between devices: 18.3 us -> 16.2 us  [to_near(): lax.all_to_all(values, ('near', 'sub'), split_axis=0, concat_axis=0, tile...]
    pallas_call x1, Pallas kernels: 9.25 us -> 7.67 us  [per_device(): pl.pallas_call(hot_kernel, grid=(windows // GROUP,), in_specs=[smem] + [v...]
    unnamed x26, local copies, waits for them, and re-layouts: 0.81 us -> 2.08 us
  transfers between devices with their start and end apart: 6 -> 6, of which waited for: 3 -> 4; matrix products, arithmetic and copies ran while one was open for 0% -> 0% of each run, Pallas kernels for 38% -> 38%
where the time goes in v7:
time: 84.5 us; the launch traced here: 83.7 us
  Pallas kernels  45.1 us (53%)
  starting transfers between devices  20.8 us (25%)
  waiting for transfers between devices  14.9 us (18%)
  local copies, waits for them, and re-layouts  2.08 us (2%)
  between operations  0.87 us (1%)
    all_to_all x4, starting transfers between devices, to_near(): lax.all_to_all(values, ('near', 'sub'), split_axis=0, concat_axis=0, tile...  16.2 us
    all_to_all x4, waiting for transfers between devices, to_near(): lax.all_to_all(values, ('near', 'sub'), split_axis=0, concat_axis=0, tile...  14.9 us
    pallas_call x1, Pallas kernels, diffuse_ocean(): pl.pallas_call(ocean_kernel, grid=(cells // block,), in_specs=[pl.BlockSp...  12.1 us
    pallas_call x1, Pallas kernels, per_device(): pl.pallas_call(hot_kernel, grid=(windows // GROUP,), in_specs=[smem] + [v...  7.67 us
    pallas_call x1, Pallas kernels, per_device(): pl.pallas_call(middle_kernel, in_specs=[smem] * 4 + [vmem] * 7 + [hbm, vm...  6.19 us
    pallas_call x1, Pallas kernels, diffuse_atmos(): pl.pallas_call(atmos_kernel, grid=(columns // block,), in_specs=[pl.Block...  5.86 us
    ppermute x2, starting transfers between devices, to_far(): return lax.ppermute(values, 'far', ((0, 1), (1, 0)))  4.52 us
    pallas_call x1, Pallas kernels, top_level(): pl.pallas_call(top_kernel, grid=(cells // block,), in_specs=[smem] + spec...  4.23 us
  transfers between devices with their start and end apart: 6, of which 4 were waited for; matrix products, arithmetic and copies ran while one was open for 0% of the time, Pallas kernels for 38%

profile of v7, /device:TPU:0, one launch (start us, length us, event | category | flops | bytes accessed | tf_op | source)
XLA Modules:
  0.0 83.7 jit_solution(14540632241448487521)
XLA Ops:
  0.6 2.4 %requests_and_rates.1 = (s32[4,64]{1,0:T(4,128)}, s32[4,64]{1,0:T(4,128)}, s32[16,32]{1,0:T(8,128)}, f32[4,8192]{1,0:T(4,128)}, f32[4,8192]{1,0:T(4,128)}) custom-call(s32[4,8192]{1,0:T(4,128)} %slot_ref.1, s32[4,8192]{1,0:T(4,128)} %column_ref.4, bf16[4,72,8192]{2,1,0:T(8,128)(2,1)} %refs_3_.1, f32[1,8192]{1,0:T(1,128)} %bitcast.30, f32[4,8192]{1,0:T(4,128)} %before_ref.1, ...), custom_call_target="tpu_custom_call" | custom-call | tf_op jit(solution)/shard_map/requests_and_rates/pallas_call | solution.py:119
  3.1 4.1 %collective-permute-start = (f32[4,8192]{1,0:T(4,128)}, f32[4,8192]{1,0:T(4,128)S(1)}, u32[]{:S(2)}, u32[]{:S(2)}) collective-permute-start(f32[4,8192]{1,0:T(4,128)} %get-tuple-element.36.own_ref), channel_id=1, source_target_pairs={{0,16},{16,0},{1,17},{17,1},{2,18},{18,2},{3,19},{19,3},{4,20},{20... | collective-permute-start | bytes 393224 | tf_op jit(solution)/shard_map/ppermute | solution.py:625
  7.2 4.8 %all-to-all-start = ((s32[16,1,32]{2,1,0:T(1,128)}), s32[16,1,32]{2,1,0:T(1,128)S(1)}, u32[]{:S(2)}, u32[]{:S(2)}) async-start(s32[16,1,32]{2,1,0:T(1,128)} %bitcast.31), calls=%async_computation | async-start | bytes 16384 | tf_op jit(solution)/shard_map/all_to_all | solution.py:622
  12.0 0.0 copy-start.7
  12.1 0.0 copy-start.1
  12.1 0.0 copy-start.2
  12.1 0.0 copy-start.4
  12.1 0.0 copy-start.6
  12.1 4.2 %top_level.1 = (f32[4,8192]{1,0:T(4,128)S(1)}, f32[4,8192]{1,0:T(4,128)S(1)}) custom-call(f32[60,60]{1,0:T(8,128)S(1)} %copy-done.3, f32[60,4,8192]{2,1,0:T(4,128)} %bitcast.21, f32[60,4,8192]{2,1,0:T(4,128)} %bitcast.22, f32[60,4,8192]{2,1,0:T(4,128)} %bitcast.23, f32[60,4,8192]{2,1,0:T(4,128)} %bitcast.24), custom_call_target="tpu_custom_call" | custom-call | flops 3932160 | bytes 7864320 | tf_op jit(solution)/shard_map/top_level/pallas_call | solution.py:205
  16.4 1.1 %all-to-all-done = s32[16,1,32]{2,1,0:T(1,128)S(1)} async-done(((s32[16,1,32]{2,1,0:T(1,128)}), s32[16,1,32]{2,1,0:T(1,128)S(1)}, u32[]{:S(2)}, u32[]{:S(2)}) %all-to-all-start) | async-done | bytes 2080 | tf_op jit(solution)/shard_map/all_to_all | solution.py:622
  17.4 0.0 collective-permute-done.other_ref
  17.4 2.8 %serve_windows.1 = f32[16,32,4,128]{3,2,1,0:T(4,128)} custom-call(s32[1]{0:T(128)} %bitcast.far_ref, s32[16,32]{1,0:T(8,128)S(1)} %bitcast.17, f32[4,8192]{1,0:T(4,128)S(1)} %copy-done.7, f32[4,8192]{1,0:T(4,128)S(1)} %collective-permute-done.other_ref), custom_call_target="tpu_custom_call" | custom-call | tf_op jit(solution)/shard_map/serve_windows/pallas_call | solution.py:641
  20.3 0.0 copy-start.10
  20.3 4.2 %all-to-all-start.1 = ((f32[16,32,4,128]{3,2,1,0:T(4,128)}), f32[16,32,4,128]{3,2,1,0:T(4,128)S(1)}, u32[]{:S(2)}, u32[]{:S(2)}) async-start(f32[16,32,4,128]{3,2,1,0:T(4,128)} %serve_windows.1), calls=%async_computation.1 | async-start | bytes 2097152 | tf_op jit(solution)/shard_map/all_to_all | solution.py:622
  24.5 0.0 copy-done.1
  24.5 7.7 %one_hot_and_shares.1 = (f8e4m3fn[64,256,256]{2,1,0:T(32,128)(4,1)S(1)}, f32[128,4,128]{2,1,0:T(4,128)S(1)}) custom-call(s32[4,64]{1,0:T(4,128)S(1)} %copy-done.11, s32[4,8192]{1,0:T(4,128)S(1)} %copy-done.1, f32[4,8192]{1,0:T(4,128)S(1)} %copy-done.2, s32[1,8192]{1,0:T(1,128)S(1)} %bitcast.13), custom_call_target="tpu_custom_call" | custom-call | tf_op jit(solution)/shard_map/one_hot_and_shares/pallas_call | solution.py:659
  32.2 0.0 copy-start
  32.2 2.0 %copy-done = f8e4m3fn[64,256,256]{2,1,0:T(32,128)(4,1)} copy-done((f8e4m3fn[64,256,256]{2,1,0:T(32,128)(4,1)}, f8e4m3fn[64,256,256]{2,1,0:T(32,128)(4,1)S(1)}, u32[]{:S(2)}) %copy-start) | copy-done | bytes 4194328
  34.2 6.4 %all-to-all-done.1 = f32[16,32,4,128]{3,2,1,0:T(4,128)S(1)} async-done(((f32[16,32,4,128]{3,2,1,0:T(4,128)}), f32[16,32,4,128]{3,2,1,0:T(4,128)S(1)}, u32[]{:S(2)}, u32[]{:S(2)}) %all-to-all-start.1) | async-done | bytes 1048608 | tf_op jit(solution)/shard_map/all_to_all | solution.py:622
  40.7 6.2 %forcing_and_windows.1 = (f32[4,8192]{1,0:T(4,128)S(1)}, f32[16,20,4,128]{3,2,1,0:T(4,128)}, f32[16,20,4,128]{3,2,1,0:T(4,128)}) custom-call(s32[1]{0:T(128)} %bitcast.far_ref, s32[4,64]{1,0:T(4,128)S(1)} %copy-done.11, s32[4,64]{1,0:T(4,128)S(1)} %copy-done.12, f32[60,60]{1,0:T(8,128)S(1)} %copy-done.3, f32[512,4,128]{2,1,0:T(4,128)S(1)} %bitcast.12, ...), custom_call_target="tpu_custom_call" | custom-call | tf_op jit(solution)/shard_map/forcing_and_windows/pallas_call | solution.py:678
  46.9 3.6 %all-to-all-start.2 = ((f32[16,20,4,128]{3,2,1,0:T(4,128)}), f32[16,20,4,128]{3,2,1,0:T(4,128)S(1)}, u32[]{:S(2)}, u32[]{:S(2)}) async-start(f32[16,20,4,128]{3,2,1,0:T(4,128)} %get-tuple-element.46), calls=%async_computation.2 | async-start | bytes 1310720 | tf_op jit(solution)/shard_map/all_to_all | solution.py:622
  50.5 5.9 %diffuse_atmos.1 = bf16[4,72,8192]{2,1,0:T(8,128)(2,1)} custom-call(bf16[72,72]{1,0:T(8,128)(2,1)S(1)} %copy-done.10, f32[4,8192]{1,0:T(4,128)S(1)} %copy-done.5, bf16[4,72,8192]{2,1,0:T(8,128)(2,1)} %refs_3_.1, bf16[4,72,8192]{2,1,0:T(8,128)(2,1)} %refs_3_.1, bf16[4,72,8192]{2,1,0:T(8,128)(2,1)} %refs_3_.1, bf16[4,72,8192]{2,1,0:T(8,128)(2,1)} %refs_3_.1), custom_call_target="tpu_custom_call" | custom-call | flops 339738624 | bytes 9437184 | tf_op jit(solution)/shard_map/diffuse_atmos/pallas_call | solution.py:159
  56.4 6.0 %all-to-all-done.2.back_ref = f32[16,20,4,128]{3,2,1,0:T(4,128)S(1)} async-done(((f32[16,20,4,128]{3,2,1,0:T(4,128)}), f32[16,20,4,128]{3,2,1,0:T(4,128)S(1)}, u32[]{:S(2)}, u32[]{:S(2)}) %all-to-all-start.2) | async-done | bytes 655392 | tf_op jit(solution)/shard_map/all_to_all | solution.py:622
  62.4 3.6 %all-to-all-start.3 = ((f32[16,20,4,128]{3,2,1,0:T(4,128)}), f32[16,20,4,128]{3,2,1,0:T(4,128)S(1)}, u32[]{:S(2)}, u32[]{:S(2)}) async-start(f32[16,20,4,128]{3,2,1,0:T(4,128)} %get-tuple-element.52), calls=%async_computation.3 | async-start | bytes 1310720 | tf_op jit(solution)/shard_map/all_to_all | solution.py:622
  66.0 1.5 %collect_away.1 = f32[4,10240]{1,0:T(4,128)S(1)} custom-call(s32[1]{0:T(128)} %bitcast.far_ref, s32[16,32]{1,0:T(8,128)S(1)} %bitcast.18, f32[16,20,4,128]{3,2,1,0:T(4,128)S(1)} %all-to-all-done.2.back_ref), custom_call_target="tpu_custom_call" | custom-call | tf_op jit(solution)/shard_map/collect_away/pallas_call | solution.py:583
  67.5 0.0 copy-start.8
  67.5 0.0 copy-start.9
  67.6 0.4 collective-permute-start.1
  68.0 12.1 %diffuse_ocean.1 = f32[60,4,8192]{2,1,0:T(4,128)} custom-call(f32[60,60]{1,0:T(8,128)S(1)} %copy-done.3, f32[4,8192]{1,0:T(4,128)S(1)} %get-tuple-element.53.forcing_ref, s32[1,8192]{1,0:T(1,128)S(1)} %bitcast.15, f32[60,4,8192]{2,1,0:T(4,128)} %bitcast.25, f32[60,4,8192]{2,1,0:T(4,128)} %bitcast.26, f32[60,4,8192]{2,1,0:T(4,128)} %bitcast.27, ...), custom_call_target="tpu_custom_call" | custom-call | flops 2831155200 | bytes 15728640 | tf_op jit(solution)/shard_map/diffuse_ocean/pallas_call | solution.py:513
  80.1 1.3 %all-to-all-done.3.back_ref = f32[16,20,4,128]{3,2,1,0:T(4,128)S(1)} async-done(((f32[16,20,4,128]{3,2,1,0:T(4,128)}), f32[16,20,4,128]{3,2,1,0:T(4,128)S(1)}, u32[]{:S(2)}, u32[]{:S(2)}) %all-to-all-start.3) | async-done | bytes 655392 | tf_op jit(solution)/shard_map/all_to_all | solution.py:622
  81.4 0.0 collective-permute-done.1.refs_0_
  81.4 2.3 %surface_state.1 = f32[4,8192]{1,0:T(4,128)} custom-call(s32[1]{0:T(128)} %bitcast.far_ref, s32[16,32]{1,0:T(8,128)S(1)} %bitcast.19, f32[16,20,4,128]{3,2,1,0:T(4,128)S(1)} %all-to-all-done.3.back_ref, f32[4,10240]{1,0:T(4,128)S(1)} %collective-permute-done.1.refs_0_, f32[1,8192]{1,0:T(1,128)S(1)} %bitcast.20, f32[4,8192]{1,0:T(4,128)S(1)} %copy-done.8), custom_call_target="tpu_custom_call" | custom-call | tf_op jit(solution)/shard_map/surface_state/pallas_call | solution.py:583
  (15 shorter events, 0.0 us)
Async XLA Ops:
  0.6 11.4 %copy-start.3 = (f32[60,60]{1,0:T(8,128)S(1)}, f32[60,60]{1,0:T(8,128)}, u32[]{:S(2)}) copy-start(f32[60,60]{1,0:T(8,128)} %mix_ref.7) | copy-start | bytes 43204
  3.1 14.4 %collective-permute-start = (f32[4,8192]{1,0:T(4,128)}, f32[4,8192]{1,0:T(4,128)S(1)}, u32[]{:S(2)}, u32[]{:S(2)}) collective-permute-start(f32[4,8192]{1,0:T(4,128)} %get-tuple-element.36.own_ref), channel_id=1, source_target_pairs={{0,16},{16,0},{1,17},{17,1},{2,18},{18,2},{3,19},{19,3},{4,20},{20... | collective-permute-start | bytes 393224 | tf_op jit(solution)/shard_map/ppermute | solution.py:625
  7.2 10.3 %all-to-all-start = ((s32[16,1,32]{2,1,0:T(1,128)}), s32[16,1,32]{2,1,0:T(1,128)S(1)}, u32[]{:S(2)}, u32[]{:S(2)}) async-start(s32[16,1,32]{2,1,0:T(1,128)} %bitcast.31), calls=%async_computation | async-start | bytes 16384 | tf_op jit(solution)/shard_map/all_to_all | solution.py:622
  12.0 5.4 %copy-start.7 = (f32[4,8192]{1,0:T(4,128)S(1)}, f32[4,8192]{1,0:T(4,128)}, u32[]{:S(2)}) copy-start(f32[4,8192]{1,0:T(4,128)} %get-tuple-element.36.own_ref) | copy-start | bytes 393220
  12.1 12.4 %copy-start.1 = (s32[4,8192]{1,0:T(4,128)S(1)}, s32[4,8192]{1,0:T(4,128)}, u32[]{:S(2)}) copy-start(s32[4,8192]{1,0:T(4,128)} %column_ref.4) | copy-start | bytes 393220
  12.1 12.4 %copy-start.2 = (f32[4,8192]{1,0:T(4,128)S(1)}, f32[4,8192]{1,0:T(4,128)}, u32[]{:S(2)}) copy-start(f32[4,8192]{1,0:T(4,128)} %atmos_weight_ref.3) | copy-start | bytes 393220
  12.1 12.4 %copy-start.4 = (s32[8192]{0:T(1024)S(1)}, s32[8192]{0:T(1024)}, u32[]{:S(2)}) copy-start(s32[8192]{0:T(1024)} %param.23) | copy-start | bytes 98308
  12.1 12.4 %copy-start.11 = (s32[4,64]{1,0:T(4,128)S(1)}, s32[4,64]{1,0:T(4,128)}, u32[]{:S(2)}) copy-start(s32[4,64]{1,0:T(4,128)} %get-tuple-element.30.place_ref) | copy-start | bytes 3076
  12.1 28.6 %copy-start.6 = (f32[4,8192]{1,0:T(4,128)S(1)}, f32[4,8192]{1,0:T(4,128)}, u32[]{:S(2)}) copy-start(f32[4,8192]{1,0:T(4,128)} %ocean_weight_ref.1) | copy-start | bytes 393220
  12.1 28.6 %copy-start.12 = (s32[4,64]{1,0:T(4,128)S(1)}, s32[4,64]{1,0:T(4,128)}, u32[]{:S(2)}) copy-start(s32[4,64]{1,0:T(4,128)} %get-tuple-element.31.spot_ref) | copy-start | bytes 3076
  20.2 30.2 %copy-start.5 = (f32[4,8192]{1,0:T(4,128)S(1)}, f32[4,8192]{1,0:T(4,128)}, u32[]{:S(2)}) copy-start(f32[4,8192]{1,0:T(4,128)} %get-tuple-element.49.tend_ref) | copy-start | bytes 393220
  20.3 30.2 %copy-start.10 = (bf16[72,72]{1,0:T(8,128)(2,1)S(1)}, bf16[72,72]{1,0:T(8,128)(2,1)}, u32[]{:S(2)}) copy-start(bf16[72,72]{1,0:T(8,128)(2,1)} %mix_ref.6) | copy-start | bytes 31108
  20.3 20.4 %all-to-all-start.1 = ((f32[16,32,4,128]{3,2,1,0:T(4,128)}), f32[16,32,4,128]{3,2,1,0:T(4,128)S(1)}, u32[]{:S(2)}, u32[]{:S(2)}) async-start(f32[16,32,4,128]{3,2,1,0:T(4,128)} %serve_windows.1), calls=%async_computation.1 | async-start | bytes 2097152 | tf_op jit(solution)/shard_map/all_to_all | solution.py:622
  32.2 2.0 %copy-start = (f8e4m3fn[64,256,256]{2,1,0:T(32,128)(4,1)}, f8e4m3fn[64,256,256]{2,1,0:T(32,128)(4,1)S(1)}, u32[]{:S(2)}) copy-start(f8e4m3fn[64,256,256]{2,1,0:T(32,128)(4,1)S(1)} %get-tuple-element.44.hot_ref) | copy-start | bytes 12582916
  46.9 15.5 %all-to-all-start.2 = ((f32[16,20,4,128]{3,2,1,0:T(4,128)}), f32[16,20,4,128]{3,2,1,0:T(4,128)S(1)}, u32[]{:S(2)}, u32[]{:S(2)}) async-start(f32[16,20,4,128]{3,2,1,0:T(4,128)} %get-tuple-element.46), calls=%async_computation.2 | async-start | bytes 1310720 | tf_op jit(solution)/shard_map/all_to_all | solution.py:622
  62.4 19.0 %all-to-all-start.3 = ((f32[16,20,4,128]{3,2,1,0:T(4,128)}), f32[16,20,4,128]{3,2,1,0:T(4,128)S(1)}, u32[]{:S(2)}, u32[]{:S(2)}) async-start(f32[16,20,4,128]{3,2,1,0:T(4,128)} %get-tuple-element.52), calls=%async_computation.3 | async-start | bytes 1310720 | tf_op jit(solution)/shard_map/all_to_all | solution.py:622
  67.5 13.9 %copy-start.8 = (f32[4,8192]{1,0:T(4,128)S(1)}, f32[4,8192]{1,0:T(4,128)}, u32[]{:S(2)}) copy-start(f32[4,8192]{1,0:T(4,128)} %refs_2_.3) | copy-start | bytes 393220
  67.5 13.9 %copy-start.9 = (f32[8192]{0:T(1024)S(1)}, f32[8192]{0:T(1024)}, u32[]{:S(2)}) copy-start(f32[8192]{0:T(1024)} %param.19) | copy-start | bytes 98308
  67.6 13.9 %collective-permute-start.1 = (f32[4,10240]{1,0:T(4,128)S(1)}, f32[4,10240]{1,0:T(4,128)S(1)}, u32[]{:S(2)}, u32[]{:S(2)}) collective-permute-start(f32[4,10240]{1,0:T(4,128)S(1)} %collect_away.1), channel_id=1, source_target_pairs={{0,16},{16,0},{1,17},{17,1},{2,18},{18,2},{3,19},{19,3},{4,20},{20... | collective-permute-start | bytes 491528 | tf_op jit(solution)/shard_map/ppermute | solution.py:625

commit v8 on v5

--- a/solution.py
+++ b/solution.py
@@ -380,25 +380,19 @@
     per_owner = packed * fields // (fields + 1)
     rows = per_owner // fields
 
-    def fetch(group):
-        part = pl.ds(group * GROUP, GROUP)
-        return pltpu.make_async_copy(hot_ref.at[part], held_ref.at[part], held_sem.at[group])
+    def fetch(step):
+        return pltpu.make_async_copy(hot_ref.at[step], held_ref.at[step], held_sem.at[step])
 
     groups = windows // GROUP
-    ahead = min(3, groups)
-    for group in range(ahead):
-        fetch(group).start()
+    for step in range(windows):
+        fetch(step).start()
     value_ref[...] = jnp.zeros(value_ref.shape, jnp.float32)
     corner = mix_ref[0, 0]
     blank = jnp.zeros((2 * fields, LANES), jnp.float32)
 
     def body(group, carry):
-        fetch(group).wait()
-
-        @pl.when(group + ahead < groups)
-        def _():
-            fetch(group + ahead).start()
-
+        for inner in range(GROUP):
+            fetch(group * GROUP + inner).wait()
         for inner in range(GROUP):
             step = group * GROUP + inner
             here = window(step)
@@ -680,7 +674,7 @@
         scratch_shapes=[
             pltpu.VMEM((near * spots, fields, LANES), jnp.float32),
             pltpu.VMEM((windows, 2 * LANES, 2 * LANES), jnp.bfloat16),
-            pltpu.SemaphoreType.DMA((windows // GROUP,)),
+            pltpu.SemaphoreType.DMA((windows,)),
             pltpu.SemaphoreType.DMA((4,)),
         ],
         compiler_params=middle_params,

time: 85.8 us -> 85.7 us (level)
  no operation moved by 1% of the time
where the time goes in v8:
time: 85.7 us; the launch traced here: 84.9 us
  Pallas kernels  47.2 us (55%)
  starting transfers between devices  21.3 us (25%)
  waiting for transfers between devices  14.7 us (17%)
    all_to_all x4, starting transfers between devices, to_near(): lax.all_to_all(values, ('near', 'sub'), split_axis=0, concat_axis=0, tile...  16.8 us
    all_to_all x4, waiting for transfers between devices, to_near(): lax.all_to_all(values, ('near', 'sub'), split_axis=0, concat_axis=0, tile...  14.7 us
    pallas_call x1, Pallas kernels, diffuse_ocean(): pl.pallas_call(ocean_kernel, grid=(cells // block,), in_specs=[pl.BlockSp...  12.1 us
    pallas_call x1, Pallas kernels, per_device(): pl.pallas_call(hot_kernel, grid=(windows // GROUP,), in_specs=[smem] + [v...  9.25 us
    pallas_call x1, Pallas kernels, per_device(): pl.pallas_call(middle_kernel, in_specs=[smem] * 4 + [vmem] * 7 + [hbm, vm...  6.91 us
    pallas_call x1, Pallas kernels, diffuse_atmos(): pl.pallas_call(atmos_kernel, grid=(columns // block,), in_specs=[pl.Block...  5.86 us
    ppermute x2, starting transfers between devices, to_far(): return lax.ppermute(values, 'far', ((0, 1), (1, 0)))  4.49 us
    pallas_call x1, Pallas kernels, top_level(): pl.pallas_call(top_kernel, grid=(cells // block,), in_specs=[smem] + spec...  4.2 us
  transfers between devices with their start and end apart: 6, of which 4 were waited for; matrix products, arithmetic and copies ran while one was open for 0% of the time, Pallas kernels for 39%

profile of v8, /device:TPU:0, one launch (start us, length us, event | category | flops | bytes accessed | tf_op | source)
XLA Modules:
  0.0 84.9 jit_solution(16410506355477763751)
XLA Ops:
  0.6 2.5 %requests_and_rates.1 = (s32[4,64]{1,0:T(4,128)}, s32[4,64]{1,0:T(4,128)}, s32[16,32]{1,0:T(8,128)}, f32[4,8192]{1,0:T(4,128)}, f32[4,8192]{1,0:T(4,128)}) custom-call(s32[4,8192]{1,0:T(4,128)} %slot_ref.1, s32[4,8192]{1,0:T(4,128)} %column_ref.4, bf16[4,72,8192]{2,1,0:T(8,128)(2,1)} %refs_3_.1, f32[1,8192]{1,0:T(1,128)} %bitcast.30, f32[4,8192]{1,0:T(4,128)} %before_ref.1, ...), custom_call_target="tpu_custom_call" | custom-call | tf_op jit(solution)/shard_map/requests_and_rates/pallas_call | solution.py:119
  3.1 4.1 %collective-permute-start = (f32[4,8192]{1,0:T(4,128)}, f32[4,8192]{1,0:T(4,128)S(1)}, u32[]{:S(2)}, u32[]{:S(2)}) collective-permute-start(f32[4,8192]{1,0:T(4,128)} %get-tuple-element.36.own_ref), channel_id=1, source_target_pairs={{0,16},{16,0},{1,17},{17,1},{2,18},{18,2},{3,19},{19,3},{4,20},{20... | collective-permute-start | bytes 393224 | tf_op jit(solution)/shard_map/ppermute | solution.py:612
  7.2 4.8 %all-to-all-start = ((s32[16,1,32]{2,1,0:T(1,128)}), s32[16,1,32]{2,1,0:T(1,128)S(1)}, u32[]{:S(2)}, u32[]{:S(2)}) async-start(s32[16,1,32]{2,1,0:T(1,128)} %bitcast.31), calls=%async_computation | async-start | bytes 16384 | tf_op jit(solution)/shard_map/all_to_all | solution.py:609
  12.0 0.0 copy-start.2
  12.0 0.7 copy-done.2
  12.8 0.0 copy-start.11
  12.8 0.0 copy-start.3
  12.8 0.0 copy-start.5
  12.8 0.0 copy-start.12
  12.8 4.2 %top_level.1 = (f32[4,8192]{1,0:T(4,128)S(1)}, f32[4,8192]{1,0:T(4,128)S(1)}) custom-call(f32[60,60]{1,0:T(8,128)S(1)} %copy-done.2, f32[60,4,8192]{2,1,0:T(4,128)} %bitcast.21, f32[60,4,8192]{2,1,0:T(4,128)} %bitcast.22, f32[60,4,8192]{2,1,0:T(4,128)} %bitcast.23, f32[60,4,8192]{2,1,0:T(4,128)} %bitcast.24), custom_call_target="tpu_custom_call" | custom-call | flops 3932160 | bytes 7864320 | tf_op jit(solution)/shard_map/top_level/pallas_call | solution.py:205
  17.1 0.0 copy-start.10
  17.1 0.4 all-to-all-done
  17.4 0.0 collective-permute-done.other_ref
  17.4 0.0 copy-done.7
  17.4 2.8 %serve_windows.1 = f32[16,32,4,128]{3,2,1,0:T(4,128)} custom-call(s32[1]{0:T(128)} %bitcast.far_ref, s32[16,32]{1,0:T(8,128)S(1)} %bitcast.17, f32[4,8192]{1,0:T(4,128)S(1)} %copy-done.7, f32[4,8192]{1,0:T(4,128)S(1)} %collective-permute-done.other_ref), custom_call_target="tpu_custom_call" | custom-call | tf_op jit(solution)/shard_map/serve_windows/pallas_call | solution.py:628
  20.2 4.8 %all-to-all-start.1 = ((f32[16,32,4,128]{3,2,1,0:T(4,128)}), f32[16,32,4,128]{3,2,1,0:T(4,128)S(1)}, u32[]{:S(2)}, u32[]{:S(2)}) async-start(f32[16,32,4,128]{3,2,1,0:T(4,128)} %serve_windows.1), calls=%async_computation.1 | async-start | bytes 2097152 | tf_op jit(solution)/shard_map/all_to_all | solution.py:609
  25.1 9.3 %one_hot_and_shares.1 = (bf16[64,256,256]{2,1,0:T(8,128)(2,1)}, f32[128,4,128]{2,1,0:T(4,128)S(1)}) custom-call(s32[4,64]{1,0:T(4,128)S(1)} %copy-done.11, s32[4,8192]{1,0:T(4,128)S(1)} %copy-done, f32[4,8192]{1,0:T(4,128)S(1)} %copy-done.1, s32[1,8192]{1,0:T(1,128)S(1)} %bitcast.13), custom_call_target="tpu_custom_call" | custom-call | tf_op jit(solution)/shard_map/one_hot_and_shares/pallas_call | solution.py:646
  34.3 6.9 %all-to-all-done.1 = f32[16,32,4,128]{3,2,1,0:T(4,128)S(1)} async-done(((f32[16,32,4,128]{3,2,1,0:T(4,128)}), f32[16,32,4,128]{3,2,1,0:T(4,128)S(1)}, u32[]{:S(2)}, u32[]{:S(2)}) %all-to-all-start.1) | async-done | bytes 1048608 | tf_op jit(solution)/shard_map/all_to_all | solution.py:609
  41.2 0.0 copy-done.5
  41.2 6.9 %forcing_and_windows.1 = (f32[4,8192]{1,0:T(4,128)S(1)}, f32[16,20,4,128]{3,2,1,0:T(4,128)}, f32[16,20,4,128]{3,2,1,0:T(4,128)}) custom-call(s32[1]{0:T(128)} %bitcast.far_ref, s32[4,64]{1,0:T(4,128)S(1)} %copy-done.11, s32[4,64]{1,0:T(4,128)S(1)} %copy-done.12, f32[60,60]{1,0:T(8,128)S(1)} %copy-done.3, f32[512,4,128]{2,1,0:T(4,128)S(1)} %bitcast.12, ...), custom_call_target="tpu_custom_call" | custom-call | tf_op jit(solution)/shard_map/forcing_and_windows/pallas_call | solution.py:665
  48.1 3.6 %all-to-all-start.2 = ((f32[16,20,4,128]{3,2,1,0:T(4,128)}), f32[16,20,4,128]{3,2,1,0:T(4,128)S(1)}, u32[]{:S(2)}, u32[]{:S(2)}) async-start(f32[16,20,4,128]{3,2,1,0:T(4,128)} %get-tuple-element.46), calls=%async_computation.2 | async-start | bytes 1310720 | tf_op jit(solution)/shard_map/all_to_all | solution.py:609
  51.8 5.9 %diffuse_atmos.1 = bf16[4,72,8192]{2,1,0:T(8,128)(2,1)} custom-call(bf16[72,72]{1,0:T(8,128)(2,1)S(1)} %copy-done.10, f32[4,8192]{1,0:T(4,128)S(1)} %copy-done.6, bf16[4,72,8192]{2,1,0:T(8,128)(2,1)} %refs_3_.1, bf16[4,72,8192]{2,1,0:T(8,128)(2,1)} %refs_3_.1, bf16[4,72,8192]{2,1,0:T(8,128)(2,1)} %refs_3_.1, bf16[4,72,8192]{2,1,0:T(8,128)(2,1)} %refs_3_.1), custom_call_target="tpu_custom_call" | custom-call | flops 339738624 | bytes 9437184 | tf_op jit(solution)/shard_map/diffuse_atmos/pallas_call | solution.py:159
  57.6 6.0 %all-to-all-done.2.back_ref = f32[16,20,4,128]{3,2,1,0:T(4,128)S(1)} async-done(((f32[16,20,4,128]{3,2,1,0:T(4,128)}), f32[16,20,4,128]{3,2,1,0:T(4,128)S(1)}, u32[]{:S(2)}, u32[]{:S(2)}) %all-to-all-start.2) | async-done | bytes 655392 | tf_op jit(solution)/shard_map/all_to_all | solution.py:609
  63.7 3.6 %all-to-all-start.3 = ((f32[16,20,4,128]{3,2,1,0:T(4,128)}), f32[16,20,4,128]{3,2,1,0:T(4,128)S(1)}, u32[]{:S(2)}, u32[]{:S(2)}) async-start(f32[16,20,4,128]{3,2,1,0:T(4,128)} %get-tuple-element.52), calls=%async_computation.3 | async-start | bytes 1310720 | tf_op jit(solution)/shard_map/all_to_all | solution.py:609
  67.3 1.4 %collect_away.1 = f32[4,10240]{1,0:T(4,128)S(1)} custom-call(s32[1]{0:T(128)} %bitcast.far_ref, s32[16,32]{1,0:T(8,128)S(1)} %bitcast.18, f32[16,20,4,128]{3,2,1,0:T(4,128)S(1)} %all-to-all-done.2.back_ref), custom_call_target="tpu_custom_call" | custom-call | tf_op jit(solution)/shard_map/collect_away/pallas_call | solution.py:569
  68.7 0.0 copy-start.8
  68.7 0.0 copy-start.9
  68.7 0.4 collective-permute-start.1
  69.1 12.1 %diffuse_ocean.1 = f32[60,4,8192]{2,1,0:T(4,128)} custom-call(f32[60,60]{1,0:T(8,128)S(1)} %copy-done.3, f32[4,8192]{1,0:T(4,128)S(1)} %get-tuple-element.53.forcing_ref, s32[1,8192]{1,0:T(1,128)S(1)} %bitcast.15, f32[60,4,8192]{2,1,0:T(4,128)} %bitcast.25, f32[60,4,8192]{2,1,0:T(4,128)} %bitcast.26, f32[60,4,8192]{2,1,0:T(4,128)} %bitcast.27, ...), custom_call_target="tpu_custom_call" | custom-call | flops 2831155200 | bytes 15728640 | tf_op jit(solution)/shard_map/diffuse_ocean/pallas_call | solution.py:499
  81.2 1.5 %all-to-all-done.3.back_ref = f32[16,20,4,128]{3,2,1,0:T(4,128)S(1)} async-done(((f32[16,20,4,128]{3,2,1,0:T(4,128)}), f32[16,20,4,128]{3,2,1,0:T(4,128)S(1)}, u32[]{:S(2)}, u32[]{:S(2)}) %all-to-all-start.3) | async-done | bytes 655392 | tf_op jit(solution)/shard_map/all_to_all | solution.py:609
  82.7 0.0 collective-permute-done.1.refs_0_
  82.7 2.1 %surface_state.1 = f32[4,8192]{1,0:T(4,128)} custom-call(s32[1]{0:T(128)} %bitcast.far_ref, s32[16,32]{1,0:T(8,128)S(1)} %bitcast.19, f32[16,20,4,128]{3,2,1,0:T(4,128)S(1)} %all-to-all-done.3.back_ref, f32[4,10240]{1,0:T(4,128)S(1)} %collective-permute-done.1.refs_0_, f32[1,8192]{1,0:T(1,128)S(1)} %bitcast.20, f32[4,8192]{1,0:T(4,128)S(1)} %copy-done.8), custom_call_target="tpu_custom_call" | custom-call | tf_op jit(solution)/shard_map/surface_state/pallas_call | solution.py:569
  (15 shorter events, 0.0 us)
Async XLA Ops:
  3.1 14.3 %collective-permute-start = (f32[4,8192]{1,0:T(4,128)}, f32[4,8192]{1,0:T(4,128)S(1)}, u32[]{:S(2)}, u32[]{:S(2)}) collective-permute-start(f32[4,8192]{1,0:T(4,128)} %get-tuple-element.36.own_ref), channel_id=1, source_target_pairs={{0,16},{16,0},{1,17},{17,1},{2,18},{18,2},{3,19},{19,3},{4,20},{20... | collective-permute-start | bytes 393224 | tf_op jit(solution)/shard_map/ppermute | solution.py:612
  7.2 10.3 %all-to-all-start = ((s32[16,1,32]{2,1,0:T(1,128)}), s32[16,1,32]{2,1,0:T(1,128)S(1)}, u32[]{:S(2)}, u32[]{:S(2)}) async-start(s32[16,1,32]{2,1,0:T(1,128)} %bitcast.31), calls=%async_computation | async-start | bytes 16384 | tf_op jit(solution)/shard_map/all_to_all | solution.py:609
  12.0 0.8 copy-start.2
  12.8 4.6 %copy-start.7 = (f32[4,8192]{1,0:T(4,128)S(1)}, f32[4,8192]{1,0:T(4,128)}, u32[]{:S(2)}) copy-start(f32[4,8192]{1,0:T(4,128)} %get-tuple-element.36.own_ref) | copy-start | bytes 393220
  12.8 12.2 %copy-start = (s32[4,8192]{1,0:T(4,128)S(1)}, s32[4,8192]{1,0:T(4,128)}, u32[]{:S(2)}) copy-start(s32[4,8192]{1,0:T(4,128)} %column_ref.4) | copy-start | bytes 393220
  12.8 12.3 %copy-start.1 = (f32[4,8192]{1,0:T(4,128)S(1)}, f32[4,8192]{1,0:T(4,128)}, u32[]{:S(2)}) copy-start(f32[4,8192]{1,0:T(4,128)} %atmos_weight_ref.3) | copy-start | bytes 393220
  12.8 12.3 %copy-start.4 = (s32[8192]{0:T(1024)S(1)}, s32[8192]{0:T(1024)}, u32[]{:S(2)}) copy-start(s32[8192]{0:T(1024)} %param.23) | copy-start | bytes 98308
  12.8 12.3 %copy-start.11 = (s32[4,64]{1,0:T(4,128)S(1)}, s32[4,64]{1,0:T(4,128)}, u32[]{:S(2)}) copy-start(s32[4,64]{1,0:T(4,128)} %get-tuple-element.30.place_ref) | copy-start | bytes 3076
  12.8 28.4 %copy-start.3 = (f32[60,60]{1,0:T(8,128)S(1)}, f32[60,60]{1,0:T(8,128)}, u32[]{:S(2)}) copy-start(f32[60,60]{1,0:T(8,128)} %mix_ref.7) | copy-start | bytes 43204
  12.8 28.4 %copy-start.5 = (f32[4,8192]{1,0:T(4,128)S(1)}, f32[4,8192]{1,0:T(4,128)}, u32[]{:S(2)}) copy-start(f32[4,8192]{1,0:T(4,128)} %ocean_weight_ref.1) | copy-start | bytes 393220
  12.8 28.4 %copy-start.12 = (s32[4,64]{1,0:T(4,128)S(1)}, s32[4,64]{1,0:T(4,128)}, u32[]{:S(2)}) copy-start(s32[4,64]{1,0:T(4,128)} %get-tuple-element.31.spot_ref) | copy-start | bytes 3076
  17.1 34.7 %copy-start.6 = (f32[4,8192]{1,0:T(4,128)S(1)}, f32[4,8192]{1,0:T(4,128)}, u32[]{:S(2)}) copy-start(f32[4,8192]{1,0:T(4,128)} %get-tuple-element.49.tend_ref) | copy-start | bytes 393220
  17.1 34.7 %copy-start.10 = (bf16[72,72]{1,0:T(8,128)(2,1)S(1)}, bf16[72,72]{1,0:T(8,128)(2,1)}, u32[]{:S(2)}) copy-start(bf16[72,72]{1,0:T(8,128)(2,1)} %mix_ref.6) | copy-start | bytes 31108
  20.2 21.0 %all-to-all-start.1 = ((f32[16,32,4,128]{3,2,1,0:T(4,128)}), f32[16,32,4,128]{3,2,1,0:T(4,128)S(1)}, u32[]{:S(2)}, u32[]{:S(2)}) async-start(f32[16,32,4,128]{3,2,1,0:T(4,128)} %serve_windows.1), calls=%async_computation.1 | async-start | bytes 2097152 | tf_op jit(solution)/shard_map/all_to_all | solution.py:609
  48.1 15.5 %all-to-all-start.2 = ((f32[16,20,4,128]{3,2,1,0:T(4,128)}), f32[16,20,4,128]{3,2,1,0:T(4,128)S(1)}, u32[]{:S(2)}, u32[]{:S(2)}) async-start(f32[16,20,4,128]{3,2,1,0:T(4,128)} %get-tuple-element.46), calls=%async_computation.2 | async-start | bytes 1310720 | tf_op jit(solution)/shard_map/all_to_all | solution.py:609
  63.7 19.0 %all-to-all-start.3 = ((f32[16,20,4,128]{3,2,1,0:T(4,128)}), f32[16,20,4,128]{3,2,1,0:T(4,128)S(1)}, u32[]{:S(2)}, u32[]{:S(2)}) async-start(f32[16,20,4,128]{3,2,1,0:T(4,128)} %get-tuple-element.52), calls=%async_computation.3 | async-start | bytes 1310720 | tf_op jit(solution)/shard_map/all_to_all | solution.py:609
  68.7 14.0 %copy-start.8 = (f32[4,8192]{1,0:T(4,128)S(1)}, f32[4,8192]{1,0:T(4,128)}, u32[]{:S(2)}) copy-start(f32[4,8192]{1,0:T(4,128)} %refs_2_.3) | copy-start | bytes 393220
  68.7 14.0 %copy-start.9 = (f32[8192]{0:T(1024)S(1)}, f32[8192]{0:T(1024)}, u32[]{:S(2)}) copy-start(f32[8192]{0:T(1024)} %param.19) | copy-start | bytes 98308
  68.7 14.0 %collective-permute-start.1 = (f32[4,10240]{1,0:T(4,128)S(1)}, f32[4,10240]{1,0:T(4,128)S(1)}, u32[]{:S(2)}, u32[]{:S(2)}) collective-permute-start(f32[4,10240]{1,0:T(4,128)S(1)} %collect_away.1), channel_id=1, source_target_pairs={{0,16},{16,0},{1,17},{17,1},{2,18},{18,2},{3,19},{19,3},{4,20},{20... | collective-permute-start | bytes 491528 | tf_op jit(solution)/shard_map/ppermute | solution.py:612

commit v9 on v5

--- a/solution.py
+++ b/solution.py
@@ -268,6 +268,7 @@
 
 
 GROUP = 8
+hot_type = jnp.float8_e4m3fn
 
 
 def hot_kernel(
@@ -328,7 +329,7 @@
             ],
             axis=0,
         )
-        hot_ref[inner] = hot
+        hot_ref[inner] = hot.astype(hot_type)
         parts = split_high(share)
         rows = jnp.concatenate(
             [jnp.where(first_half, parts, 0.0), jnp.where(first_half, 0.0, parts)], axis=1
@@ -366,8 +367,7 @@
     hot_ref,
     share_ref,
     forcing_ref,
-    away_ref,
-    home_ref,
+    send_ref,
     value_ref,
     held_ref,
     held_sem,
@@ -376,7 +376,7 @@
     intersections, cells = column_ref.shape
     windows = cells // LANES
     fields = base_ref.shape[0]
-    near, packed = away_ref.shape[:2]
+    near, _, packed = send_ref.shape[:3]
     per_owner = packed * fields // (fields + 1)
     rows = per_owner // fields
 
@@ -385,8 +385,7 @@
         return pltpu.make_async_copy(hot_ref.at[part], held_ref.at[part], held_sem.at[group])
 
     groups = windows // GROUP
-    ahead = min(3, groups)
-    for group in range(ahead):
+    for group in range(groups):
         fetch(group).start()
     value_ref[...] = jnp.zeros(value_ref.shape, jnp.float32)
     corner = mix_ref[0, 0]
@@ -394,11 +393,6 @@
 
     def body(group, carry):
         fetch(group).wait()
-
-        @pl.when(group + ahead < groups)
-        def _():
-            fetch(group + ahead).start()
-
         for inner in range(GROUP):
             step = group * GROUP + inner
             here = window(step)
@@ -428,7 +422,9 @@
             parts = jnp.concatenate(
                 [jnp.concatenate(left, axis=0), jnp.concatenate(right, axis=0)], axis=1
             ).astype(jnp.bfloat16)
-            spread = jnp.dot(parts, held_ref[step], preferred_element_type=jnp.float32)
+            spread = jnp.dot(
+                parts, held_ref[step].astype(jnp.bfloat16), preferred_element_type=jnp.float32
+            )
             for k in range(intersections):
                 side = slice((k % 2) * LANES, (k % 2 + 1) * LANES)
                 at = 2 * fields * k
@@ -437,20 +433,22 @@
                 )
         return carry
 
-    lax.fori_loop(0, windows // GROUP, body, 0)
+    lax.fori_loop(0, groups, body, 0)
     far = far_ref[0]
     shards = value_ref.reshape(2, near, per_owner, fields, LANES)
     copies = []
-    for index, (ref, shard) in enumerate(((away_ref, 1 - far), (home_ref, far))):
+    for index, shard in enumerate((1 - far, far)):
         copies.append(
             pltpu.make_async_copy(
-                shards.at[shard], ref.at[:, pl.ds(0, per_owner)], sent_sem.at[2 * index]
+                shards.at[shard],
+                send_ref.at[:, index, pl.ds(0, per_owner)],
+                sent_sem.at[2 * index],
             )
         )
         copies.append(
             pltpu.make_async_copy(
                 share_ref.at[shard],
-                ref.at[:, pl.ds(per_owner, rows)],
+                send_ref.at[:, index, pl.ds(per_owner, rows)],
                 sent_sem.at[2 * index + 1],
             )
         )
@@ -524,14 +522,12 @@
     )(mixing, forcing, mask, *[state] * len(specs))
 
 
-def collect_kernel(per_owner, far_ref, asked_ref, back_ref, *refs):
-    near, _, fields, _ = back_ref.shape
-    chains = 4
-    sums = refs[-2 * chains :]
-    rest = refs[: -2 * chains]
-    home = len(rest) > 1
+def collect_kernel(per_owner, home, far_ref, asked_ref, back_ref, out_ref, *sums):
+    near, _, _, fields, _ = back_ref.shape
     columns = sums[0].shape[1]
     quarter = columns // fields
+    chains = len(sums) // 2
+    half = 1 if home else 0
     far = far_ref[0]
     first = (far if home else 1 - far) * per_owner
     for ref in sums:
@@ -543,8 +539,8 @@
                 peer = step * chains + chain
                 at = window(asked_ref[peer, first + slot])
                 tile, row = per_owner + slot // fields, slot % fields
-                sums[chain][:, at] += back_ref[peer, slot]
-                sums[chains + chain][:, at] += back_ref[peer, tile, row : row + 1]
+                sums[chain][:, at] += back_ref[peer, half, slot]
+                sums[chains + chain][:, at] += back_ref[peer, half, tile, row : row + 1]
         return carry
 
     lax.fori_loop(0, near // chains, body, 0)
@@ -552,36 +548,36 @@
     for chain in range(1, chains):
         values = values + sums[chain][...]
         shares = shares + sums[chains + chain][...]
-    out_ref = rest[-1]
-    if home:
-        other_ref, land_weight_ref, land_ref = rest[:3]
-        land_weight = land_weight_ref[...]
-        total = values + other_ref[:, :columns] + land_weight * land_ref[...]
-        weight = shares + land_weight
-        for row in range(fields):
-            part = slice(row * quarter, (row + 1) * quarter)
-            other_shares = other_ref[row : row + 1, columns:]
-            out_ref[:, part] = total[:, part] / (weight[:, part] + other_shares)
-    else:
-        out_ref[:, :columns] = values
-        for row in range(fields):
-            out_ref[row : row + 1, columns:] = shares[:, row * quarter : (row + 1) * quarter]
-
-
-def collect(asked, far, back, per_owner, columns, rest):
-    fields = back.shape[2]
+    out_ref[:, :columns] = values
+    for row in range(fields):
+        out_ref[row : row + 1, columns:] = shares[:, row * quarter : (row + 1) * quarter]
+
+
+def collect(asked, far, back, per_owner, columns, home):
+    fields = back.shape[3]
     chains = 4
-    width = columns if rest else columns + columns // fields
     return pl.pallas_call(
-        functools.partial(collect_kernel, per_owner),
-        in_specs=[smem, smem, vmem] + [vmem] * len(rest),
+        functools.partial(collect_kernel, per_owner, home),
+        in_specs=[smem, smem, vmem],
         out_specs=vmem,
-        out_shape=jax.ShapeDtypeStruct((fields, width), jnp.float32),
+        out_shape=jax.ShapeDtypeStruct((fields, columns + columns // fields), jnp.float32),
         scratch_shapes=[pltpu.VMEM((fields, columns), jnp.float32)] * chains
         + [pltpu.VMEM((1, columns), jnp.float32)] * chains,
         compiler_params=params,
-        name="surface_state" if rest else "collect_away",
-    )(far, asked, back, *rest)
+        name="collect_home" if home else "collect_away",
+    )(far, asked, back)
+
+
+def final_kernel(keep_ref, other_ref, land_weight_ref, land_ref, out_ref):
+    fields, columns = out_ref.shape
+    quarter = columns // fields
+    both = keep_ref[:, :columns] + other_ref[:, :columns]
+    shares = keep_ref[:, columns:] + other_ref[:, columns:]
+    land_weight = land_weight_ref[...]
+    total = both + land_weight * land_ref[...]
+    for row in range(fields):
+        part = slice(row * quarter, (row + 1) * quarter)
+        out_ref[:, part] = total[:, part] / (shares[row : row + 1] + land_weight[:, part])
 
 
 def per_device(
@@ -658,7 +654,7 @@
             pl.BlockSpec((2 * near * rows, fields, LANES), lambda i: (0, 0, 0)),
         ],
         out_shape=[
-            jax.ShapeDtypeStruct((windows, 2 * LANES, 2 * LANES), jnp.bfloat16),
+            jax.ShapeDtypeStruct((windows, 2 * LANES, 2 * LANES), hot_type),
             jax.ShapeDtypeStruct((2 * near * rows, fields, LANES), jnp.float32),
         ],
         scratch_shapes=[pltpu.VMEM((windows // GROUP, LANES, LANES), jnp.bfloat16)]
@@ -667,19 +663,18 @@
         name="one_hot_and_shares",
     )(place, columns_asked, atmos_weight, mask)
     arrived, hot, shares = lax.optimization_barrier((arrived, hot, shares))
-    sent = (near, per_owner + rows, fields, LANES)
-    forcing, away, home = pl.pallas_call(
+    sent = (near, 2, per_owner + rows, fields, LANES)
+    forcing, send = pl.pallas_call(
         middle_kernel,
         in_specs=[smem] * 4 + [vmem] * 7 + [hbm, vmem],
-        out_specs=[vmem, hbm, hbm],
+        out_specs=[vmem, hbm],
         out_shape=[
             jax.ShapeDtypeStruct((fields, cells), jnp.float32),
-            jax.ShapeDtypeStruct(sent, jnp.float32),
             jax.ShapeDtypeStruct(sent, jnp.float32),
         ],
         scratch_shapes=[
             pltpu.VMEM((near * spots, fields, LANES), jnp.float32),
-            pltpu.VMEM((windows, 2 * LANES, 2 * LANES), jnp.bfloat16),
+            pltpu.VMEM((windows, 2 * LANES, 2 * LANES), hot_type),
             pltpu.SemaphoreType.DMA((windows // GROUP,)),
             pltpu.SemaphoreType.DMA((4,)),
         ],
@@ -700,24 +695,24 @@
         hot,
         shares.reshape(2, near, rows, fields, LANES),
     )
-    tendency, forcing = lax.optimization_barrier((tendency, forcing))
+    ocean_updated = diffuse_ocean(state, ocean_mixing, forcing, mask).transpose(1, 0, 2)
+    back, ocean_updated = lax.optimization_barrier((to_near(send), ocean_updated))
+    sums_away = collect(asked, far, back, per_owner, columns, False)
+    sums_away, back, tendency = lax.optimization_barrier((sums_away, back, tendency))
+    other_sums = to_far(sums_away)
+    sums_home = collect(asked, far, back, per_owner, columns, True)
     atmos_updated = diffuse_atmos(atmos_profiles, atmos_mixing, tendency)
-    back_away, atmos_updated, home = lax.optimization_barrier(
-        (to_near(away), atmos_updated, home)
+    other_sums, sums_home, atmos_updated = lax.optimization_barrier(
+        (other_sums, sums_home, atmos_updated)
     )
-    back_home = to_near(home)
-    sums_away = collect(asked, far, back_away, per_owner, columns, ())
-    other_sums = to_far(sums_away)
-    ocean_updated = diffuse_ocean(state, ocean_mixing, forcing, mask).transpose(1, 0, 2)
-    back_home, ocean_updated = lax.optimization_barrier((back_home, ocean_updated))
-    surface_state = collect(
-        asked,
-        far,
-        back_home,
-        per_owner,
-        columns,
-        (other_sums, land_weight.reshape(1, columns), land_surface),
-    )
+    surface_state = pl.pallas_call(
+        final_kernel,
+        in_specs=[vmem] * 4,
+        out_specs=vmem,
+        out_shape=jax.ShapeDtypeStruct((fields, columns), jnp.float32),
+        compiler_params=params,
+        name="surface_state",
+    )(sums_home, other_sums, land_weight.reshape(1, columns), land_surface)
     return (atmos_updated, ocean_updated, surface_state)
 
 

time: 85.8 us -> 82.5 us (0.962)
  starting transfers between devices: 21.3 us -> 17.1 us
  Pallas kernels: 47.3 us -> 44.8 us
  waiting for transfers between devices: 14.8 us -> 17 us
  local copies, waits for them, and re-layouts: 0.81 us -> 2.08 us
    all_to_all x4 -> x3, starting transfers between devices: 16.8 us -> 12.6 us  [to_near(): lax.all_to_all(values, ('near', 'sub'), split_axis=0, concat_axis=0, tile...]
    ppermute x2, waiting for transfers between devices: 0.01 us -> 2.38 us  [to_far(): return lax.ppermute(values, 'far', ((0, 1), (1, 0)))]
    pallas_call x1, Pallas kernels: 9.25 us -> 7.67 us  [per_device(): pl.pallas_call(hot_kernel, grid=(windows // GROUP,), in_specs=[smem] + [v...]
    unnamed x26, local copies, waits for them, and re-layouts: 0.81 us -> 2.08 us
    pallas_call x1, Pallas kernels: 7.02 us -> 6.06 us  [per_device(): pl.pallas_call(middle_kernel, in_specs=[smem] * 4 + [vmem] * 7 + [hbm, vm...]
    all_to_all x4 -> x3, waiting for transfers between devices: 14.8 us -> 14.7 us  [to_near(): lax.all_to_all(values, ('near', 'sub'), split_axis=0, concat_axis=0, tile...]
    pallas_call x2 -> x3, Pallas kernels: 3.56 us -> 3.57 us  [the longest x2 2.84 us: collect(): pl.pallas_call(functools.partial(collect_kernel, per_owner, home), in_spe...]
  transfers between devices with their start and end apart: 6 -> 5, of which waited for: 4 -> 4; matrix products, arithmetic and copies ran while one was open for 0% -> 0% of each run, Pallas kernels for 39% -> 38%
where the time goes in v9:
time: 82.5 us; the launch traced here: 81.9 us
  Pallas kernels  44.8 us (54%)
  starting transfers between devices  17.1 us (21%)
  waiting for transfers between devices  17 us (21%)
  local copies, waits for them, and re-layouts  2.08 us (3%)
  between operations  0.87 us (1%)
    all_to_all x3, waiting for transfers between devices, to_near(): lax.all_to_all(values, ('near', 'sub'), split_axis=0, concat_axis=0, tile...  14.7 us
    all_to_all x3, starting transfers between devices, to_near(): lax.all_to_all(values, ('near', 'sub'), split_axis=0, concat_axis=0, tile...  12.6 us
    pallas_call x1, Pallas kernels, diffuse_ocean(): pl.pallas_call(ocean_kernel, grid=(cells // block,), in_specs=[pl.BlockSp...  12.1 us
    pallas_call x1, Pallas kernels, per_device(): pl.pallas_call(hot_kernel, grid=(windows // GROUP,), in_specs=[smem] + [v...  7.67 us
    pallas_call x1, Pallas kernels, per_device(): pl.pallas_call(middle_kernel, in_specs=[smem] * 4 + [vmem] * 7 + [hbm, vm...  6.06 us
    pallas_call x1, Pallas kernels, diffuse_atmos(): pl.pallas_call(atmos_kernel, grid=(columns // block,), in_specs=[pl.Block...  5.89 us
    ppermute x2, starting transfers between devices, to_far(): return lax.ppermute(values, 'far', ((0, 1), (1, 0)))  4.49 us
    pallas_call x1, Pallas kernels, top_level(): pl.pallas_call(top_kernel, grid=(cells // block,), in_specs=[smem] + spec...  4.23 us
  transfers between devices with their start and end apart: 5, of which 4 were waited for; matrix products, arithmetic and copies ran while one was open for 0% of the time, Pallas kernels for 38%

profile of v9, /device:TPU:0, one launch (start us, length us, event | category | flops | bytes accessed | tf_op | source)
XLA Modules:
  0.0 81.9 jit_solution(10636499818981246399)
XLA Ops:
  0.6 0.0 copy-start.3
  0.6 2.4 %requests_and_rates.1 = (s32[4,64]{1,0:T(4,128)}, s32[4,64]{1,0:T(4,128)}, s32[16,32]{1,0:T(8,128)}, f32[4,8192]{1,0:T(4,128)}, f32[4,8192]{1,0:T(4,128)}) custom-call(s32[4,8192]{1,0:T(4,128)} %slot_ref.1, s32[4,8192]{1,0:T(4,128)} %column_ref.4, bf16[4,72,8192]{2,1,0:T(8,128)(2,1)} %refs_3_.1, f32[1,8192]{1,0:T(1,128)} %bitcast.30, f32[4,8192]{1,0:T(4,128)} %before_ref.1, ...), custom_call_target="tpu_custom_call" | custom-call | tf_op jit(solution)/shard_map/requests_and_rates/pallas_call | solution.py:119
  3.1 4.1 %collective-permute-start = (f32[4,8192]{1,0:T(4,128)}, f32[4,8192]{1,0:T(4,128)S(1)}, u32[]{:S(2)}, u32[]{:S(2)}) collective-permute-start(f32[4,8192]{1,0:T(4,128)} %get-tuple-element.36.own_ref), channel_id=1, source_target_pairs={{0,16},{16,0},{1,17},{17,1},{2,18},{18,2},{3,19},{19,3},{4,20},{20... | collective-permute-start | bytes 393224 | tf_op jit(solution)/shard_map/ppermute | solution.py:614
  7.2 4.8 %all-to-all-start = ((s32[16,1,32]{2,1,0:T(1,128)}), s32[16,1,32]{2,1,0:T(1,128)S(1)}, u32[]{:S(2)}, u32[]{:S(2)}) async-start(s32[16,1,32]{2,1,0:T(1,128)} %bitcast.31), calls=%async_computation | async-start | bytes 16384 | tf_op jit(solution)/shard_map/all_to_all | solution.py:611
  12.0 0.0 copy-start.8
  12.1 0.0 copy-start.1
  12.1 0.0 copy-start.2
  12.1 0.0 copy-start.4
  12.1 0.0 copy-start.6
  12.1 4.2 %top_level.1 = (f32[4,8192]{1,0:T(4,128)S(1)}, f32[4,8192]{1,0:T(4,128)S(1)}) custom-call(f32[60,60]{1,0:T(8,128)S(1)} %copy-done.3, f32[60,4,8192]{2,1,0:T(4,128)} %bitcast.21, f32[60,4,8192]{2,1,0:T(4,128)} %bitcast.22, f32[60,4,8192]{2,1,0:T(4,128)} %bitcast.23, f32[60,4,8192]{2,1,0:T(4,128)} %bitcast.24), custom_call_target="tpu_custom_call" | custom-call | flops 3932160 | bytes 7864320 | tf_op jit(solution)/shard_map/top_level/pallas_call | solution.py:205
  16.4 1.1 %all-to-all-done = s32[16,1,32]{2,1,0:T(1,128)S(1)} async-done(((s32[16,1,32]{2,1,0:T(1,128)}), s32[16,1,32]{2,1,0:T(1,128)S(1)}, u32[]{:S(2)}, u32[]{:S(2)}) %all-to-all-start) | async-done | bytes 2080 | tf_op jit(solution)/shard_map/all_to_all | solution.py:611
  17.4 0.0 collective-permute-done.other_ref
  17.4 2.8 %serve_windows.1 = f32[16,32,4,128]{3,2,1,0:T(4,128)} custom-call(s32[1]{0:T(128)} %bitcast.far_ref, s32[16,32]{1,0:T(8,128)S(1)} %bitcast.17, f32[4,8192]{1,0:T(4,128)S(1)} %copy-done.8, f32[4,8192]{1,0:T(4,128)S(1)} %collective-permute-done.other_ref), custom_call_target="tpu_custom_call" | custom-call | tf_op jit(solution)/shard_map/serve_windows/pallas_call | solution.py:630
  20.2 4.1 %all-to-all-start.1 = ((f32[16,32,4,128]{3,2,1,0:T(4,128)}), f32[16,32,4,128]{3,2,1,0:T(4,128)S(1)}, u32[]{:S(2)}, u32[]{:S(2)}) async-start(f32[16,32,4,128]{3,2,1,0:T(4,128)} %serve_windows.1), calls=%async_computation.1 | async-start | bytes 2097152 | tf_op jit(solution)/shard_map/all_to_all | solution.py:611
  24.4 7.7 %one_hot_and_shares.1 = (f8e4m3fn[64,256,256]{2,1,0:T(32,128)(4,1)S(1)}, f32[128,4,128]{2,1,0:T(4,128)S(1)}) custom-call(s32[4,64]{1,0:T(4,128)S(1)} %copy-done.11, s32[4,8192]{1,0:T(4,128)S(1)} %copy-done.1, f32[4,8192]{1,0:T(4,128)S(1)} %copy-done.2, s32[1,8192]{1,0:T(1,128)S(1)} %bitcast.13), custom_call_target="tpu_custom_call" | custom-call | tf_op jit(solution)/shard_map/one_hot_and_shares/pallas_call | solution.py:648
  32.0 0.0 copy-start
  32.1 2.0 %copy-done = f8e4m3fn[64,256,256]{2,1,0:T(32,128)(4,1)} copy-done((f8e4m3fn[64,256,256]{2,1,0:T(32,128)(4,1)}, f8e4m3fn[64,256,256]{2,1,0:T(32,128)(4,1)S(1)}, u32[]{:S(2)}) %copy-start) | copy-done | bytes 4194328
  34.1 6.4 %all-to-all-done.1 = f32[16,32,4,128]{3,2,1,0:T(4,128)S(1)} async-done(((f32[16,32,4,128]{3,2,1,0:T(4,128)}), f32[16,32,4,128]{3,2,1,0:T(4,128)S(1)}, u32[]{:S(2)}, u32[]{:S(2)}) %all-to-all-start.1) | async-done | bytes 1048608 | tf_op jit(solution)/shard_map/all_to_all | solution.py:611
  40.5 6.1 %forcing_and_windows.1 = (f32[4,8192]{1,0:T(4,128)S(1)}, f32[16,2,20,4,128]{4,3,2,1,0:T(4,128)}) custom-call(s32[1]{0:T(128)} %bitcast.far_ref, s32[4,64]{1,0:T(4,128)S(1)} %copy-done.11, s32[4,64]{1,0:T(4,128)S(1)} %copy-done.12, f32[60,60]{1,0:T(8,128)S(1)} %copy-done.3, f32[512,4,128]{2,1,0:T(4,128)S(1)} %bitcast.12, s32[4,8192]{1,0:T(4,128)S(1)} %copy-done.1, ...), custom_call_target="tpu_custom_call" | custom-call | tf_op jit(solution)/shard_map/forcing_and_windows/pallas_call | solution.py:667
  46.6 3.7 %all-to-all-start.2 = ((f32[16,2,20,4,128]{4,3,2,1,0:T(4,128)}), f32[16,2,20,4,128]{4,3,2,1,0:T(4,128)S(1)}, u32[]{:S(2)}, u32[]{:S(2)}) async-start(f32[16,2,20,4,128]{4,3,2,1,0:T(4,128)} %get-tuple-element.46), calls=%async_computation.2 | async-start | bytes 2621440 | tf_op jit(solution)/shard_map/all_to_all | solution.py:611
  50.3 0.0 copy-start.10
  50.3 12.1 %diffuse_ocean.1 = f32[60,4,8192]{2,1,0:T(4,128)} custom-call(f32[60,60]{1,0:T(8,128)S(1)} %copy-done.3, f32[4,8192]{1,0:T(4,128)S(1)} %get-tuple-element.47.forcing_ref, s32[1,8192]{1,0:T(1,128)S(1)} %bitcast.15, f32[60,4,8192]{2,1,0:T(4,128)} %bitcast.25, f32[60,4,8192]{2,1,0:T(4,128)} %bitcast.26, f32[60,4,8192]{2,1,0:T(4,128)} %bitcast.27, ...), custom_call_target="tpu_custom_call" | custom-call | flops 2831155200 | bytes 15728640 | tf_op jit(solution)/shard_map/diffuse_ocean/pallas_call | solution.py:503
  62.5 7.1 %all-to-all-done.2.back_ref = f32[16,2,20,4,128]{4,3,2,1,0:T(4,128)S(1)} async-done(((f32[16,2,20,4,128]{4,3,2,1,0:T(4,128)}), f32[16,2,20,4,128]{4,3,2,1,0:T(4,128)S(1)}, u32[]{:S(2)}, u32[]{:S(2)}) %all-to-all-start.2) | async-done | bytes 1310752 | tf_op jit(solution)/shard_map/all_to_all | solution.py:611
  69.6 1.4 %collect_away.1 = f32[4,10240]{1,0:T(4,128)S(1)} custom-call(s32[1]{0:T(128)} %bitcast.far_ref, s32[16,32]{1,0:T(8,128)S(1)} %bitcast.18, f32[16,2,20,4,128]{4,3,2,1,0:T(4,128)S(1)} %all-to-all-done.2.back_ref), custom_call_target="tpu_custom_call" | custom-call | tf_op jit(solution)/shard_map/collect_away/pallas_call | solution.py:559
  71.0 0.4 collective-permute-start.1
  71.4 1.4 %collect_home.1.keep_ref = f32[4,10240]{1,0:T(4,128)S(1)} custom-call(s32[1]{0:T(128)} %bitcast.far_ref, s32[16,32]{1,0:T(8,128)S(1)} %bitcast.19, f32[16,2,20,4,128]{4,3,2,1,0:T(4,128)S(1)} %all-to-all-done.2.back_ref), custom_call_target="tpu_custom_call" | custom-call | tf_op jit(solution)/shard_map/collect_home/pallas_call | solution.py:559
  72.9 0.0 copy-start.7
  72.9 0.0 copy-start.9
  72.9 5.9 %diffuse_atmos.1 = bf16[4,72,8192]{2,1,0:T(8,128)(2,1)} custom-call(bf16[72,72]{1,0:T(8,128)(2,1)S(1)} %copy-done.10, f32[4,8192]{1,0:T(4,128)S(1)} %copy-done.5, bf16[4,72,8192]{2,1,0:T(8,128)(2,1)} %refs_3_.1, bf16[4,72,8192]{2,1,0:T(8,128)(2,1)} %refs_3_.1, bf16[4,72,8192]{2,1,0:T(8,128)(2,1)} %refs_3_.1, bf16[4,72,8192]{2,1,0:T(8,128)(2,1)} %refs_3_.1), custom_call_target="tpu_custom_call" | custom-call | flops 339738624 | bytes 9437184 | tf_op jit(solution)/shard_map/diffuse_atmos/pallas_call | solution.py:159
  78.8 2.4 %collective-permute-done.1.other_ref = f32[4,10240]{1,0:T(4,128)S(1)} collective-permute-done((f32[4,10240]{1,0:T(4,128)S(1)}, f32[4,10240]{1,0:T(4,128)S(1)}, u32[]{:S(2)}, u32[]{:S(2)}) %collective-permute-start.1) | collective-permute-done | bytes 163872 | tf_op jit(solution)/shard_map/ppermute | solution.py:614
  81.2 0.0 copy-done.9
  81.2 0.7 surface_state.1
  (14 shorter events, 0.0 us)
Async XLA Ops:
  0.6 11.4 %copy-start.3 = (f32[60,60]{1,0:T(8,128)S(1)}, f32[60,60]{1,0:T(8,128)}, u32[]{:S(2)}) copy-start(f32[60,60]{1,0:T(8,128)} %mix_ref.6) | copy-start | bytes 43204
  3.1 14.4 %collective-permute-start = (f32[4,8192]{1,0:T(4,128)}, f32[4,8192]{1,0:T(4,128)S(1)}, u32[]{:S(2)}, u32[]{:S(2)}) collective-permute-start(f32[4,8192]{1,0:T(4,128)} %get-tuple-element.36.own_ref), channel_id=1, source_target_pairs={{0,16},{16,0},{1,17},{17,1},{2,18},{18,2},{3,19},{19,3},{4,20},{20... | collective-permute-start | bytes 393224 | tf_op jit(solution)/shard_map/ppermute | solution.py:614
  7.2 10.3 %all-to-all-start = ((s32[16,1,32]{2,1,0:T(1,128)}), s32[16,1,32]{2,1,0:T(1,128)S(1)}, u32[]{:S(2)}, u32[]{:S(2)}) async-start(s32[16,1,32]{2,1,0:T(1,128)} %bitcast.31), calls=%async_computation | async-start | bytes 16384 | tf_op jit(solution)/shard_map/all_to_all | solution.py:611
  12.0 5.4 %copy-start.8 = (f32[4,8192]{1,0:T(4,128)S(1)}, f32[4,8192]{1,0:T(4,128)}, u32[]{:S(2)}) copy-start(f32[4,8192]{1,0:T(4,128)} %get-tuple-element.36.own_ref) | copy-start | bytes 393220
  12.1 12.3 %copy-start.1 = (s32[4,8192]{1,0:T(4,128)S(1)}, s32[4,8192]{1,0:T(4,128)}, u32[]{:S(2)}) copy-start(s32[4,8192]{1,0:T(4,128)} %column_ref.4) | copy-start | bytes 393220
  12.1 12.3 %copy-start.2 = (f32[4,8192]{1,0:T(4,128)S(1)}, f32[4,8192]{1,0:T(4,128)}, u32[]{:S(2)}) copy-start(f32[4,8192]{1,0:T(4,128)} %atmos_weight_ref.3) | copy-start | bytes 393220
  12.1 12.3 %copy-start.4 = (s32[8192]{0:T(1024)S(1)}, s32[8192]{0:T(1024)}, u32[]{:S(2)}) copy-start(s32[8192]{0:T(1024)} %param.23) | copy-start | bytes 98308
  12.1 12.3 %copy-start.11 = (s32[4,64]{1,0:T(4,128)S(1)}, s32[4,64]{1,0:T(4,128)}, u32[]{:S(2)}) copy-start(s32[4,64]{1,0:T(4,128)} %get-tuple-element.34.place_ref) | copy-start | bytes 3076
  12.1 28.4 %copy-start.6 = (f32[4,8192]{1,0:T(4,128)S(1)}, f32[4,8192]{1,0:T(4,128)}, u32[]{:S(2)}) copy-start(f32[4,8192]{1,0:T(4,128)} %ocean_weight_ref.1) | copy-start | bytes 393220
  12.1 28.4 %copy-start.12 = (s32[4,64]{1,0:T(4,128)S(1)}, s32[4,64]{1,0:T(4,128)}, u32[]{:S(2)}) copy-start(s32[4,64]{1,0:T(4,128)} %get-tuple-element.35.spot_ref) | copy-start | bytes 3076
  20.2 20.3 %all-to-all-start.1 = ((f32[16,32,4,128]{3,2,1,0:T(4,128)}), f32[16,32,4,128]{3,2,1,0:T(4,128)S(1)}, u32[]{:S(2)}, u32[]{:S(2)}) async-start(f32[16,32,4,128]{3,2,1,0:T(4,128)} %serve_windows.1), calls=%async_computation.1 | async-start | bytes 2097152 | tf_op jit(solution)/shard_map/all_to_all | solution.py:611
  32.0 2.0 %copy-start = (f8e4m3fn[64,256,256]{2,1,0:T(32,128)(4,1)}, f8e4m3fn[64,256,256]{2,1,0:T(32,128)(4,1)S(1)}, u32[]{:S(2)}) copy-start(f8e4m3fn[64,256,256]{2,1,0:T(32,128)(4,1)S(1)} %get-tuple-element.44.hot_ref) | copy-start | bytes 12582916
  46.6 23.0 %all-to-all-start.2 = ((f32[16,2,20,4,128]{4,3,2,1,0:T(4,128)}), f32[16,2,20,4,128]{4,3,2,1,0:T(4,128)S(1)}, u32[]{:S(2)}, u32[]{:S(2)}) async-start(f32[16,2,20,4,128]{4,3,2,1,0:T(4,128)} %get-tuple-element.46), calls=%async_computation.2 | async-start | bytes 2621440 | tf_op jit(solution)/shard_map/all_to_all | solution.py:611
  50.3 22.5 %copy-start.5 = (f32[4,8192]{1,0:T(4,128)S(1)}, f32[4,8192]{1,0:T(4,128)}, u32[]{:S(2)}) copy-start(f32[4,8192]{1,0:T(4,128)} %get-tuple-element.52.tend_ref) | copy-start | bytes 393220
  50.3 22.5 %copy-start.10 = (bf16[72,72]{1,0:T(8,128)(2,1)S(1)}, bf16[72,72]{1,0:T(8,128)(2,1)}, u32[]{:S(2)}) copy-start(bf16[72,72]{1,0:T(8,128)(2,1)} %mix_ref.7) | copy-start | bytes 31108
  71.0 10.1 %collective-permute-start.1 = (f32[4,10240]{1,0:T(4,128)S(1)}, f32[4,10240]{1,0:T(4,128)S(1)}, u32[]{:S(2)}, u32[]{:S(2)}) collective-permute-start(f32[4,10240]{1,0:T(4,128)S(1)} %collect_away.1), channel_id=1, source_target_pairs={{0,16},{16,0},{1,17},{17,1},{2,18},{18,2},{3,19},{19,3},{4,20},{20... | collective-permute-start | bytes 491528 | tf_op jit(solution)/shard_map/ppermute | solution.py:614
  72.9 8.3 %copy-start.7 = (f32[4,8192]{1,0:T(4,128)S(1)}, f32[4,8192]{1,0:T(4,128)}, u32[]{:S(2)}) copy-start(f32[4,8192]{1,0:T(4,128)} %land_ref.1) | copy-start | bytes 393220
  72.9 8.3 %copy-start.9 = (f32[8192]{0:T(1024)S(1)}, f32[8192]{0:T(1024)}, u32[]{:S(2)}) copy-start(f32[8192]{0:T(1024)} %param.19) | copy-start | bytes 98308

commit v10 on v9

--- a/solution.py
+++ b/solution.py
@@ -354,7 +354,7 @@
 
 def middle_kernel(
     far_ref,
-    place_ref,
+    target_ref,
     spot_ref,
     mix_ref,
     arrived_ref,
@@ -368,17 +368,12 @@
     share_ref,
     forcing_ref,
     send_ref,
-    value_ref,
     held_ref,
     held_sem,
-    sent_sem,
 ):
     intersections, cells = column_ref.shape
     windows = cells // LANES
     fields = base_ref.shape[0]
-    near, _, packed = send_ref.shape[:3]
-    per_owner = packed * fields // (fields + 1)
-    rows = per_owner // fields
 
     def fetch(group):
         part = pl.ds(group * GROUP, GROUP)
@@ -387,7 +382,7 @@
     groups = windows // GROUP
     for group in range(groups):
         fetch(group).start()
-    value_ref[...] = jnp.zeros(value_ref.shape, jnp.float32)
+    send_ref[...] = jnp.zeros(send_ref.shape, jnp.float32)
     corner = mix_ref[0, 0]
     blank = jnp.zeros((2 * fields, LANES), jnp.float32)
 
@@ -428,34 +423,19 @@
             for k in range(intersections):
                 side = slice((k % 2) * LANES, (k % 2 + 1) * LANES)
                 at = 2 * fields * k
-                value_ref[place_ref[k, step]] = (
+                send_ref[target_ref[k, step]] = (
                     spread[at : at + fields, side] + spread[at + fields : at + 2 * fields, side]
                 )
         return carry
 
     lax.fori_loop(0, groups, body, 0)
     far = far_ref[0]
-    shards = value_ref.reshape(2, near, per_owner, fields, LANES)
-    copies = []
-    for index, shard in enumerate((1 - far, far)):
-        copies.append(
-            pltpu.make_async_copy(
-                shards.at[shard],
-                send_ref.at[:, index, pl.ds(0, per_owner)],
-                sent_sem.at[2 * index],
-            )
-        )
-        copies.append(
-            pltpu.make_async_copy(
-                share_ref.at[shard],
-                send_ref.at[:, index, pl.ds(per_owner, rows)],
-                sent_sem.at[2 * index + 1],
-            )
-        )
-    for copy in copies:
-        copy.start()
-    for copy in copies:
-        copy.wait()
+    near, rows = share_ref.shape[1:3]
+    packed = send_ref.shape[0] // (2 * near)
+    for half, shard in enumerate((1 - far, far)):
+        for peer in range(near):
+            first = (2 * peer + half + 1) * packed - rows
+            send_ref[first : first + rows] = share_ref[shard, peer]
 
 
 def ocean_kernel(mix_ref, forcing_ref, mask_ref, *refs):
@@ -663,26 +643,28 @@
         name="one_hot_and_shares",
     )(place, columns_asked, atmos_weight, mask)
     arrived, hot, shares = lax.optimization_barrier((arrived, hot, shares))
-    sent = (near, 2, per_owner + rows, fields, LANES)
+    packed = per_owner + rows
+    shard, within = place // (near * per_owner), place % (near * per_owner)
+    half = jnp.where(shard == far, 1, 0)
+    target = (within // per_owner * 2 + half) * packed + within % per_owner
+    sent = (near * 2 * packed, fields, LANES)
     forcing, send = pl.pallas_call(
         middle_kernel,
         in_specs=[smem] * 4 + [vmem] * 7 + [hbm, vmem],
-        out_specs=[vmem, hbm],
+        out_specs=[vmem, vmem],
         out_shape=[
             jax.ShapeDtypeStruct((fields, cells), jnp.float32),
             jax.ShapeDtypeStruct(sent, jnp.float32),
         ],
         scratch_shapes=[
-            pltpu.VMEM((near * spots, fields, LANES), jnp.float32),
             pltpu.VMEM((windows, 2 * LANES, 2 * LANES), hot_type),
             pltpu.SemaphoreType.DMA((windows // GROUP,)),
-            pltpu.SemaphoreType.DMA((4,)),
         ],
         compiler_params=middle_params,
         name="forcing_and_windows",
     )(
         far,
-        place,
+        target,
         spot,
         ocean_mixing,
         arrived.reshape(near * spots, fields, LANES),
@@ -696,15 +678,17 @@
         shares.reshape(2, near, rows, fields, LANES),
     )
     ocean_updated = diffuse_ocean(state, ocean_mixing, forcing, mask).transpose(1, 0, 2)
-    back, ocean_updated = lax.optimization_barrier((to_near(send), ocean_updated))
+    tendency, forcing = lax.optimization_barrier((tendency, forcing))
+    atmos_updated = diffuse_atmos(atmos_profiles, atmos_mixing, tendency)
+    back = to_near(send.reshape(near, 2, packed, fields, LANES))
+    back, ocean_updated, atmos_updated = lax.optimization_barrier(
+        (back, ocean_updated, atmos_updated)
+    )
     sums_away = collect(asked, far, back, per_owner, columns, False)
-    sums_away, back, tendency = lax.optimization_barrier((sums_away, back, tendency))
+    sums_away, back = lax.optimization_barrier((sums_away, back))
     other_sums = to_far(sums_away)
     sums_home = collect(asked, far, back, per_owner, columns, True)
-    atmos_updated = diffuse_atmos(atmos_profiles, atmos_mixing, tendency)
-    other_sums, sums_home, atmos_updated = lax.optimization_barrier(
-        (other_sums, sums_home, atmos_updated)
-    )
+    other_sums, sums_home = lax.optimization_barrier((other_sums, sums_home))
     surface_state = pl.pallas_call(
         final_kernel,
         in_specs=[vmem] * 4,

time: 82.5 us -> 82.6 us (level)
    ppermute x2, waiting for transfers between devices: 2.38 us -> 8.4 us  [to_far(): return lax.ppermute(values, 'far', ((0, 1), (1, 0)))]
    all_to_all x3, waiting for transfers between devices: 14.7 us -> 8.76 us  [to_near(): lax.all_to_all(values, ('near', 'sub'), split_axis=0, concat_axis=0, tile...]
where the time goes in v10:
time: 82.6 us; the launch traced here: 81.9 us
  Pallas kernels  44.7 us (54%)
  waiting for transfers between devices  17.2 us (21%)
  starting transfers between devices  17.1 us (21%)
  local copies, waits for them, and re-layouts  2.07 us (3%)
  between operations  0.86 us (1%)
    all_to_all x3, starting transfers between devices, to_near(): lax.all_to_all(values, ('near', 'sub'), split_axis=0, concat_axis=0, tile...  12.6 us
    pallas_call x1, Pallas kernels, diffuse_ocean(): pl.pallas_call(ocean_kernel, grid=(cells // block,), in_specs=[pl.BlockSp...  12.1 us
    all_to_all x3, waiting for transfers between devices, to_near(): lax.all_to_all(values, ('near', 'sub'), split_axis=0, concat_axis=0, tile...  8.76 us
    ppermute x2, waiting for transfers between devices, to_far(): return lax.ppermute(values, 'far', ((0, 1), (1, 0)))  8.4 us
    pallas_call x1, Pallas kernels, per_device(): pl.pallas_call(hot_kernel, grid=(windows // GROUP,), in_specs=[smem] + [v...  7.67 us
    pallas_call x1, Pallas kernels, per_device(): pl.pallas_call(middle_kernel, in_specs=[smem] * 4 + [vmem] * 7 + [hbm, vm...  6.01 us
    pallas_call x1, Pallas kernels, diffuse_atmos(): pl.pallas_call(atmos_kernel, grid=(columns // block,), in_specs=[pl.Block...  5.85 us
    ppermute x2, starting transfers between devices, to_far(): return lax.ppermute(values, 'far', ((0, 1), (1, 0)))  4.49 us
  transfers between devices with their start and end apart: 5, of which 4 were waited for; matrix products, arithmetic and copies ran while one was open for 0% of the time, Pallas kernels for 38%

profile of v10, /device:TPU:0, one launch (start us, length us, event | category | flops | bytes accessed | tf_op | source)
XLA Modules:
  0.0 81.9 jit_solution(5661909863493841964)
XLA Ops:
  0.6 0.0 copy-start.3
  0.6 2.4 %requests_and_rates.1 = (s32[4,64]{1,0:T(4,128)}, s32[4,64]{1,0:T(4,128)}, s32[16,32]{1,0:T(8,128)}, f32[4,8192]{1,0:T(4,128)}, f32[4,8192]{1,0:T(4,128)}) custom-call(s32[4,8192]{1,0:T(4,128)} %slot_ref.1, s32[4,8192]{1,0:T(4,128)} %column_ref.4, bf16[4,72,8192]{2,1,0:T(8,128)(2,1)} %refs_3_.1, f32[1,8192]{1,0:T(1,128)} %bitcast.31, f32[4,8192]{1,0:T(4,128)} %before_ref.1, ...), custom_call_target="tpu_custom_call" | custom-call | tf_op jit(solution)/shard_map/requests_and_rates/pallas_call | solution.py:119
  3.1 4.1 %collective-permute-start = (f32[4,8192]{1,0:T(4,128)}, f32[4,8192]{1,0:T(4,128)S(1)}, u32[]{:S(2)}, u32[]{:S(2)}) collective-permute-start(f32[4,8192]{1,0:T(4,128)} %get-tuple-element.36.own_ref), channel_id=1, source_target_pairs={{0,16},{16,0},{1,17},{17,1},{2,18},{18,2},{3,19},{19,3},{4,20},{20... | collective-permute-start | bytes 393224 | tf_op jit(solution)/shard_map/ppermute | solution.py:594
  7.2 4.8 %all-to-all-start = ((s32[16,1,32]{2,1,0:T(1,128)}), s32[16,1,32]{2,1,0:T(1,128)S(1)}, u32[]{:S(2)}, u32[]{:S(2)}) async-start(s32[16,1,32]{2,1,0:T(1,128)} %bitcast.32), calls=%async_computation | async-start | bytes 16384 | tf_op jit(solution)/shard_map/all_to_all | solution.py:591
  12.0 0.0 copy-done.3
  12.0 0.0 copy-start.8
  12.1 0.0 copy-start.1
  12.1 0.0 copy-start.2
  12.1 0.0 copy-start.4
  12.1 0.0 copy-start.6
  12.1 4.2 %top_level.1 = (f32[4,8192]{1,0:T(4,128)S(1)}, f32[4,8192]{1,0:T(4,128)S(1)}) custom-call(f32[60,60]{1,0:T(8,128)S(1)} %copy-done.3, f32[60,4,8192]{2,1,0:T(4,128)} %bitcast.22, f32[60,4,8192]{2,1,0:T(4,128)} %bitcast.23, f32[60,4,8192]{2,1,0:T(4,128)} %bitcast.24, f32[60,4,8192]{2,1,0:T(4,128)} %bitcast.25), custom_call_target="tpu_custom_call" | custom-call | flops 3932160 | bytes 7864320 | tf_op jit(solution)/shard_map/top_level/pallas_call | solution.py:205
  16.4 1.1 %all-to-all-done = s32[16,1,32]{2,1,0:T(1,128)S(1)} async-done(((s32[16,1,32]{2,1,0:T(1,128)}), s32[16,1,32]{2,1,0:T(1,128)S(1)}, u32[]{:S(2)}, u32[]{:S(2)}) %all-to-all-start) | async-done | bytes 2080 | tf_op jit(solution)/shard_map/all_to_all | solution.py:591
  17.4 0.0 collective-permute-done.other_ref
  17.4 2.8 %serve_windows.1 = f32[16,32,4,128]{3,2,1,0:T(4,128)} custom-call(s32[1]{0:T(128)} %bitcast.far_ref, s32[16,32]{1,0:T(8,128)S(1)} %bitcast.18, f32[4,8192]{1,0:T(4,128)S(1)} %copy-done.8, f32[4,8192]{1,0:T(4,128)S(1)} %collective-permute-done.other_ref), custom_call_target="tpu_custom_call" | custom-call | tf_op jit(solution)/shard_map/serve_windows/pallas_call | solution.py:610
  20.2 4.1 %all-to-all-start.1 = ((f32[16,32,4,128]{3,2,1,0:T(4,128)}), f32[16,32,4,128]{3,2,1,0:T(4,128)S(1)}, u32[]{:S(2)}, u32[]{:S(2)}) async-start(f32[16,32,4,128]{3,2,1,0:T(4,128)} %serve_windows.1), calls=%async_computation.1 | async-start | bytes 2097152 | tf_op jit(solution)/shard_map/all_to_all | solution.py:591
  24.3 0.0 copy-start.10
  24.3 0.0 copy-done.11
  24.4 7.7 %one_hot_and_shares.1 = (f8e4m3fn[64,256,256]{2,1,0:T(32,128)(4,1)S(1)}, f32[128,4,128]{2,1,0:T(4,128)S(1)}) custom-call(s32[4,64]{1,0:T(4,128)S(1)} %copy-done.11, s32[4,8192]{1,0:T(4,128)S(1)} %copy-done.1, f32[4,8192]{1,0:T(4,128)S(1)} %copy-done.2, s32[1,8192]{1,0:T(1,128)S(1)} %bitcast.14), custom_call_target="tpu_custom_call" | custom-call | tf_op jit(solution)/shard_map/one_hot_and_shares/pallas_call | solution.py:628
  32.1 0.0 copy-start
  32.1 2.0 %copy-done = f8e4m3fn[64,256,256]{2,1,0:T(32,128)(4,1)} copy-done((f8e4m3fn[64,256,256]{2,1,0:T(32,128)(4,1)}, f8e4m3fn[64,256,256]{2,1,0:T(32,128)(4,1)S(1)}, u32[]{:S(2)}) %copy-start) | copy-done | bytes 4194328
  34.1 6.4 %all-to-all-done.1 = f32[16,32,4,128]{3,2,1,0:T(4,128)S(1)} async-done(((f32[16,32,4,128]{3,2,1,0:T(4,128)}), f32[16,32,4,128]{3,2,1,0:T(4,128)S(1)}, u32[]{:S(2)}, u32[]{:S(2)}) %all-to-all-start.1) | async-done | bytes 1048608 | tf_op jit(solution)/shard_map/all_to_all | solution.py:591
  40.5 6.0 %forcing_and_windows.1 = (f32[4,8192]{1,0:T(4,128)S(1)}, f32[640,4,128]{2,1,0:T(4,128)}) custom-call(s32[1]{0:T(128)} %bitcast.far_ref, s32[4,64]{1,0:T(4,128)S(1)} %fusion.3.target_ref, s32[4,64]{1,0:T(4,128)S(1)} %copy-done.12, f32[60,60]{1,0:T(8,128)S(1)} %copy-done.3, f32[512,4,128]{2,1,0:T(4,128)S(1)} %bitcast.13, s32[4,8192]{1,0:T(4,128)S(1)} %copy-done.1, ...), custom_call_target="tpu_custom_call" | custom-call | tf_op jit(solution)/shard_map/forcing_and_windows/pallas_call | solution.py:651
  46.5 3.7 %all-to-all-start.2 = ((f32[16,2,20,4,128]{4,3,2,1,0:T(4,128)}), f32[16,2,20,4,128]{4,3,2,1,0:T(4,128)S(1)}, u32[]{:S(2)}, u32[]{:S(2)}) async-start(f32[16,2,20,4,128]{4,3,2,1,0:T(4,128)} %bitcast.9), calls=%async_computation.2 | async-start | bytes 2621440 | tf_op jit(solution)/shard_map/all_to_all | solution.py:591
  50.3 5.9 %diffuse_atmos.1 = bf16[4,72,8192]{2,1,0:T(8,128)(2,1)} custom-call(bf16[72,72]{1,0:T(8,128)(2,1)S(1)} %copy-done.10, f32[4,8192]{1,0:T(4,128)S(1)} %copy-done.5, bf16[4,72,8192]{2,1,0:T(8,128)(2,1)} %refs_3_.1, bf16[4,72,8192]{2,1,0:T(8,128)(2,1)} %refs_3_.1, bf16[4,72,8192]{2,1,0:T(8,128)(2,1)} %refs_3_.1, bf16[4,72,8192]{2,1,0:T(8,128)(2,1)} %refs_3_.1), custom_call_target="tpu_custom_call" | custom-call | flops 339738624 | bytes 9437184 | tf_op jit(solution)/shard_map/diffuse_atmos/pallas_call | solution.py:159
  56.1 12.1 %diffuse_ocean.1 = f32[60,4,8192]{2,1,0:T(4,128)} custom-call(f32[60,60]{1,0:T(8,128)S(1)} %copy-done.3, f32[4,8192]{1,0:T(4,128)S(1)} %get-tuple-element.47.forcing_ref, s32[1,8192]{1,0:T(1,128)S(1)} %bitcast.16, f32[60,4,8192]{2,1,0:T(4,128)} %bitcast.26, f32[60,4,8192]{2,1,0:T(4,128)} %bitcast.27, f32[60,4,8192]{2,1,0:T(4,128)} %bitcast.28, ...), custom_call_target="tpu_custom_call" | custom-call | flops 2831155200 | bytes 15728640 | tf_op jit(solution)/shard_map/diffuse_ocean/pallas_call | solution.py:483
  68.3 1.3 %all-to-all-done.2.back_ref = f32[16,2,20,4,128]{4,3,2,1,0:T(4,128)S(1)} async-done(((f32[16,2,20,4,128]{4,3,2,1,0:T(4,128)}), f32[16,2,20,4,128]{4,3,2,1,0:T(4,128)S(1)}, u32[]{:S(2)}, u32[]{:S(2)}) %all-to-all-start.2) | async-done | bytes 1310752 | tf_op jit(solution)/shard_map/all_to_all | solution.py:591
  69.5 1.4 %collect_away.1 = f32[4,10240]{1,0:T(4,128)S(1)} custom-call(s32[1]{0:T(128)} %bitcast.far_ref, s32[16,32]{1,0:T(8,128)S(1)} %bitcast.19, f32[16,2,20,4,128]{4,3,2,1,0:T(4,128)S(1)} %all-to-all-done.2.back_ref), custom_call_target="tpu_custom_call" | custom-call | tf_op jit(solution)/shard_map/collect_away/pallas_call | solution.py:539
  71.0 0.4 collective-permute-start.1
  71.4 1.4 %collect_home.1.keep_ref = f32[4,10240]{1,0:T(4,128)S(1)} custom-call(s32[1]{0:T(128)} %bitcast.far_ref, s32[16,32]{1,0:T(8,128)S(1)} %bitcast.20, f32[16,2,20,4,128]{4,3,2,1,0:T(4,128)S(1)} %all-to-all-done.2.back_ref), custom_call_target="tpu_custom_call" | custom-call | tf_op jit(solution)/shard_map/collect_home/pallas_call | solution.py:539
  72.8 8.4 %collective-permute-done.1.other_ref = f32[4,10240]{1,0:T(4,128)S(1)} collective-permute-done((f32[4,10240]{1,0:T(4,128)S(1)}, f32[4,10240]{1,0:T(4,128)S(1)}, u32[]{:S(2)}, u32[]{:S(2)}) %collective-permute-start.1) | collective-permute-done | bytes 163872 | tf_op jit(solution)/shard_map/ppermute | solution.py:594
  81.2 0.0 copy-done.9
  81.2 0.7 surface_state.1
  (15 shorter events, 0.1 us)
Async XLA Ops:
  0.6 11.4 %copy-start.3 = (f32[60,60]{1,0:T(8,128)S(1)}, f32[60,60]{1,0:T(8,128)}, u32[]{:S(2)}) copy-start(f32[60,60]{1,0:T(8,128)} %mix_ref.6) | copy-start | bytes 43204
  3.1 14.4 %collective-permute-start = (f32[4,8192]{1,0:T(4,128)}, f32[4,8192]{1,0:T(4,128)S(1)}, u32[]{:S(2)}, u32[]{:S(2)}) collective-permute-start(f32[4,8192]{1,0:T(4,128)} %get-tuple-element.36.own_ref), channel_id=1, source_target_pairs={{0,16},{16,0},{1,17},{17,1},{2,18},{18,2},{3,19},{19,3},{4,20},{20... | collective-permute-start | bytes 393224 | tf_op jit(solution)/shard_map/ppermute | solution.py:594
  7.2 10.3 %all-to-all-start = ((s32[16,1,32]{2,1,0:T(1,128)}), s32[16,1,32]{2,1,0:T(1,128)S(1)}, u32[]{:S(2)}, u32[]{:S(2)}) async-start(s32[16,1,32]{2,1,0:T(1,128)} %bitcast.32), calls=%async_computation | async-start | bytes 16384 | tf_op jit(solution)/shard_map/all_to_all | solution.py:591
  12.0 5.4 %copy-start.8 = (f32[4,8192]{1,0:T(4,128)S(1)}, f32[4,8192]{1,0:T(4,128)}, u32[]{:S(2)}) copy-start(f32[4,8192]{1,0:T(4,128)} %get-tuple-element.36.own_ref) | copy-start | bytes 393220
  12.1 12.3 %copy-start.11 = (s32[4,64]{1,0:T(4,128)S(1)}, s32[4,64]{1,0:T(4,128)}, u32[]{:S(2)}) copy-start(s32[4,64]{1,0:T(4,128)} %get-tuple-element.30.place_ref) | copy-start | bytes 3076
  12.1 12.3 %copy-start.1 = (s32[4,8192]{1,0:T(4,128)S(1)}, s32[4,8192]{1,0:T(4,128)}, u32[]{:S(2)}) copy-start(s32[4,8192]{1,0:T(4,128)} %column_ref.4) | copy-start | bytes 393220
  12.1 12.3 %copy-start.2 = (f32[4,8192]{1,0:T(4,128)S(1)}, f32[4,8192]{1,0:T(4,128)}, u32[]{:S(2)}) copy-start(f32[4,8192]{1,0:T(4,128)} %atmos_weight_ref.3) | copy-start | bytes 393220
  12.1 12.3 %copy-start.4 = (s32[8192]{0:T(1024)S(1)}, s32[8192]{0:T(1024)}, u32[]{:S(2)}) copy-start(s32[8192]{0:T(1024)} %param.23) | copy-start | bytes 98308
  12.1 28.4 %copy-start.6 = (f32[4,8192]{1,0:T(4,128)S(1)}, f32[4,8192]{1,0:T(4,128)}, u32[]{:S(2)}) copy-start(f32[4,8192]{1,0:T(4,128)} %ocean_weight_ref.1) | copy-start | bytes 393220
  12.1 28.4 %copy-start.12 = (s32[4,64]{1,0:T(4,128)S(1)}, s32[4,64]{1,0:T(4,128)}, u32[]{:S(2)}) copy-start(s32[4,64]{1,0:T(4,128)} %get-tuple-element.31.spot_ref) | copy-start | bytes 3076
  20.2 20.3 %all-to-all-start.1 = ((f32[16,32,4,128]{3,2,1,0:T(4,128)}), f32[16,32,4,128]{3,2,1,0:T(4,128)S(1)}, u32[]{:S(2)}, u32[]{:S(2)}) async-start(f32[16,32,4,128]{3,2,1,0:T(4,128)} %serve_windows.1), calls=%async_computation.1 | async-start | bytes 2097152 | tf_op jit(solution)/shard_map/all_to_all | solution.py:591
  24.3 25.9 %copy-start.5 = (f32[4,8192]{1,0:T(4,128)S(1)}, f32[4,8192]{1,0:T(4,128)}, u32[]{:S(2)}) copy-start(f32[4,8192]{1,0:T(4,128)} %get-tuple-element.49.tend_ref) | copy-start | bytes 393220
  24.3 25.9 %copy-start.10 = (bf16[72,72]{1,0:T(8,128)(2,1)S(1)}, bf16[72,72]{1,0:T(8,128)(2,1)}, u32[]{:S(2)}) copy-start(bf16[72,72]{1,0:T(8,128)(2,1)} %mix_ref.7) | copy-start | bytes 31108
  32.1 2.0 %copy-start = (f8e4m3fn[64,256,256]{2,1,0:T(32,128)(4,1)}, f8e4m3fn[64,256,256]{2,1,0:T(32,128)(4,1)S(1)}, u32[]{:S(2)}) copy-start(f8e4m3fn[64,256,256]{2,1,0:T(32,128)(4,1)S(1)} %get-tuple-element.44.hot_ref) | copy-start | bytes 12582916
  46.5 23.0 %all-to-all-start.2 = ((f32[16,2,20,4,128]{4,3,2,1,0:T(4,128)}), f32[16,2,20,4,128]{4,3,2,1,0:T(4,128)S(1)}, u32[]{:S(2)}, u32[]{:S(2)}) async-start(f32[16,2,20,4,128]{4,3,2,1,0:T(4,128)} %bitcast.9), calls=%async_computation.2 | async-start | bytes 2621440 | tf_op jit(solution)/shard_map/all_to_all | solution.py:591
  56.1 25.1 %copy-start.7 = (f32[4,8192]{1,0:T(4,128)S(1)}, f32[4,8192]{1,0:T(4,128)}, u32[]{:S(2)}) copy-start(f32[4,8192]{1,0:T(4,128)} %land_ref.1) | copy-start | bytes 393220
  56.1 25.1 %copy-start.9 = (f32[8192]{0:T(1024)S(1)}, f32[8192]{0:T(1024)}, u32[]{:S(2)}) copy-start(f32[8192]{0:T(1024)} %param.19) | copy-start | bytes 98308
  71.0 10.2 %collective-permute-start.1 = (f32[4,10240]{1,0:T(4,128)S(1)}, f32[4,10240]{1,0:T(4,128)S(1)}, u32[]{:S(2)}, u32[]{:S(2)}) collective-permute-start(f32[4,10240]{1,0:T(4,128)S(1)} %collect_away.1), channel_id=1, source_target_pairs={{0,16},{16,0},{1,17},{17,1},{2,18},{18,2},{3,19},{19,3},{4,20},{20... | collective-permute-start | bytes 491528 | tf_op jit(solution)/shard_map/ppermute | solution.py:594

commit v11 on v10

--- a/solution.py
+++ b/solution.py
@@ -186,7 +186,7 @@
 
 
 def top_kernel(mix_ref, *refs):
-    state_refs, base_ref, first_ref = refs[:-2], refs[-2], refs[-1]
+    state_refs, base_ref = refs[:-1], refs[-1]
     total = None
     level = 0
     for ref in state_refs:
@@ -195,7 +195,6 @@
             total = term if total is None else total + term
             level += 1
     base_ref[...] = total
-    first_ref[...] = state_refs[0][0]
 
 
 def top_level(state, mixing):
@@ -206,8 +205,8 @@
         top_kernel,
         grid=(cells // block,),
         in_specs=[smem] + specs,
-        out_specs=[pl.BlockSpec((fields, block), lambda i: (0, i))] * 2,
-        out_shape=[jax.ShapeDtypeStruct((fields, cells), jnp.float32)] * 2,
+        out_specs=pl.BlockSpec((fields, block), lambda i: (0, i)),
+        out_shape=jax.ShapeDtypeStruct((fields, cells), jnp.float32),
         compiler_params=stream_params,
         cost_estimate=pl.CostEstimate(
             flops=2 * fields * levels * cells,
@@ -274,10 +273,13 @@
 def hot_kernel(
     place_ref,
     column_ref,
+    ocean_weight_ref,
     atmos_weight_ref,
     mask_ref,
     hot_ref,
     share_ref,
+    scaled_ref,
+    sea_share_ref,
     lanes_ref,
     *sums,
 ):
@@ -317,6 +319,10 @@
         step = group * GROUP + inner
         here = window(step)
         share = atmos_weight_ref[:, here] * mask_ref[:, here].astype(jnp.float32)
+        block = slice(inner * LANES, (inner + 1) * LANES)
+        sea_share_ref[:, block] = share
+        ocean_weight = ocean_weight_ref[:, here]
+        scaled_ref[:, block] = ocean_weight / jnp.sum(ocean_weight, axis=0, keepdims=True)
         hot = []
         for k in range(intersections):
             tile = inner * intersections + k
@@ -359,11 +365,9 @@
     mix_ref,
     arrived_ref,
     column_ref,
-    ocean_weight_ref,
-    atmos_weight_ref,
-    mask_ref,
+    scaled_ref,
+    sea_share_ref,
     base_ref,
-    state_ref,
     hot_ref,
     share_ref,
     forcing_ref,
@@ -392,9 +396,8 @@
             step = group * GROUP + inner
             here = window(step)
             lanes = column_ref[:, here] & (LANES - 1)
-            ocean_weight = ocean_weight_ref[:, here]
-            total = jnp.zeros((fields, LANES), jnp.float32)
-            weight = jnp.zeros((1, LANES), jnp.float32)
+            scaled = scaled_ref[:, here]
+            forcing = jnp.zeros((fields, LANES), jnp.float32)
             for k in range(intersections):
                 picked = jnp.take_along_axis(
                     arrived_ref[spot_ref[k, step]],
@@ -402,15 +405,10 @@
                     axis=1,
                     mode="promise_in_bounds",
                 )
-                total = total + ocean_weight[k : k + 1] * picked
-                weight = weight + ocean_weight[k : k + 1]
-            forcing = total / weight
+                forcing = forcing + scaled[k : k + 1] * picked
             forcing_ref[:, here] = forcing
-            mask = mask_ref[:, here]
-            surface = jnp.where(
-                mask == 1, base_ref[:, here] + corner * forcing, state_ref[:, here]
-            )
-            share = atmos_weight_ref[:, here] * mask.astype(jnp.float32)
+            surface = base_ref[:, here] + corner * forcing
+            share = sea_share_ref[:, here]
             parts = [split_high(share[k : k + 1] * surface) for k in range(intersections)]
             left = [parts[0], parts[1], blank, blank]
             right = [blank, blank, parts[2], parts[3]]
@@ -605,8 +603,8 @@
     )
     asked = to_near(wanted)
     other_rows = to_far(forcing_rows)
-    base, first_level = top_level(state, ocean_mixing)
-    asked, base, first_level = lax.optimization_barrier((asked, base, first_level))
+    base = top_level(state, ocean_mixing)
+    asked, base = lax.optimization_barrier((asked, base))
     served = pl.pallas_call(
         functools.partial(serve_kernel, per_owner),
         in_specs=[smem, smem, hbm, hbm],
@@ -625,24 +623,30 @@
     arrived = to_near(served)
     rows = per_owner // fields
     windows = cells // LANES
-    hot, shares = pl.pallas_call(
+    hot, shares, scaled, sea_share = pl.pallas_call(
         hot_kernel,
         grid=(windows // GROUP,),
-        in_specs=[smem] + [vmem] * 3,
+        in_specs=[smem] + [vmem] * 4,
         out_specs=[
             pl.BlockSpec((GROUP, 2 * LANES, 2 * LANES), lambda i: (i, 0, 0)),
             pl.BlockSpec((2 * near * rows, fields, LANES), lambda i: (0, 0, 0)),
+            pl.BlockSpec((intersections, GROUP * LANES), lambda i: (0, i)),
+            pl.BlockSpec((intersections, GROUP * LANES), lambda i: (0, i)),
         ],
         out_shape=[
             jax.ShapeDtypeStruct((windows, 2 * LANES, 2 * LANES), hot_type),
             jax.ShapeDtypeStruct((2 * near * rows, fields, LANES), jnp.float32),
+            jax.ShapeDtypeStruct((intersections, cells), jnp.float32),
+            jax.ShapeDtypeStruct((intersections, cells), jnp.float32),
         ],
         scratch_shapes=[pltpu.VMEM((windows // GROUP, LANES, LANES), jnp.bfloat16)]
         + [pltpu.VMEM((2 * near * rows, fields, LANES), jnp.float32)] * intersections,
         compiler_params=middle_params,
         name="one_hot_and_shares",
-    )(place, columns_asked, atmos_weight, mask)
-    arrived, hot, shares = lax.optimization_barrier((arrived, hot, shares))
+    )(place, columns_asked, ocean_weight, atmos_weight, mask)
+    arrived, hot, shares, scaled, sea_share = lax.optimization_barrier(
+        (arrived, hot, shares, scaled, sea_share)
+    )
     packed = per_owner + rows
     shard, within = place // (near * per_owner), place % (near * per_owner)
     half = jnp.where(shard == far, 1, 0)
@@ -650,7 +654,7 @@
     sent = (near * 2 * packed, fields, LANES)
     forcing, send = pl.pallas_call(
         middle_kernel,
-        in_specs=[smem] * 4 + [vmem] * 7 + [hbm, vmem],
+        in_specs=[smem] * 4 + [vmem] * 5 + [hbm, vmem],
         out_specs=[vmem, vmem],
         out_shape=[
             jax.ShapeDtypeStruct((fields, cells), jnp.float32),
@@ -669,11 +673,9 @@
         ocean_mixing,
         arrived.reshape(near * spots, fields, LANES),
         parent_column,
-        ocean_weight,
-        atmos_weight,
-        mask,
+        scaled,
+        sea_share,
         base,
-        first_level,
         hot,
         shares.reshape(2, near, rows, fields, LANES),
     )

time: 82.6 us -> 82.5 us (level)
  no operation moved by 1% of the time
where the time goes in v11:
time: 82.5 us; the launch traced here: 81.9 us
  Pallas kernels  44.7 us (54%)
  waiting for transfers between devices  17.2 us (21%)
  starting transfers between devices  17.1 us (21%)
  local copies, waits for them, and re-layouts  2.07 us (3%)
  between operations  0.87 us (1%)
    all_to_all x3, starting transfers between devices, to_near(): lax.all_to_all(values, ('near', 'sub'), split_axis=0, concat_axis=0, tile...  12.6 us
    pallas_call x1, Pallas kernels, diffuse_ocean(): pl.pallas_call(ocean_kernel, grid=(cells // block,), in_specs=[pl.BlockSp...  12.1 us
    all_to_all x3, waiting for transfers between devices, to_near(): lax.all_to_all(values, ('near', 'sub'), split_axis=0, concat_axis=0, tile...  8.76 us
    ppermute x2, waiting for transfers between devices, to_far(): return lax.ppermute(values, 'far', ((0, 1), (1, 0)))  8.4 us
    pallas_call x1, Pallas kernels, per_device(): pl.pallas_call(hot_kernel, grid=(windows // GROUP,), in_specs=[smem] + [v...  7.66 us
    pallas_call x1, Pallas kernels, per_device(): pl.pallas_call(middle_kernel, in_specs=[smem] * 4 + [vmem] * 5 + [hbm, vm...  6.01 us
    pallas_call x1, Pallas kernels, diffuse_atmos(): pl.pallas_call(atmos_kernel, grid=(columns // block,), in_specs=[pl.Block...  5.86 us
    ppermute x2, starting transfers between devices, to_far(): return lax.ppermute(values, 'far', ((0, 1), (1, 0)))  4.49 us
  transfers between devices with their start and end apart: 5, of which 4 were waited for; matrix products, arithmetic and copies ran while one was open for 0% of the time, Pallas kernels for 38%

profile of v11, /device:TPU:0, one launch (start us, length us, event | category | flops | bytes accessed | tf_op | source)
XLA Modules:
  0.0 81.9 jit_solution(14697307078250048889)
XLA Ops:
  0.6 2.4 %requests_and_rates.1 = (s32[4,64]{1,0:T(4,128)}, s32[4,64]{1,0:T(4,128)}, s32[16,32]{1,0:T(8,128)}, f32[4,8192]{1,0:T(4,128)}, f32[4,8192]{1,0:T(4,128)}) custom-call(s32[4,8192]{1,0:T(4,128)} %slot_ref.1, s32[4,8192]{1,0:T(4,128)} %column_ref.4, bf16[4,72,8192]{2,1,0:T(8,128)(2,1)} %refs_3_.1, f32[1,8192]{1,0:T(1,128)} %bitcast.30, f32[4,8192]{1,0:T(4,128)} %before_ref.1, ...), custom_call_target="tpu_custom_call" | custom-call | tf_op jit(solution)/shard_map/requests_and_rates/pallas_call | solution.py:119
  3.1 4.1 %collective-permute-start = (f32[4,8192]{1,0:T(4,128)}, f32[4,8192]{1,0:T(4,128)S(1)}, u32[]{:S(2)}, u32[]{:S(2)}) collective-permute-start(f32[4,8192]{1,0:T(4,128)} %get-tuple-element.35.own_ref), channel_id=1, source_target_pairs={{0,16},{16,0},{1,17},{17,1},{2,18},{18,2},{3,19},{19,3},{4,20},{20... | collective-permute-start | bytes 393224 | tf_op jit(solution)/shard_map/ppermute | solution.py:592
  7.2 4.8 %all-to-all-start = ((s32[16,1,32]{2,1,0:T(1,128)}), s32[16,1,32]{2,1,0:T(1,128)S(1)}, u32[]{:S(2)}, u32[]{:S(2)}) async-start(s32[16,1,32]{2,1,0:T(1,128)} %bitcast.31), calls=%async_computation | async-start | bytes 16384 | tf_op jit(solution)/shard_map/all_to_all | solution.py:589
  12.0 0.0 copy-start.6
  12.1 0.0 copy-start.1
  12.1 0.0 copy-start.4
  12.1 0.0 copy-start.7
  12.1 0.0 copy-start.8
  12.1 4.2 %top_level.1.base_ref = f32[4,8192]{1,0:T(4,128)S(1)} custom-call(f32[60,60]{1,0:T(8,128)S(1)} %copy-done.2, f32[60,4,8192]{2,1,0:T(4,128)} %bitcast.21, f32[60,4,8192]{2,1,0:T(4,128)} %bitcast.22, f32[60,4,8192]{2,1,0:T(4,128)} %bitcast.23, f32[60,4,8192]{2,1,0:T(4,128)} %bitcast.24), custom_call_target="tpu_custom_call" | custom-call | flops 3932160 | bytes 7864320 | tf_op jit(solution)/shard_map/top_level/pallas_call | solution.py:204
  16.4 1.1 %all-to-all-done = s32[16,1,32]{2,1,0:T(1,128)S(1)} async-done(((s32[16,1,32]{2,1,0:T(1,128)}), s32[16,1,32]{2,1,0:T(1,128)S(1)}, u32[]{:S(2)}, u32[]{:S(2)}) %all-to-all-start) | async-done | bytes 2080 | tf_op jit(solution)/shard_map/all_to_all | solution.py:589
  17.4 0.0 collective-permute-done.other_ref
  17.4 0.0 copy-done.6
  17.4 2.8 %serve_windows.1 = f32[16,32,4,128]{3,2,1,0:T(4,128)} custom-call(s32[1]{0:T(128)} %bitcast.far_ref, s32[16,32]{1,0:T(8,128)S(1)} %bitcast.15, f32[4,8192]{1,0:T(4,128)S(1)} %copy-done.6, f32[4,8192]{1,0:T(4,128)S(1)} %collective-permute-done.other_ref), custom_call_target="tpu_custom_call" | custom-call | tf_op jit(solution)/shard_map/serve_windows/pallas_call | solution.py:608
  20.2 4.1 %all-to-all-start.1 = ((f32[16,32,4,128]{3,2,1,0:T(4,128)}), f32[16,32,4,128]{3,2,1,0:T(4,128)S(1)}, u32[]{:S(2)}, u32[]{:S(2)}) async-start(f32[16,32,4,128]{3,2,1,0:T(4,128)} %serve_windows.1), calls=%async_computation.1 | async-start | bytes 2097152 | tf_op jit(solution)/shard_map/all_to_all | solution.py:589
  24.3 0.0 copy-start.3
  24.3 0.0 copy-start.10
  24.4 7.7 %one_hot_and_shares.1 = (f8e4m3fn[64,256,256]{2,1,0:T(32,128)(4,1)S(1)}, f32[128,4,128]{2,1,0:T(4,128)S(1)}, f32[4,8192]{1,0:T(4,128)S(1)}, f32[4,8192]{1,0:T(4,128)S(1)}) custom-call(s32[4,64]{1,0:T(4,128)S(1)} %copy-done.11, s32[4,8192]{1,0:T(4,128)S(1)} %copy-done.1, f32[4,8192]{1,0:T(4,128)S(1)} %copy-done.7, f32[4,8192]{1,0:T(4,128)S(1)} %copy-done.8, ...), custom_call_target="tpu_custom_call" | custom-call | tf_op jit(solution)/shard_map/one_hot_and_shares/pallas_call | solution.py:626
  32.1 0.0 copy-start
  32.1 2.0 %copy-done = f8e4m3fn[64,256,256]{2,1,0:T(32,128)(4,1)} copy-done((f8e4m3fn[64,256,256]{2,1,0:T(32,128)(4,1)}, f8e4m3fn[64,256,256]{2,1,0:T(32,128)(4,1)S(1)}, u32[]{:S(2)}) %copy-start) | copy-done | bytes 4194328
  34.1 6.4 %all-to-all-done.1 = f32[16,32,4,128]{3,2,1,0:T(4,128)S(1)} async-done(((f32[16,32,4,128]{3,2,1,0:T(4,128)}), f32[16,32,4,128]{3,2,1,0:T(4,128)S(1)}, u32[]{:S(2)}, u32[]{:S(2)}) %all-to-all-start.1) | async-done | bytes 1048608 | tf_op jit(solution)/shard_map/all_to_all | solution.py:589
  40.5 6.0 %forcing_and_windows.1 = (f32[4,8192]{1,0:T(4,128)S(1)}, f32[640,4,128]{2,1,0:T(4,128)}) custom-call(s32[1]{0:T(128)} %bitcast.far_ref, s32[4,64]{1,0:T(4,128)S(1)} %fusion.3.target_ref, s32[4,64]{1,0:T(4,128)S(1)} %copy-done.12, f32[60,60]{1,0:T(8,128)S(1)} %copy-done.2, f32[512,4,128]{2,1,0:T(4,128)S(1)} %bitcast.13, s32[4,8192]{1,0:T(4,128)S(1)} %copy-done.1, ...), custom_call_target="tpu_custom_call" | custom-call | tf_op jit(solution)/shard_map/forcing_and_windows/pallas_call | solution.py:655
  46.5 3.7 %all-to-all-start.2 = ((f32[16,2,20,4,128]{4,3,2,1,0:T(4,128)}), f32[16,2,20,4,128]{4,3,2,1,0:T(4,128)S(1)}, u32[]{:S(2)}, u32[]{:S(2)}) async-start(f32[16,2,20,4,128]{4,3,2,1,0:T(4,128)} %bitcast.9), calls=%async_computation.2 | async-start | bytes 2621440 | tf_op jit(solution)/shard_map/all_to_all | solution.py:589
  50.2 0.0 copy-done.3
  50.3 0.0 copy-done.10
  50.3 5.9 %diffuse_atmos.1 = bf16[4,72,8192]{2,1,0:T(8,128)(2,1)} custom-call(bf16[72,72]{1,0:T(8,128)(2,1)S(1)} %copy-done.10, f32[4,8192]{1,0:T(4,128)S(1)} %copy-done.3, bf16[4,72,8192]{2,1,0:T(8,128)(2,1)} %refs_3_.1, bf16[4,72,8192]{2,1,0:T(8,128)(2,1)} %refs_3_.1, bf16[4,72,8192]{2,1,0:T(8,128)(2,1)} %refs_3_.1, bf16[4,72,8192]{2,1,0:T(8,128)(2,1)} %refs_3_.1), custom_call_target="tpu_custom_call" | custom-call | flops 339738624 | bytes 9437184 | tf_op jit(solution)/shard_map/diffuse_atmos/pallas_call | solution.py:159
  56.1 12.1 %diffuse_ocean.1 = f32[60,4,8192]{2,1,0:T(4,128)} custom-call(f32[60,60]{1,0:T(8,128)S(1)} %copy-done.2, f32[4,8192]{1,0:T(4,128)S(1)} %get-tuple-element.49.forcing_ref, s32[1,8192]{1,0:T(1,128)S(1)} %bitcast.19, f32[60,4,8192]{2,1,0:T(4,128)} %bitcast.25, f32[60,4,8192]{2,1,0:T(4,128)} %bitcast.26, f32[60,4,8192]{2,1,0:T(4,128)} %bitcast.27, ...), custom_call_target="tpu_custom_call" | custom-call | flops 2831155200 | bytes 15728640 | tf_op jit(solution)/shard_map/diffuse_ocean/pallas_call | solution.py:481
  68.3 1.3 %all-to-all-done.2.back_ref = f32[16,2,20,4,128]{4,3,2,1,0:T(4,128)S(1)} async-done(((f32[16,2,20,4,128]{4,3,2,1,0:T(4,128)}), f32[16,2,20,4,128]{4,3,2,1,0:T(4,128)S(1)}, u32[]{:S(2)}, u32[]{:S(2)}) %all-to-all-start.2) | async-done | bytes 1310752 | tf_op jit(solution)/shard_map/all_to_all | solution.py:589
  69.5 1.4 %collect_away.1 = f32[4,10240]{1,0:T(4,128)S(1)} custom-call(s32[1]{0:T(128)} %bitcast.far_ref, s32[16,32]{1,0:T(8,128)S(1)} %bitcast.16, f32[16,2,20,4,128]{4,3,2,1,0:T(4,128)S(1)} %all-to-all-done.2.back_ref), custom_call_target="tpu_custom_call" | custom-call | tf_op jit(solution)/shard_map/collect_away/pallas_call | solution.py:537
  71.0 0.4 collective-permute-start.1
  71.4 1.4 %collect_home.1.keep_ref = f32[4,10240]{1,0:T(4,128)S(1)} custom-call(s32[1]{0:T(128)} %bitcast.far_ref, s32[16,32]{1,0:T(8,128)S(1)} %bitcast.17, f32[16,2,20,4,128]{4,3,2,1,0:T(4,128)S(1)} %all-to-all-done.2.back_ref), custom_call_target="tpu_custom_call" | custom-call | tf_op jit(solution)/shard_map/collect_home/pallas_call | solution.py:537
  72.8 8.4 %collective-permute-done.1.other_ref = f32[4,10240]{1,0:T(4,128)S(1)} collective-permute-done((f32[4,10240]{1,0:T(4,128)S(1)}, f32[4,10240]{1,0:T(4,128)S(1)}, u32[]{:S(2)}, u32[]{:S(2)}) %collective-permute-start.1) | collective-permute-done | bytes 163872 | tf_op jit(solution)/shard_map/ppermute | solution.py:592
  81.2 0.7 surface_state.1
  (15 shorter events, 0.1 us)
Async XLA Ops:
  0.6 11.4 %copy-start.2 = (f32[60,60]{1,0:T(8,128)S(1)}, f32[60,60]{1,0:T(8,128)}, u32[]{:S(2)}) copy-start(f32[60,60]{1,0:T(8,128)} %mix_ref.6) | copy-start | bytes 43204
  3.1 14.4 %collective-permute-start = (f32[4,8192]{1,0:T(4,128)}, f32[4,8192]{1,0:T(4,128)S(1)}, u32[]{:S(2)}, u32[]{:S(2)}) collective-permute-start(f32[4,8192]{1,0:T(4,128)} %get-tuple-element.35.own_ref), channel_id=1, source_target_pairs={{0,16},{16,0},{1,17},{17,1},{2,18},{18,2},{3,19},{19,3},{4,20},{20... | collective-permute-start | bytes 393224 | tf_op jit(solution)/shard_map/ppermute | solution.py:592
  7.2 10.3 %all-to-all-start = ((s32[16,1,32]{2,1,0:T(1,128)}), s32[16,1,32]{2,1,0:T(1,128)S(1)}, u32[]{:S(2)}, u32[]{:S(2)}) async-start(s32[16,1,32]{2,1,0:T(1,128)} %bitcast.31), calls=%async_computation | async-start | bytes 16384 | tf_op jit(solution)/shard_map/all_to_all | solution.py:589
  12.0 5.4 %copy-start.6 = (f32[4,8192]{1,0:T(4,128)S(1)}, f32[4,8192]{1,0:T(4,128)}, u32[]{:S(2)}) copy-start(f32[4,8192]{1,0:T(4,128)} %get-tuple-element.35.own_ref) | copy-start | bytes 393220
  12.1 12.3 %copy-start.11 = (s32[4,64]{1,0:T(4,128)S(1)}, s32[4,64]{1,0:T(4,128)}, u32[]{:S(2)}) copy-start(s32[4,64]{1,0:T(4,128)} %get-tuple-element.31.place_ref) | copy-start | bytes 3076
  12.1 12.3 %copy-start.1 = (s32[4,8192]{1,0:T(4,128)S(1)}, s32[4,8192]{1,0:T(4,128)}, u32[]{:S(2)}) copy-start(s32[4,8192]{1,0:T(4,128)} %column_ref.4) | copy-start | bytes 393220
  12.1 12.3 %copy-start.4 = (s32[8192]{0:T(1024)S(1)}, s32[8192]{0:T(1024)}, u32[]{:S(2)}) copy-start(s32[8192]{0:T(1024)} %param.23) | copy-start | bytes 98308
  12.1 12.3 %copy-start.7 = (f32[4,8192]{1,0:T(4,128)S(1)}, f32[4,8192]{1,0:T(4,128)}, u32[]{:S(2)}) copy-start(f32[4,8192]{1,0:T(4,128)} %ocean_weight_ref.1) | copy-start | bytes 393220
  12.1 12.3 %copy-start.8 = (f32[4,8192]{1,0:T(4,128)S(1)}, f32[4,8192]{1,0:T(4,128)}, u32[]{:S(2)}) copy-start(f32[4,8192]{1,0:T(4,128)} %atmos_weight_ref.1) | copy-start | bytes 393220
  12.1 28.4 %copy-start.12 = (s32[4,64]{1,0:T(4,128)S(1)}, s32[4,64]{1,0:T(4,128)}, u32[]{:S(2)}) copy-start(s32[4,64]{1,0:T(4,128)} %get-tuple-element.32.spot_ref) | copy-start | bytes 3076
  20.2 20.2 %all-to-all-start.1 = ((f32[16,32,4,128]{3,2,1,0:T(4,128)}), f32[16,32,4,128]{3,2,1,0:T(4,128)S(1)}, u32[]{:S(2)}, u32[]{:S(2)}) async-start(f32[16,32,4,128]{3,2,1,0:T(4,128)} %serve_windows.1), calls=%async_computation.1 | async-start | bytes 2097152 | tf_op jit(solution)/shard_map/all_to_all | solution.py:589
  24.3 25.9 %copy-start.3 = (f32[4,8192]{1,0:T(4,128)S(1)}, f32[4,8192]{1,0:T(4,128)}, u32[]{:S(2)}) copy-start(f32[4,8192]{1,0:T(4,128)} %get-tuple-element.51.tend_ref) | copy-start | bytes 393220
  24.3 25.9 %copy-start.10 = (bf16[72,72]{1,0:T(8,128)(2,1)S(1)}, bf16[72,72]{1,0:T(8,128)(2,1)}, u32[]{:S(2)}) copy-start(bf16[72,72]{1,0:T(8,128)(2,1)} %mix_ref.7) | copy-start | bytes 31108
  32.1 2.0 %copy-start = (f8e4m3fn[64,256,256]{2,1,0:T(32,128)(4,1)}, f8e4m3fn[64,256,256]{2,1,0:T(32,128)(4,1)S(1)}, u32[]{:S(2)}) copy-start(f8e4m3fn[64,256,256]{2,1,0:T(32,128)(4,1)S(1)} %get-tuple-element.46.hot_ref) | copy-start | bytes 12582916
  46.5 23.0 %all-to-all-start.2 = ((f32[16,2,20,4,128]{4,3,2,1,0:T(4,128)}), f32[16,2,20,4,128]{4,3,2,1,0:T(4,128)S(1)}, u32[]{:S(2)}, u32[]{:S(2)}) async-start(f32[16,2,20,4,128]{4,3,2,1,0:T(4,128)} %bitcast.9), calls=%async_computation.2 | async-start | bytes 2621440 | tf_op jit(solution)/shard_map/all_to_all | solution.py:589
  56.1 25.1 %copy-start.5 = (f32[4,8192]{1,0:T(4,128)S(1)}, f32[4,8192]{1,0:T(4,128)}, u32[]{:S(2)}) copy-start(f32[4,8192]{1,0:T(4,128)} %land_ref.1) | copy-start | bytes 393220
  56.1 25.1 %copy-start.9 = (f32[8192]{0:T(1024)S(1)}, f32[8192]{0:T(1024)}, u32[]{:S(2)}) copy-start(f32[8192]{0:T(1024)} %param.19) | copy-start | bytes 98308
  71.0 10.2 %collective-permute-start.1 = (f32[4,10240]{1,0:T(4,128)S(1)}, f32[4,10240]{1,0:T(4,128)S(1)}, u32[]{:S(2)}, u32[]{:S(2)}) collective-permute-start(f32[4,10240]{1,0:T(4,128)S(1)} %collect_away.1), channel_id=1, source_target_pairs={{0,16},{16,0},{1,17},{17,1},{2,18},{18,2},{3,19},{19,3},{4,20},{20... | collective-permute-start | bytes 491528 | tf_op jit(solution)/shard_map/ppermute | solution.py:592

commit v12 on v11

--- a/solution.py
+++ b/solution.py
@@ -266,7 +266,7 @@
     return jnp.concatenate([high, values - high], axis=0)
 
 
-GROUP = 8
+GROUP = 16
 hot_type = jnp.float8_e4m3fn
 
 

time: 82.5 us -> 81.9 us (level)
  Pallas kernels: 44.7 us -> 43.1 us
  waiting for transfers between devices: 17.2 us -> 18.1 us
    pallas_call x1, Pallas kernels: 7.66 us -> 6.65 us  [per_device(): pl.pallas_call(hot_kernel, grid=(windows // GROUP,), in_specs=[smem] + [v...]
    all_to_all x3, waiting for transfers between devices: 8.76 us -> 9.74 us  [to_near(): lax.all_to_all(values, ('near', 'sub'), split_axis=0, concat_axis=0, tile...]
  transfers between devices with their start and end apart: 5 -> 5, of which waited for: 4 -> 4; matrix products, arithmetic and copies ran while one was open for 0% -> 0% of each run, Pallas kernels for 38% -> 37%
where the time goes in v12:
time: 81.9 us; the launch traced here: 81.3 us
  Pallas kernels  43.1 us (53%)
  waiting for transfers between devices  18.1 us (22%)
  starting transfers between devices  17.1 us (21%)
  local copies, waits for them, and re-layouts  2.07 us (3%)
  between operations  0.86 us (1%)
    all_to_all x3, starting transfers between devices, to_near(): lax.all_to_all(values, ('near', 'sub'), split_axis=0, concat_axis=0, tile...  12.6 us
    pallas_call x1, Pallas kernels, diffuse_ocean(): pl.pallas_call(ocean_kernel, grid=(cells // block,), in_specs=[pl.BlockSp...  12.2 us
    all_to_all x3, waiting for transfers between devices, to_near(): lax.all_to_all(values, ('near', 'sub'), split_axis=0, concat_axis=0, tile...  9.74 us
    ppermute x2, waiting for transfers between devices, to_far(): return lax.ppermute(values, 'far', ((0, 1), (1, 0)))  8.4 us
    pallas_call x1, Pallas kernels, per_device(): pl.pallas_call(hot_kernel, grid=(windows // GROUP,), in_specs=[smem] + [v...  6.65 us
    pallas_call x1, Pallas kernels, diffuse_atmos(): pl.pallas_call(atmos_kernel, grid=(columns // block,), in_specs=[pl.Block...  5.86 us
    pallas_call x1, Pallas kernels, per_device(): pl.pallas_call(middle_kernel, in_specs=[smem] * 4 + [vmem] * 5 + [hbm, vm...  5.4 us
    ppermute x2, starting transfers between devices, to_far(): return lax.ppermute(values, 'far', ((0, 1), (1, 0)))  4.49 us
  transfers between devices with their start and end apart: 5, of which 4 were waited for; matrix products, arithmetic and copies ran while one was open for 0% of the time, Pallas kernels for 37%

profile of v12, /device:TPU:0, one launch (start us, length us, event | category | flops | bytes accessed | tf_op | source)
XLA Modules:
  0.0 81.3 jit_solution(12845347378744895707)
XLA Ops:
  0.6 2.4 %requests_and_rates.1 = (s32[4,64]{1,0:T(4,128)}, s32[4,64]{1,0:T(4,128)}, s32[16,32]{1,0:T(8,128)}, f32[4,8192]{1,0:T(4,128)}, f32[4,8192]{1,0:T(4,128)}) custom-call(s32[4,8192]{1,0:T(4,128)} %slot_ref.1, s32[4,8192]{1,0:T(4,128)} %column_ref.4, bf16[4,72,8192]{2,1,0:T(8,128)(2,1)} %refs_3_.1, f32[1,8192]{1,0:T(1,128)} %bitcast.30, f32[4,8192]{1,0:T(4,128)} %before_ref.1, ...), custom_call_target="tpu_custom_call" | custom-call | tf_op jit(solution)/shard_map/requests_and_rates/pallas_call | solution.py:119
  3.1 4.1 %collective-permute-start = (f32[4,8192]{1,0:T(4,128)}, f32[4,8192]{1,0:T(4,128)S(1)}, u32[]{:S(2)}, u32[]{:S(2)}) collective-permute-start(f32[4,8192]{1,0:T(4,128)} %get-tuple-element.35.own_ref), channel_id=1, source_target_pairs={{0,16},{16,0},{1,17},{17,1},{2,18},{18,2},{3,19},{19,3},{4,20},{20... | collective-permute-start | bytes 393224 | tf_op jit(solution)/shard_map/ppermute | solution.py:592
  7.2 4.8 %all-to-all-start = ((s32[16,1,32]{2,1,0:T(1,128)}), s32[16,1,32]{2,1,0:T(1,128)S(1)}, u32[]{:S(2)}, u32[]{:S(2)}) async-start(s32[16,1,32]{2,1,0:T(1,128)} %bitcast.31), calls=%async_computation | async-start | bytes 16384 | tf_op jit(solution)/shard_map/all_to_all | solution.py:589
  12.0 0.0 copy-start.6
  12.1 0.0 copy-start.11
  12.1 0.0 copy-start.1
  12.1 0.0 copy-start.4
  12.1 0.0 copy-start.7
  12.1 0.0 copy-start.8
  12.1 0.0 copy-start.12
  12.1 4.2 %top_level.1.base_ref = f32[4,8192]{1,0:T(4,128)S(1)} custom-call(f32[60,60]{1,0:T(8,128)S(1)} %copy-done.2, f32[60,4,8192]{2,1,0:T(4,128)} %bitcast.21, f32[60,4,8192]{2,1,0:T(4,128)} %bitcast.22, f32[60,4,8192]{2,1,0:T(4,128)} %bitcast.23, f32[60,4,8192]{2,1,0:T(4,128)} %bitcast.24), custom_call_target="tpu_custom_call" | custom-call | flops 3932160 | bytes 7864320 | tf_op jit(solution)/shard_map/top_level/pallas_call | solution.py:204
  16.4 1.1 %all-to-all-done = s32[16,1,32]{2,1,0:T(1,128)S(1)} async-done(((s32[16,1,32]{2,1,0:T(1,128)}), s32[16,1,32]{2,1,0:T(1,128)S(1)}, u32[]{:S(2)}, u32[]{:S(2)}) %all-to-all-start) | async-done | bytes 2080 | tf_op jit(solution)/shard_map/all_to_all | solution.py:589
  17.4 0.0 collective-permute-done.other_ref
  17.4 2.8 %serve_windows.1 = f32[16,32,4,128]{3,2,1,0:T(4,128)} custom-call(s32[1]{0:T(128)} %bitcast.far_ref, s32[16,32]{1,0:T(8,128)S(1)} %bitcast.15, f32[4,8192]{1,0:T(4,128)S(1)} %copy-done.6, f32[4,8192]{1,0:T(4,128)S(1)} %collective-permute-done.other_ref), custom_call_target="tpu_custom_call" | custom-call | tf_op jit(solution)/shard_map/serve_windows/pallas_call | solution.py:608
  20.2 4.1 %all-to-all-start.1 = ((f32[16,32,4,128]{3,2,1,0:T(4,128)}), f32[16,32,4,128]{3,2,1,0:T(4,128)S(1)}, u32[]{:S(2)}, u32[]{:S(2)}) async-start(f32[16,32,4,128]{3,2,1,0:T(4,128)} %serve_windows.1), calls=%async_computation.1 | async-start | bytes 2097152 | tf_op jit(solution)/shard_map/all_to_all | solution.py:589
  24.3 0.0 copy-start.10
  24.4 0.0 copy-done.1
  24.4 0.0 copy-done.4
  24.4 6.7 %one_hot_and_shares.1 = (f8e4m3fn[64,256,256]{2,1,0:T(32,128)(4,1)S(1)}, f32[128,4,128]{2,1,0:T(4,128)S(1)}, f32[4,8192]{1,0:T(4,128)S(1)}, f32[4,8192]{1,0:T(4,128)S(1)}) custom-call(s32[4,64]{1,0:T(4,128)S(1)} %copy-done.11, s32[4,8192]{1,0:T(4,128)S(1)} %copy-done.1, f32[4,8192]{1,0:T(4,128)S(1)} %copy-done.7, f32[4,8192]{1,0:T(4,128)S(1)} %copy-done.8, ...), custom_call_target="tpu_custom_call" | custom-call | tf_op jit(solution)/shard_map/one_hot_and_shares/pallas_call | solution.py:626
  31.1 0.0 copy-start
  31.1 2.0 %copy-done = f8e4m3fn[64,256,256]{2,1,0:T(32,128)(4,1)} copy-done((f8e4m3fn[64,256,256]{2,1,0:T(32,128)(4,1)}, f8e4m3fn[64,256,256]{2,1,0:T(32,128)(4,1)S(1)}, u32[]{:S(2)}) %copy-start) | copy-done | bytes 4194328
  33.1 7.4 %all-to-all-done.1 = f32[16,32,4,128]{3,2,1,0:T(4,128)S(1)} async-done(((f32[16,32,4,128]{3,2,1,0:T(4,128)}), f32[16,32,4,128]{3,2,1,0:T(4,128)S(1)}, u32[]{:S(2)}, u32[]{:S(2)}) %all-to-all-start.1) | async-done | bytes 1048608 | tf_op jit(solution)/shard_map/all_to_all | solution.py:589
  40.5 5.4 %forcing_and_windows.1 = (f32[4,8192]{1,0:T(4,128)S(1)}, f32[640,4,128]{2,1,0:T(4,128)}) custom-call(s32[1]{0:T(128)} %bitcast.far_ref, s32[4,64]{1,0:T(4,128)S(1)} %fusion.3.target_ref, s32[4,64]{1,0:T(4,128)S(1)} %copy-done.12, f32[60,60]{1,0:T(8,128)S(1)} %copy-done.2, f32[512,4,128]{2,1,0:T(4,128)S(1)} %bitcast.13, s32[4,8192]{1,0:T(4,128)S(1)} %copy-done.1, ...), custom_call_target="tpu_custom_call" | custom-call | tf_op jit(solution)/shard_map/forcing_and_windows/pallas_call | solution.py:655
  45.9 3.7 %all-to-all-start.2 = ((f32[16,2,20,4,128]{4,3,2,1,0:T(4,128)}), f32[16,2,20,4,128]{4,3,2,1,0:T(4,128)S(1)}, u32[]{:S(2)}, u32[]{:S(2)}) async-start(f32[16,2,20,4,128]{4,3,2,1,0:T(4,128)} %bitcast.9), calls=%async_computation.2 | async-start | bytes 2621440 | tf_op jit(solution)/shard_map/all_to_all | solution.py:589
  49.7 5.9 %diffuse_atmos.1 = bf16[4,72,8192]{2,1,0:T(8,128)(2,1)} custom-call(bf16[72,72]{1,0:T(8,128)(2,1)S(1)} %copy-done.10, f32[4,8192]{1,0:T(4,128)S(1)} %copy-done.3, bf16[4,72,8192]{2,1,0:T(8,128)(2,1)} %refs_3_.1, bf16[4,72,8192]{2,1,0:T(8,128)(2,1)} %refs_3_.1, bf16[4,72,8192]{2,1,0:T(8,128)(2,1)} %refs_3_.1, bf16[4,72,8192]{2,1,0:T(8,128)(2,1)} %refs_3_.1), custom_call_target="tpu_custom_call" | custom-call | flops 339738624 | bytes 9437184 | tf_op jit(solution)/shard_map/diffuse_atmos/pallas_call | solution.py:159
  55.5 12.2 %diffuse_ocean.1 = f32[60,4,8192]{2,1,0:T(4,128)} custom-call(f32[60,60]{1,0:T(8,128)S(1)} %copy-done.2, f32[4,8192]{1,0:T(4,128)S(1)} %get-tuple-element.49.forcing_ref, s32[1,8192]{1,0:T(1,128)S(1)} %bitcast.19, f32[60,4,8192]{2,1,0:T(4,128)} %bitcast.25, f32[60,4,8192]{2,1,0:T(4,128)} %bitcast.26, f32[60,4,8192]{2,1,0:T(4,128)} %bitcast.27, ...), custom_call_target="tpu_custom_call" | custom-call | flops 2831155200 | bytes 15728640 | tf_op jit(solution)/shard_map/diffuse_ocean/pallas_call | solution.py:481
  67.7 1.2 %all-to-all-done.2.back_ref = f32[16,2,20,4,128]{4,3,2,1,0:T(4,128)S(1)} async-done(((f32[16,2,20,4,128]{4,3,2,1,0:T(4,128)}), f32[16,2,20,4,128]{4,3,2,1,0:T(4,128)S(1)}, u32[]{:S(2)}, u32[]{:S(2)}) %all-to-all-start.2) | async-done | bytes 1310752 | tf_op jit(solution)/shard_map/all_to_all | solution.py:589
  68.9 1.4 %collect_away.1 = f32[4,10240]{1,0:T(4,128)S(1)} custom-call(s32[1]{0:T(128)} %bitcast.far_ref, s32[16,32]{1,0:T(8,128)S(1)} %bitcast.16, f32[16,2,20,4,128]{4,3,2,1,0:T(4,128)S(1)} %all-to-all-done.2.back_ref), custom_call_target="tpu_custom_call" | custom-call | tf_op jit(solution)/shard_map/collect_away/pallas_call | solution.py:537
  70.4 0.4 collective-permute-start.1
  70.8 1.4 %collect_home.1.keep_ref = f32[4,10240]{1,0:T(4,128)S(1)} custom-call(s32[1]{0:T(128)} %bitcast.far_ref, s32[16,32]{1,0:T(8,128)S(1)} %bitcast.17, f32[16,2,20,4,128]{4,3,2,1,0:T(4,128)S(1)} %all-to-all-done.2.back_ref), custom_call_target="tpu_custom_call" | custom-call | tf_op jit(solution)/shard_map/collect_home/pallas_call | solution.py:537
  72.2 8.4 %collective-permute-done.1.other_ref = f32[4,10240]{1,0:T(4,128)S(1)} collective-permute-done((f32[4,10240]{1,0:T(4,128)S(1)}, f32[4,10240]{1,0:T(4,128)S(1)}, u32[]{:S(2)}, u32[]{:S(2)}) %collective-permute-start.1) | collective-permute-done | bytes 163872 | tf_op jit(solution)/shard_map/ppermute | solution.py:592
  80.6 0.7 surface_state.1
  (15 shorter events, 0.1 us)
Async XLA Ops:
  0.6 11.4 %copy-start.2 = (f32[60,60]{1,0:T(8,128)S(1)}, f32[60,60]{1,0:T(8,128)}, u32[]{:S(2)}) copy-start(f32[60,60]{1,0:T(8,128)} %mix_ref.6) | copy-start | bytes 43204
  3.1 14.4 %collective-permute-start = (f32[4,8192]{1,0:T(4,128)}, f32[4,8192]{1,0:T(4,128)S(1)}, u32[]{:S(2)}, u32[]{:S(2)}) collective-permute-start(f32[4,8192]{1,0:T(4,128)} %get-tuple-element.35.own_ref), channel_id=1, source_target_pairs={{0,16},{16,0},{1,17},{17,1},{2,18},{18,2},{3,19},{19,3},{4,20},{20... | collective-permute-start | bytes 393224 | tf_op jit(solution)/shard_map/ppermute | solution.py:592
  7.2 10.3 %all-to-all-start = ((s32[16,1,32]{2,1,0:T(1,128)}), s32[16,1,32]{2,1,0:T(1,128)S(1)}, u32[]{:S(2)}, u32[]{:S(2)}) async-start(s32[16,1,32]{2,1,0:T(1,128)} %bitcast.31), calls=%async_computation | async-start | bytes 16384 | tf_op jit(solution)/shard_map/all_to_all | solution.py:589
  12.0 5.4 %copy-start.6 = (f32[4,8192]{1,0:T(4,128)S(1)}, f32[4,8192]{1,0:T(4,128)}, u32[]{:S(2)}) copy-start(f32[4,8192]{1,0:T(4,128)} %get-tuple-element.35.own_ref) | copy-start | bytes 393220
  12.1 12.3 %copy-start.11 = (s32[4,64]{1,0:T(4,128)S(1)}, s32[4,64]{1,0:T(4,128)}, u32[]{:S(2)}) copy-start(s32[4,64]{1,0:T(4,128)} %get-tuple-element.31.place_ref) | copy-start | bytes 3076
  12.1 12.3 %copy-start.1 = (s32[4,8192]{1,0:T(4,128)S(1)}, s32[4,8192]{1,0:T(4,128)}, u32[]{:S(2)}) copy-start(s32[4,8192]{1,0:T(4,128)} %column_ref.4) | copy-start | bytes 393220
  12.1 12.3 %copy-start.4 = (s32[8192]{0:T(1024)S(1)}, s32[8192]{0:T(1024)}, u32[]{:S(2)}) copy-start(s32[8192]{0:T(1024)} %param.23) | copy-start | bytes 98308
  12.1 12.3 %copy-start.7 = (f32[4,8192]{1,0:T(4,128)S(1)}, f32[4,8192]{1,0:T(4,128)}, u32[]{:S(2)}) copy-start(f32[4,8192]{1,0:T(4,128)} %ocean_weight_ref.1) | copy-start | bytes 393220
  12.1 12.3 %copy-start.8 = (f32[4,8192]{1,0:T(4,128)S(1)}, f32[4,8192]{1,0:T(4,128)}, u32[]{:S(2)}) copy-start(f32[4,8192]{1,0:T(4,128)} %atmos_weight_ref.1) | copy-start | bytes 393220
  12.1 28.4 %copy-start.12 = (s32[4,64]{1,0:T(4,128)S(1)}, s32[4,64]{1,0:T(4,128)}, u32[]{:S(2)}) copy-start(s32[4,64]{1,0:T(4,128)} %get-tuple-element.32.spot_ref) | copy-start | bytes 3076
  20.2 20.2 %all-to-all-start.1 = ((f32[16,32,4,128]{3,2,1,0:T(4,128)}), f32[16,32,4,128]{3,2,1,0:T(4,128)S(1)}, u32[]{:S(2)}, u32[]{:S(2)}) async-start(f32[16,32,4,128]{3,2,1,0:T(4,128)} %serve_windows.1), calls=%async_computation.1 | async-start | bytes 2097152 | tf_op jit(solution)/shard_map/all_to_all | solution.py:589
  24.3 25.3 %copy-start.3 = (f32[4,8192]{1,0:T(4,128)S(1)}, f32[4,8192]{1,0:T(4,128)}, u32[]{:S(2)}) copy-start(f32[4,8192]{1,0:T(4,128)} %get-tuple-element.51.tend_ref) | copy-start | bytes 393220
  24.3 25.3 %copy-start.10 = (bf16[72,72]{1,0:T(8,128)(2,1)S(1)}, bf16[72,72]{1,0:T(8,128)(2,1)}, u32[]{:S(2)}) copy-start(bf16[72,72]{1,0:T(8,128)(2,1)} %mix_ref.7) | copy-start | bytes 31108
  31.1 2.0 %copy-start = (f8e4m3fn[64,256,256]{2,1,0:T(32,128)(4,1)}, f8e4m3fn[64,256,256]{2,1,0:T(32,128)(4,1)S(1)}, u32[]{:S(2)}) copy-start(f8e4m3fn[64,256,256]{2,1,0:T(32,128)(4,1)S(1)} %get-tuple-element.46.hot_ref) | copy-start | bytes 12582916
  45.9 23.0 %all-to-all-start.2 = ((f32[16,2,20,4,128]{4,3,2,1,0:T(4,128)}), f32[16,2,20,4,128]{4,3,2,1,0:T(4,128)S(1)}, u32[]{:S(2)}, u32[]{:S(2)}) async-start(f32[16,2,20,4,128]{4,3,2,1,0:T(4,128)} %bitcast.9), calls=%async_computation.2 | async-start | bytes 2621440 | tf_op jit(solution)/shard_map/all_to_all | solution.py:589
  55.5 25.1 %copy-start.5 = (f32[4,8192]{1,0:T(4,128)S(1)}, f32[4,8192]{1,0:T(4,128)}, u32[]{:S(2)}) copy-start(f32[4,8192]{1,0:T(4,128)} %land_ref.1) | copy-start | bytes 393220
  55.5 25.1 %copy-start.9 = (f32[8192]{0:T(1024)S(1)}, f32[8192]{0:T(1024)}, u32[]{:S(2)}) copy-start(f32[8192]{0:T(1024)} %param.19) | copy-start | bytes 98308
  70.4 10.2 %collective-permute-start.1 = (f32[4,10240]{1,0:T(4,128)S(1)}, f32[4,10240]{1,0:T(4,128)S(1)}, u32[]{:S(2)}, u32[]{:S(2)}) collective-permute-start(f32[4,10240]{1,0:T(4,128)S(1)} %collect_away.1), channel_id=1, source_target_pairs={{0,16},{16,0},{1,17},{17,1},{2,18},{18,2},{3,19},{19,3},{4,20},{20... | collective-permute-start | bytes 491528 | tf_op jit(solution)/shard_map/ppermute | solution.py:592
